TPU v7x, 32 devices: a whole 2x2x4 slice. The times are simulated.
32 devices in a mesh: slab: 8 (over z, y), mode: 4 (over x, core).
Axes of the slice: x: 2, y: 2, z: 4, core: 2. Of those that a mesh axis runs over, the one named last changes fastest.
Arguments:
- positions: float32 [3, 65536], P(None, ('slab', 'mode')), may hold values from 0 to 1, as said below
- charges: float32 [65536], P(('slab', 'mode')), may hold values from -0.0546875 to 0.0546875
- counts: int32 [8], replicated, may hold values from 1792 to 8192, as said below
- box: float32 [2], replicated, may hold values from 0.8 to 1.25
Outputs:
- forces: float32 [3, 65536], P(None, ('slab', 'mode'))
Inputs may be any that keep to these rules, and one draw needn't show every extreme that they name: positions[0] and positions[1] are fractional coordinates; positions[2, i] lies strictly between s 0.08 / 8 and (s + 1) 0.08 / 8 for s = i // 8192, and never falls with i within a slab. The live ions of a slab are its first counts[s] slots; some slab is full.
All inputs are finite; a program needn't handle non-finite values.
Results may differ from a plain program's by a relative error of at most 0.0003.
Values sent between devices are 32-bit elements; how exact they have to be, the bound alone decides.
No kernel may reach another device: no remote copies, remote signals or barrier semaphores. Data moves between devices by JAX's collectives and lax.ppermute only.
A program may use at most 64 MiB of HBM per device.

v0:
```python
import math

import jax
import jax.numpy as jnp
from jax import lax
from jax.sharding import PartitionSpec as P

QDIM = 64
BLOCK = 512
MODES = 4096


two_pi = 2.0 * math.pi
slab_span = 0.08


def wave_table(first_mode, mode_count, box):
    mode_index = first_mode + jnp.arange(mode_count, dtype=jnp.int32)
    order_p = (mode_index // QDIM + 1).astype(jnp.float32)
    order_q = (mode_index % QDIM - QDIM // 2).astype(jnp.float32)
    wave_x = two_pi * order_p / box[0]
    wave_y = two_pi * order_q / box[1]
    wave_norm = jnp.sqrt(wave_x * wave_x + wave_y * wave_y)
    return (order_p, order_q, wave_x / wave_norm, wave_y / wave_norm, wave_norm)


def phase_terms(mode_info, coords, lower_edge, height):
    order_p, order_q, unit_x, unit_y, wave_norm = mode_info
    phase_angle = two_pi * (
        order_p[:, None] * coords[0][None, :] + order_q[:, None] * coords[1][None, :]
    )
    ion_depth = coords[2][None, :] - lower_edge
    e_low = jnp.exp(-wave_norm[:, None] * ion_depth)
    e_high = jnp.exp(-wave_norm[:, None] * (height - ion_depth))
    return (jnp.cos(phase_angle), jnp.sin(phase_angle), e_low, e_high)


def block_moments(mode_info, coords, weight, lower_edge, height):
    cosine, sine_part, e_low, e_high = phase_terms(mode_info, coords, lower_edge, height)
    upward = weight[None, :] * e_high
    downward = weight[None, :] * e_low
    row_stack = jnp.stack(
        [upward * cosine, upward * sine_part, downward * cosine, downward * sine_part]
    )
    mode_count = cosine.shape[0]
    return jnp.sum(row_stack.reshape(4, mode_count, cosine.shape[1] // BLOCK, BLOCK), axis=3)


def force_terms(mode_info, coords, weight, coefficients, lower_edge, height, box):
    order_p, order_q, unit_x, unit_y, wave_norm = mode_info
    cosine, sine_part, e_low, e_high = phase_terms(mode_info, coords, lower_edge, height)
    mode_count, ion_count = cosine.shape
    block_count = coefficients.shape[2]

    def spread(row_values):
        return jnp.broadcast_to(row_values[:, :, None], (mode_count, block_count, BLOCK)).reshape(
            mode_count, ion_count
        )

    below_c = e_low * spread(coefficients[0])
    below_s = e_low * spread(coefficients[1])
    above_c = e_high * spread(coefficients[2])
    above_s = e_high * spread(coefficients[3])
    in_plane = sine_part * (below_c + above_c) - cosine * (below_s + above_s)
    normal = cosine * (below_c - above_c) + sine_part * (below_s - above_s)
    scale = 2.0 * two_pi / (box[0] * box[1]) * weight
    return (
        jnp.stack(
            [
                jnp.sum(unit_x[:, None] * in_plane, axis=0),
                jnp.sum(unit_y[:, None] * in_plane, axis=0),
                jnp.sum(normal, axis=0),
            ]
        )
        * scale[None, :]
    )


def group_blocks(ion_total):
    block_count = ion_total // BLOCK
    chosen = 1
    for factor in range(1, 5):
        if block_count % factor == 0:
            chosen = factor
    return chosen


def sweep_moments(mode_info, coords, weight, lower_edge, height):
    ion_total = coords.shape[1]
    per_group = group_blocks(ion_total)
    group_width = per_group * BLOCK
    group_count = ion_total // group_width
    coord_groups = coords.reshape(3, group_count, group_width).transpose(1, 0, 2)
    weight_groups = weight.reshape(group_count, group_width)

    def advance(carried, group_item):
        return (carried, block_moments(mode_info, group_item[0], group_item[1], lower_edge, height))

    _, pieces = lax.scan(advance, jnp.int32(0), (coord_groups, weight_groups))
    mode_count = pieces.shape[2]
    return pieces.transpose(1, 2, 0, 3).reshape(4, mode_count, group_count * per_group)


def sweep_forces(mode_info, coords, weight, coefficients, lower_edge, height, box):
    ion_total = coords.shape[1]
    per_group = group_blocks(ion_total)
    group_width = per_group * BLOCK
    group_count = ion_total // group_width
    mode_count = coefficients.shape[1]
    coord_groups = coords.reshape(3, group_count, group_width).transpose(1, 0, 2)
    weight_groups = weight.reshape(group_count, group_width)
    coeff_groups = coefficients.reshape(4, mode_count, group_count, per_group).transpose(2, 0, 1, 3)

    def advance(carried, group_item):
        return (
            carried,
            force_terms(
                mode_info, group_item[0], group_item[1], group_item[2], lower_edge, height, box
            ),
        )

    _, pieces = lax.scan(advance, jnp.int32(0), (coord_groups, weight_groups, coeff_groups))
    return pieces.transpose(1, 0, 2).reshape(3, ion_total)


def carry_coefficients(moments, wave_norm, height):
    mode_count = moments.shape[1]
    block_count = moments.shape[2]
    block_ids = jnp.arange(block_count, dtype=jnp.int32)
    lower_tri = (block_ids[:, None] < block_ids[None, :]).astype(jnp.float32)
    upper_tri = (block_ids[:, None] > block_ids[None, :]).astype(jnp.float32)
    prefix_up = jnp.dot(
        moments[0:2].reshape(2 * mode_count, block_count),
        lower_tri,
        precision=lax.Precision.HIGHEST,
    ).reshape(2, mode_count, block_count)
    suffix_down = jnp.dot(
        moments[2:4].reshape(2 * mode_count, block_count),
        upper_tri,
        precision=lax.Precision.HIGHEST,
    ).reshape(2, mode_count, block_count)
    totals = jnp.sum(moments, axis=2)
    all_totals = lax.all_gather(totals[None], "slab", axis=0, tiled=True)
    slab_count = all_totals.shape[0]
    slab_rank = lax.axis_index("slab")
    slab_ids = jnp.arange(slab_count, dtype=jnp.int32)
    gap_up = jnp.maximum(slab_rank - 1 - slab_ids, 0).astype(jnp.float32)
    gap_down = jnp.maximum(slab_ids - slab_rank - 1, 0).astype(jnp.float32)
    weight_up = jnp.where(
        (slab_ids < slab_rank)[None, :],
        jnp.exp(-wave_norm[:, None] * height * gap_up[None, :]),
        0.0,
    )
    weight_down = jnp.where(
        (slab_ids > slab_rank)[None, :],
        jnp.exp(-wave_norm[:, None] * height * gap_down[None, :]),
        0.0,
    )
    carry_up = jnp.einsum(
        "mt,tcm->cm", weight_up, all_totals[:, 0:2], precision=lax.Precision.HIGHEST
    )
    carry_down = jnp.einsum(
        "mt,tcm->cm", weight_down, all_totals[:, 2:4], precision=lax.Precision.HIGHEST
    )
    boost_step = jnp.exp(wave_norm * height)[None, :, None]
    return jnp.concatenate(
        [
            carry_up[:, :, None] + boost_step * prefix_up,
            carry_down[:, :, None] + boost_step * suffix_down,
        ],
        axis=0,
    )


def shards(positions, charges, counts, box):
    slab_count = lax.axis_size("slab")
    mode_parts = lax.axis_size("mode")
    slab_rank = lax.axis_index("slab")
    mode_rank = lax.axis_index("mode")
    modes_dev = MODES // mode_parts
    height = slab_span / slab_count
    lower_edge = slab_rank.astype(jnp.float32) * height
    live_count = jnp.sum(jnp.where(jnp.arange(slab_count, dtype=jnp.int32) == slab_rank, counts, 0))
    coords, charge = (
        lax.all_gather(positions, "mode", axis=1, tiled=True),
        lax.all_gather(charges, "mode", axis=0, tiled=True),
    )
    live_mask = jnp.arange(coords.shape[1], dtype=jnp.int32) < live_count
    weight = jnp.where(live_mask, charge, jnp.float32(0.0))
    mode_info = wave_table(mode_rank * modes_dev, modes_dev, box)
    moments = sweep_moments(mode_info, coords, weight, lower_edge, height)
    coefficients = carry_coefficients(moments, mode_info[4], height)
    partial_force = sweep_forces(mode_info, coords, weight, coefficients, lower_edge, height, box)
    return lax.psum_scatter(partial_force, "mode", scatter_dimension=1, tiled=True)


def solution(mesh):
    return jax.shard_map(
        shards,
        mesh=mesh,
        in_specs=(P(None, ("slab", "mode")), P(("slab", "mode")), P(), P()),
        out_specs=P(None, ("slab", "mode")),
        check_vma=False,
    )
```

profile of v0, /device:TPU:0, one launch (start us, length us, event | category | flops | bytes accessed | tf_op | source)
XLA Modules:
  0.0 435.1 jit_solution(7502131354000507790)
XLA Ops:
  6.5 1.4 fusion.87
  11.0 1.4 fusion.85
  12.4 6.4 %all_gather.10 = f32[8192]{0:T(1024)S(1)} all-gather(f32[2048]{0:T(1024)} %param.9), channel_id=1, replica_groups=mesh['slab'=8,'mode'=4] {'mode'}, dimensions={0}, use_global_device_ids=true | all-gather | bytes 40960 | tf_op jit(solution)/shard_map/all_gather | solution.py:186
  19.4 5.9 %all_gather.9 = f32[3,8192]{1,0:T(4,128)S(1)} all-gather(f32[3,2048]{1,0:T(4,128)} %param.8), channel_id=1, replica_groups=mesh['slab'=8,'mode'=4] {'mode'}, dimensions={1}, use_global_device_ids=true | all-gather | bytes 122880 | tf_op jit(solution)/shard_map/all_gather | solution.py:185
  25.3 153.6 %while.28 = (s32[]{:T(128)}, f32[4,4,1024,4]{2,3,1,0:T(4,128)S(1)}, f32[4,2048]{1,0:T(4,128)S(1)}, f32[4,3,2048]{2,1,0:T(4,128)S(1)}, f32[]{:T(128)}, /*index=5*...) while((s32[]{:T(128)}, f32[4,4,1024,4]{2,3,1,0:T(4,128)S(1)}, ...), condition=%wide.region_3.4_spmd.clone.clone, body=%wide.region_1.3_spmd.clone.clone.sunk | while | flops 58765316 | bytes 67518648 | solution.py:99
  26.8 33.9 %fusion.95 = (f32[1,1024,4,512]{3,1,2,0:T(8,128)S(1)}, f32[1,1024,4,512]{3,1,2,0:T(8,128)S(1)}, f32[1,1024,4,512]{3,1,2,0:T(8,128)S(1)}, f32[1,1024,4,512]{3,1,2,0:T(8,128)S(1)}) fusion(f32[4,512]{1,0:T(4,128)S(1)} %mul.1314, f32[1024]{0:T(1024)S(1)} %get-tuple-element.571, f32[4,512]{1,0:T(4,128)S(1)} %mul.1315, f32[1024]{0:T(1024)S(1)} %get-tuple-element.573, ...), kind=kLoop, calls=%fused_computation.15.clone.1 | loop fusion | flops 25165824 | bytes 33607680 | tf_op jit(solution)/shard_map/while/body/eval_jaxpr/mul | solution.py:43
  60.8 2.9 maximum_reduce_fusion.2
  65.2 33.9 %fusion.95 = (f32[1,1024,4,512]{3,1,2,0:T(8,128)S(1)}, f32[1,1024,4,512]{3,1,2,0:T(8,128)S(1)}, f32[1,1024,4,512]{3,1,2,0:T(8,128)S(1)}, f32[1,1024,4,512]{3,1,2,0:T(8,128)S(1)}) fusion(f32[4,512]{1,0:T(4,128)S(1)} %mul.1314, f32[1024]{0:T(1024)S(1)} %get-tuple-element.571, f32[4,512]{1,0:T(4,128)S(1)} %mul.1315, f32[1024]{0:T(1024)S(1)} %get-tuple-element.573, ...), kind=kLoop, calls=%fused_computation.15.clone.1 | loop fusion | flops 25165824 | bytes 33607680 | tf_op jit(solution)/shard_map/while/body/eval_jaxpr/mul | solution.py:43
  99.2 2.9 maximum_reduce_fusion.2
  103.6 33.9 %fusion.95 = (f32[1,1024,4,512]{3,1,2,0:T(8,128)S(1)}, f32[1,1024,4,512]{3,1,2,0:T(8,128)S(1)}, f32[1,1024,4,512]{3,1,2,0:T(8,128)S(1)}, f32[1,1024,4,512]{3,1,2,0:T(8,128)S(1)}) fusion(f32[4,512]{1,0:T(4,128)S(1)} %mul.1314, f32[1024]{0:T(1024)S(1)} %get-tuple-element.571, f32[4,512]{1,0:T(4,128)S(1)} %mul.1315, f32[1024]{0:T(1024)S(1)} %get-tuple-element.573, ...), kind=kLoop, calls=%fused_computation.15.clone.1 | loop fusion | flops 25165824 | bytes 33607680 | tf_op jit(solution)/shard_map/while/body/eval_jaxpr/mul | solution.py:43
  137.6 2.9 maximum_reduce_fusion.2
  142.1 33.9 %fusion.95 = (f32[1,1024,4,512]{3,1,2,0:T(8,128)S(1)}, f32[1,1024,4,512]{3,1,2,0:T(8,128)S(1)}, f32[1,1024,4,512]{3,1,2,0:T(8,128)S(1)}, f32[1,1024,4,512]{3,1,2,0:T(8,128)S(1)}) fusion(f32[4,512]{1,0:T(4,128)S(1)} %mul.1314, f32[1024]{0:T(1024)S(1)} %get-tuple-element.571, f32[4,512]{1,0:T(4,128)S(1)} %mul.1315, f32[1024]{0:T(1024)S(1)} %get-tuple-element.573, ...), kind=kLoop, calls=%fused_computation.15.clone.1 | loop fusion | flops 25165824 | bytes 33607680 | tf_op jit(solution)/shard_map/while/body/eval_jaxpr/mul | solution.py:43
  176.0 2.9 maximum_reduce_fusion.2
  179.0 31.3 %all-gather.1 = f32[8,4,1024]{2,1,0:T(4,128)S(1)} all-gather(f32[1,4,1024]{2,1,0:T(4,128)S(1)} %bitcast.76), channel_id=2, replica_groups=mesh['slab'=8,'mode'=4] {'slab'}, dimensions={0}, use_global_device_ids=true | all-gather | bytes 147456 | tf_op jit(solution)/shard_map/all_gather | solution.py:143
  211.2 166.7 %while.29 = (s32[]{:T(128)}, f32[4,3,2048]{2,1,0:T(4,128)S(1)}, f32[4,3,2048]{2,1,0:T(4,128)S(1)}, f32[]{:T(128)}, f32[4,4,1024,4]{2,3,1,0:T(4,128)S(1)}, /*inde...) while((s32[]{:T(128)}, f32[4,3,2048]{2,1,0:T(4,128)S(1)}, ...), condition=%wide.region_9.10_spmd.clone.clone, body=%wide.region_5.9_spmd.clone.clone.sunk | while | flops 52540420 | bytes 540921 | solution.py:122
  212.6 1.3 sqrt_negate_fusion.5
  213.9 38.7 %multiply_reduce_fusion.3 = (f32[4,512]{1,0:T(4,128)S(1)}, f32[4,512]{1,0:T(4,128)S(1)}, f32[4,512]{1,0:T(4,128)S(1)}) fusion(f32[1024,4]{0,1:T(4,128)S(1)} %get-tuple-element.589, f32[1024,4]{0,1:T(4,128)S(1)} %get-tuple-element.590, f32[1024,4]{0,1:T(4,128)S(1)} %get-tuple-element.591, f32[4,512]{1,0:T(4,128)S(1)} %broadcast_subtract_fusion.5, ...), kind=kLoop, calls=%fused_computation.55.clone.1 | loop fusion | flops 52422656 | bytes 143360 | tf_op jit(solution)/shard_map/while/body/eval_jaxpr/reduce_sum | solution.py:70
  254.3 1.3 sqrt_negate_fusion.5
  255.6 38.7 %multiply_reduce_fusion.3 = (f32[4,512]{1,0:T(4,128)S(1)}, f32[4,512]{1,0:T(4,128)S(1)}, f32[4,512]{1,0:T(4,128)S(1)}) fusion(f32[1024,4]{0,1:T(4,128)S(1)} %get-tuple-element.589, f32[1024,4]{0,1:T(4,128)S(1)} %get-tuple-element.590, f32[1024,4]{0,1:T(4,128)S(1)} %get-tuple-element.591, f32[4,512]{1,0:T(4,128)S(1)} %broadcast_subtract_fusion.5, ...), kind=kLoop, calls=%fused_computation.55.clone.1 | loop fusion | flops 52422656 | bytes 143360 | tf_op jit(solution)/shard_map/while/body/eval_jaxpr/reduce_sum | solution.py:70
  297.3 38.7 %multiply_reduce_fusion.3 = (f32[4,512]{1,0:T(4,128)S(1)}, f32[4,512]{1,0:T(4,128)S(1)}, f32[4,512]{1,0:T(4,128)S(1)}) fusion(f32[1024,4]{0,1:T(4,128)S(1)} %get-tuple-element.589, f32[1024,4]{0,1:T(4,128)S(1)} %get-tuple-element.590, f32[1024,4]{0,1:T(4,128)S(1)} %get-tuple-element.591, f32[4,512]{1,0:T(4,128)S(1)} %broadcast_subtract_fusion.5, ...), kind=kLoop, calls=%fused_computation.55.clone.1 | loop fusion | flops 52422656 | bytes 143360 | tf_op jit(solution)/shard_map/while/body/eval_jaxpr/reduce_sum | solution.py:70
  339.0 38.8 %multiply_reduce_fusion.3 = (f32[4,512]{1,0:T(4,128)S(1)}, f32[4,512]{1,0:T(4,128)S(1)}, f32[4,512]{1,0:T(4,128)S(1)}) fusion(f32[1024,4]{0,1:T(4,128)S(1)} %get-tuple-element.589, f32[1024,4]{0,1:T(4,128)S(1)} %get-tuple-element.590, f32[1024,4]{0,1:T(4,128)S(1)} %get-tuple-element.591, f32[4,512]{1,0:T(4,128)S(1)} %broadcast_subtract_fusion.5, ...), kind=kLoop, calls=%fused_computation.55.clone.1 | loop fusion | flops 52422656 | bytes 143360 | tf_op jit(solution)/shard_map/while/body/eval_jaxpr/reduce_sum | solution.py:70
  377.9 2.6 copy.45
  380.5 45.6 %reduce-scatter.4.cloned.1.call-done = f32[2048,3]{1,0:T(8,128)} async-done(((f32[8192,3]{1,0:T(8,128)}), f32[2048,3]{1,0:T(8,128)}) %reduce-scatter.4.cloned.1.call-update) | async-done | bytes 24592
  426.1 2.2 copy.46
  (118 shorter events, 18.1 us)
Async XLA Ops:
  6.5 419.6 %reduce-scatter.4.cloned.1.call-start = ((), (), s32[]{:S(2)}) async-start(), calls=%async_computation.1 | async-start | bytes 5242880
Sparse Core Ops, SparseCore 0:
  380.7 45.3 reduce-scatter.3
where the time goes:
time: 436 us; the launch traced here: 435 us
  other arithmetic  323 us (74%)
  waiting for transfers between devices  45.6 us (10%)
  blocking collectives  43.5 us (10%)
  between operations  14.8 us (3%)
  local copies, waits for them, and re-layouts  7.56 us (2%)
    reduce_sum x4, other arithmetic, force_terms(): jnp.sum(unit_x[:, None] * in_plane, axis=0)  155 us
    mul x4, other arithmetic, block_moments(): upward * cosine  136 us
    unnamed x2, waiting for transfers between devices  45.6 us
    all_gather x1, blocking collectives, carry_coefficients(): all_totals = lax.all_gather(totals[None], 'slab', axis=0, tiled=True)  31.3 us
    reduce_sum x4, other arithmetic, block_moments(): jnp.sum(row_stack.reshape(4, mode_count, cosine.shape[1] // BLOCK, BLOCK)...  11.6 us
    neg x8, other arithmetic, phase_terms(): e_high = jnp.exp(-wave_norm[:, None] * (height - ion_depth))  10.5 us
  transfers between devices with their start and end apart: 1, of which 1 were waited for; matrix products, arithmetic and copies ran while one was open for 0% of the time, Pallas kernels for 0%

commit v1 on v0

v1 whole, which is shorter than its diff:
```python
import functools
import math

import jax
import jax.numpy as jnp
import numpy as np
from jax import lax
from jax.experimental import pallas as pl
from jax.experimental.pallas import tpu as pltpu
from jax.sharding import PartitionSpec as P

QDIM = 64
BLOCK = 512
MODES = 4096
PDIM = MODES // QDIM
HALF = QDIM // 2
LANES = 4 * HALF

two_pi = 2.0 * math.pi
slab_span = 0.08
box_low = 0.8

SIN_TERMS = (3.14159264, -5.16771008, 2.55007752, -0.59829129, 0.07765766)
COS_TERMS = (1.0, -4.93480214, 4.05870916, -1.335212, 0.23493731, -0.02439632)


def series_terms(height):
    a = 0.5 * height * two_pi * math.hypot(PDIM, HALF) / box_low
    nodes = np.cos(np.pi * (np.arange(64) + 0.5) / 64)
    order = np.arange(32)[:, None]
    coefficients = np.abs((np.exp(-a * (1.0 + nodes)) * np.cos(order * np.arccos(nodes))).sum(1) / 32.0)
    count = 4
    while coefficients[count:].sum() > 2.0**-24:
        count += 4
    return count


def poly(terms, u):
    value = jnp.full_like(u, terms[-1])
    for term in terms[-2::-1]:
        value = value * u + term
    return value


def turn(angle):
    r = angle - jnp.floor(angle + 0.5)
    u = r * r
    s = r * poly(SIN_TERMS, u)
    c = poly(COS_TERMS, u)
    return 1.0 - 2.0 * s * s, 2.0 * s * c


def split(x):
    high = x.astype(jnp.bfloat16)
    return high, (x - high.astype(jnp.float32)).astype(jnp.bfloat16)


def iota(shape, dim):
    return lax.broadcasted_iota(jnp.int32, shape, dim)


def roll(x, shift):
    return pltpu.roll(x, shift % LANES, x.ndim - 1)


def even_group(shape):
    return (iota(shape, 1) // HALF) % 2 == 0


def swap_groups(x):
    return jnp.where(even_group(x.shape), roll(x, -HALF), roll(x, HALF))


def half_sign(shape):
    return jnp.where(iota(shape, 1) < LANES // 2, -1.0, 1.0)


def wave(order_p, order_q, box_x, box_y):
    wave_x = two_pi * order_p / box_x
    wave_y = two_pi * order_q / box_y
    return wave_x, wave_y, jnp.sqrt(wave_x * wave_x + wave_y * wave_y)


def tile_orders():
    shape = (PDIM, LANES)
    p = (iota(shape, 0) + 1).astype(jnp.float32)
    j = iota(shape, 1) % HALF
    return p, j.astype(jnp.float32), (-1 - j).astype(jnp.float32)


def table_terms(count, height, box_x, box_y):
    p, q_plus, q_minus = tile_orders()
    even = even_group(p.shape)
    a = (0.5 * height) * wave(p, jnp.where(even, q_plus, q_minus), box_x, box_y)[2]
    ratio = jnp.zeros_like(a)
    ratios = {}
    for n in range(count + 6, 0, -1):
        ratio = a / (2.0 * n + a * ratio)
        ratios[n] = ratio
    products = [jnp.ones_like(a)]
    total = jnp.ones_like(a)
    for n in range(1, count + 7):
        products.append(products[-1] * ratios[n])
        total = total + 2.0 * products[n]
    first = 1.0 / total
    terms = [first] + [(2.0 * first) * products[n] for n in range(1, count)]
    plus, minus = [], []
    for m in range(count // 2):
        low, high = terms[2 * m], terms[2 * m + 1]
        plus.append(jnp.where(even, low, roll(high, HALF)))
        minus.append(jnp.where(even, roll(low, -HALF), high))
    return plus, minus


def moments_kernel(
    count, height, counts_ref, box_ref, positions_ref, charges_ref,
    totals_ref, decay_ref, before_ref, table_ref, high_ref, low_ref, phase_ref, weight_ref,
):
    ions = positions_ref.shape[1]
    blocks = ions // BLOCK
    pairs = count // 2
    slab_rank = lax.axis_index("slab")
    mode_rank = lax.axis_index("mode")
    box_x = jnp.full((1, 1), box_ref[0], jnp.float32)
    box_y = jnp.full((1, 1), box_ref[1], jnp.float32)
    live = counts_ref[slab_rank]
    lower_edge = slab_rank.astype(jnp.float32) * height
    scale = (2.0 * two_pi) / (box_x * box_y)

    plus, minus = table_terms(count, height, box_x, box_y)
    for m in range(pairs):
        table_ref[0, :, m * LANES : (m + 1) * LANES] = plus[m]
        table_ref[1, :, m * LANES : (m + 1) * LANES] = minus[m]

    rows = iota((8, BLOCK), 0).astype(jnp.float32)
    upward, downward = [], []
    tile = (PDIM, LANES)
    sign = half_sign(tile)
    group_sign = jnp.where(even_group(tile), 1.0, -1.0)
    found = []
    for b in range(blocks):
        span = slice(b * BLOCK, (b + 1) * BLOCK)
        x = positions_ref[0:1, span]
        y = positions_ref[1:2, span]
        t = (positions_ref[2:3, span] - lower_edge) * (2.0 / height) - 1.0
        slot = mode_rank * ions + b * BLOCK + iota((1, BLOCK), 1)
        weight = jnp.where(slot < live, charges_ref[0:1, span], 0.0)
        weight_ref[0:1, span] = weight * scale

        x8 = 8.0 * x
        y8 = 8.0 * y
        x8 = x8 - jnp.floor(x8)
        y8 = y8 - jnp.floor(y8)
        base_c, base_s = turn((rows + 1.0) * x - 0.5 * y)
        step_c, step_s = turn(rows * x8)
        phase_c, phase_s = [base_c], [base_s]
        for m in range(1, PDIM // 8):
            c, s = step_c[m : m + 1], step_s[m : m + 1]
            phase_c.append(base_c * c - base_s * s)
            phase_s.append(base_s * c + base_c * s)
        phase = jnp.concatenate(phase_c + phase_s, axis=0)
        phase_ref[:, span] = phase
        base_c, base_s = turn((rows + 0.5) * y)
        step_c, step_s = turn(rows * y8)
        side_c, side_s = [base_c], [base_s]
        for m in range(1, HALF // 8):
            c, s = step_c[m : m + 1], step_s[m : m + 1]
            side_c.append(base_c * c - base_s * s)
            side_s.append(base_s * c + base_c * s)
        sides = (jnp.concatenate(side_c, axis=0), jnp.concatenate(side_s, axis=0))

        powers = [jnp.ones_like(t), t]
        for n in range(2, count):
            powers.append(2.0 * t * powers[-1] - powers[-2])
        for m in range(pairs):
            for part in range(2):
                for parity in range(2):
                    at = m * LANES + part * 2 * HALF + parity * HALF
                    high, low = split(powers[2 * m + parity] * sides[part])
                    high_ref[at : at + HALF, span] = high
                    low_ref[at : at + HALF, span] = low

        heavy_high, heavy_low = split(phase * weight)
        both = jnp.concatenate([heavy_high, heavy_low], axis=0)
        across = (((1,), (1,)), ((), ()))
        first = lax.dot_general(both, high_ref[:, span], across, preferred_element_type=jnp.float32)
        second = lax.dot_general(heavy_high, low_ref[:, span], across, preferred_element_type=jnp.float32)
        moments = first[: 2 * PDIM] + first[2 * PDIM :] + second

        sums = [jnp.zeros(tile, jnp.float32) for _ in range(4)]
        for m in range(pairs):
            piece = moments[:, m * LANES : (m + 1) * LANES]
            for kind, values in enumerate((plus[m], minus[m])):
                sums[2 * kind] += values * piece[:PDIM]
                sums[2 * kind + 1] += values * piece[PDIM:]
        added = sums[0] + sign * roll(sums[1], LANES // 2)
        taken = roll(sums[3], LANES // 2) - sign * sums[2]
        found.append([swap_groups(v) + group_sign * v for v in (added, taken)])

    p, q_plus, q_minus = tile_orders()
    even = even_group(tile)
    for kind, order_q in enumerate((q_plus, q_minus)):
        wave_norm = wave(p, order_q, box_x, box_y)[2]
        boost = jnp.exp(wave_norm * height)
        prefix = [jnp.zeros(tile, jnp.float32)]
        for b in range(blocks):
            prefix.append(prefix[-1] + found[b][kind])
        total = prefix[-1]
        for b in range(blocks):
            before_ref[b, kind] = boost * jnp.where(even, prefix[b], total - prefix[b + 1])
        top, bottom = total[: PDIM // 2], total[PDIM // 2 :]
        small = even_group(top.shape)
        totals_ref[kind, 0] = jnp.where(small, top, roll(bottom, HALF))
        totals_ref[kind, 1] = jnp.where(small, roll(top, -HALF), bottom)
        depth = wave_norm * height
        decay_ref[kind] = jnp.where(small, depth[: PDIM // 2], depth[PDIM // 2 :])


def forces_kernel(
    count, box_ref, carry_ref, before_ref, table_ref, high_ref, low_ref, phase_ref, weight_ref,
    forces_ref, coarse_ref, fine_ref,
):
    blocks = before_ref.shape[0]
    pairs = count // 2
    box_x = jnp.full((1, 1), box_ref[0], jnp.float32)
    box_y = jnp.full((1, 1), box_ref[1], jnp.float32)
    tile = (PDIM, LANES)
    sign = half_sign(tile)
    group_sign = jnp.where(even_group(tile), 1.0, -1.0)
    p, q_plus, q_minus = tile_orders()
    base, units = [], []
    small = even_group((PDIM // 2, LANES))
    for kind, order_q in enumerate((q_plus, q_minus)):
        up, down = carry_ref[kind, 0], carry_ref[kind, 1]
        top = jnp.where(small, up, roll(down, HALF))
        bottom = jnp.where(small, roll(up, -HALF), down)
        base.append(jnp.concatenate([top, bottom], axis=0))
        wave_x, wave_y, wave_norm = wave(p, order_q, box_x, box_y)
        units.append((wave_x / wave_norm, wave_y / wave_norm))

    for b in range(blocks):
        span = slice(b * BLOCK, (b + 1) * BLOCK)
        sides = []
        for kind in range(2):
            held = base[kind] + before_ref[b, kind]
            mixed = held + group_sign * swap_groups(held)
            turned = sign * roll(mixed, LANES // 2)
            sides.append((units[kind][0] * turned, units[kind][1] * turned, -swap_groups(mixed)))
        for o in range(3):
            plus, minus = sides[0][o], sides[1][o]
            plus_rows = (plus, -sign * roll(plus, LANES // 2))
            minus_rows = (-sign * minus, roll(minus, LANES // 2))
            for m in range(pairs):
                lanes = slice(m * LANES, (m + 1) * LANES)
                table_plus = table_ref[0, :, lanes]
                table_minus = table_ref[1, :, lanes]
                for part in range(2):
                    at = (2 * o + part) * PDIM
                    high, low = split(table_plus * plus_rows[part] + table_minus * minus_rows[part])
                    coarse_ref[at : at + PDIM, lanes] = high
                    fine_ref[at : at + PDIM, lanes] = low
        field = jnp.dot(coarse_ref[...], high_ref[:, span], preferred_element_type=jnp.float32)
        field += jnp.dot(fine_ref[...], high_ref[:, span], preferred_element_type=jnp.float32)
        field += jnp.dot(coarse_ref[...], low_ref[:, span], preferred_element_type=jnp.float32)
        phase = phase_ref[:, span]
        for o in range(3):
            part = field[o * 2 * PDIM : (o + 1) * 2 * PDIM]
            forces_ref[o : o + 1, span] = jnp.sum(phase * part, axis=0, keepdims=True) * weight_ref[0:1, span]


def shards(positions, charges, counts, box):
    slab_count = lax.axis_size("slab")
    mode_parts = lax.axis_size("mode")
    slab_rank = lax.axis_index("slab")
    mode_rank = lax.axis_index("mode")
    height = slab_span / slab_count
    count = series_terms(height)
    ions = positions.shape[1]
    blocks = ions // BLOCK
    terms = count * 2 * HALF
    scalar = pl.BlockSpec(memory_space=pltpu.SMEM)
    vector = pl.BlockSpec(memory_space=pltpu.VMEM)
    params = pltpu.CompilerParams(vmem_limit_bytes=48 * 1024 * 1024)
    half = PDIM // 2
    totals, decay, before, table, high, low, phase, weight = pl.pallas_call(
        functools.partial(moments_kernel, count, height),
        out_shape=[
            pltpu.VMEM((2, 2, half, LANES), jnp.float32),
            pltpu.VMEM((2, half, LANES), jnp.float32),
            pltpu.VMEM((blocks, 2, PDIM, LANES), jnp.float32),
            pltpu.VMEM((2, PDIM, terms), jnp.float32),
            pltpu.VMEM((terms, ions), jnp.bfloat16),
            pltpu.VMEM((terms, ions), jnp.bfloat16),
            pltpu.VMEM((2 * PDIM, ions), jnp.float32),
            pltpu.VMEM((1, ions), jnp.float32),
        ],
        in_specs=[scalar, scalar, vector, vector],
        out_specs=[vector] * 8,
        compiler_params=params,
        name="moments",
    )(counts, box, positions, charges[None, :])

    gathered = lax.all_gather(totals, "mode", axis=0)
    slab_totals = jnp.sum(gathered, axis=0)
    slab_ids = jnp.arange(slab_count, dtype=jnp.int32)[:, None, None, None]
    sent = jnp.where(slab_ids > slab_rank, slab_totals[None, :, 0], slab_totals[None, :, 1])
    got = lax.all_to_all(sent, "slab", split_axis=0, concat_axis=0, tiled=True)
    gap = jnp.maximum(jnp.abs(slab_ids - slab_rank) - 1, 0).astype(jnp.float32)
    got = got * jnp.exp(-decay[None] * gap)
    boost = jnp.exp(decay)
    mode_ids = jnp.arange(mode_parts, dtype=jnp.int32)[:, None, None, None]
    up = jnp.sum(jnp.where(slab_ids < slab_rank, got, 0.0), axis=0)
    down = jnp.sum(jnp.where(slab_ids > slab_rank, got, 0.0), axis=0)
    up += boost * jnp.sum(jnp.where(mode_ids < mode_rank, gathered[:, :, 0], 0.0), axis=0)
    down += boost * jnp.sum(jnp.where(mode_ids > mode_rank, gathered[:, :, 1], 0.0), axis=0)
    carry = jnp.stack([up, down], axis=1)

    kept = [pltpu.with_memory_space_constraint(v, pltpu.VMEM) for v in (before, table, high, low, phase, weight)]
    return pl.pallas_call(
        functools.partial(forces_kernel, count),
        out_shape=jax.ShapeDtypeStruct((3, ions), jnp.float32),
        in_specs=[scalar] + [vector] * 7,
        out_specs=vector,
        scratch_shapes=[
            pltpu.VMEM((6 * PDIM, terms), jnp.bfloat16),
            pltpu.VMEM((6 * PDIM, terms), jnp.bfloat16),
        ],
        compiler_params=params,
        name="forces",
    )(box, carry, *kept)


def solution(mesh):
    return jax.shard_map(
        shards,
        mesh=mesh,
        in_specs=(P(None, ("slab", "mode")), P(("slab", "mode")), P(), P()),
        out_specs=P(None, ("slab", "mode")),
        check_vma=False,
    )
```

time: 436 us -> 48 us (0.11)
  other arithmetic: 323 us -> 8.63 us
  waiting for transfers between devices: 45.6 us -> 5.87 us
  blocking collectives: 43.5 us -> 7.63 us
  between operations: 14.8 us -> 0.04 us
  Pallas kernels: 0 us -> 10.4 us
  starting transfers between devices: 0.01 us -> 5.88 us
    reduce_sum x10 -> x3, other arithmetic: 168 us -> 4.4 us  [the longest x1 1.68 us: shards(): jnp.sum(jnp.where(mode_ids < mode_rank, gathered[:, :, 0], 0.0), axis=0)]
    mul x8 -> x0, other arithmetic: 136 us -> none  [the longest x4 136 us: block_moments(): upward * cosine]
    unnamed x2 -> x0, waiting for transfers between devices: 45.6 us -> none
    all_gather x3 -> x1, blocking collectives: 43.5 us -> 7.63 us  [shards(): gathered = lax.all_gather(totals, 'mode', axis=0)]
    pallas_call x0 -> x2, Pallas kernels: none -> 10.4 us  [the longest x1 6.6 us: shards(): pl.pallas_call(functools.partial(forces_kernel, count), out_shape=jax.Sha...]
    neg x8 -> x1, other arithmetic: 10.5 us -> 1.37 us  [shards(): got = got * jnp.exp(-decay[None] * gap)]
    all_to_all x0 -> x1, starting transfers between devices: none -> 5.88 us  [shards(): got = lax.all_to_all(sent, 'slab', split_axis=0, concat_axis=0, tiled=True)]
    all_to_all x0 -> x1, waiting for transfers between devices: none -> 5.87 us  [shards(): got = lax.all_to_all(sent, 'slab', split_axis=0, concat_axis=0, tiled=True)]
  transfers between devices with their start and end apart: 1 -> 1, of which waited for: 1 -> 1; matrix products, arithmetic and copies ran while one was open for 0% -> 8% of each run, Pallas kernels for 0% -> 0%
where the time goes in v1:
time: 48 us; the launch traced here: 47.2 us
  Pallas kernels  10.4 us (22%)
  local copies, waits for them, and re-layouts  8.78 us (18%)
  other arithmetic  8.63 us (18%)
  blocking collectives  7.63 us (16%)
  starting transfers between devices  5.88 us (12%)
  waiting for transfers between devices  5.87 us (12%)
    unnamed x14, local copies, waits for them, and re-layouts  8 us
    all_gather x1, blocking collectives, shards(): gathered = lax.all_gather(totals, 'mode', axis=0)  7.63 us
    pallas_call x1, Pallas kernels, shards(): pl.pallas_call(functools.partial(forces_kernel, count), out_shape=jax.Sha...  6.6 us
    all_to_all x1, starting transfers between devices, shards(): got = lax.all_to_all(sent, 'slab', split_axis=0, concat_axis=0, tiled=True)  5.88 us
    all_to_all x1, waiting for transfers between devices, shards(): got = lax.all_to_all(sent, 'slab', split_axis=0, concat_axis=0, tiled=True)  5.87 us
    pallas_call x1, Pallas kernels, shards(): pl.pallas_call(functools.partial(moments_kernel, count, height), out_shap...  3.83 us
    reduce_sum x1, other arithmetic, shards(): jnp.sum(jnp.where(mode_ids < mode_rank, gathered[:, :, 0], 0.0), axis=0)  1.68 us
    reduce_sum x1, other arithmetic, shards(): slab_totals = jnp.sum(gathered, axis=0)  1.61 us
  transfers between devices with their start and end apart: 1, of which 1 were waited for; matrix products, arithmetic and copies ran while one was open for 8% of the time, Pallas kernels for 0%

profile of v1, /device:TPU:0, one launch (start us, length us, event | category | flops | bytes accessed | tf_op | source)
XLA Modules:
  0.0 47.2 jit_solution(3374904721405480754)
XLA Ops:
  0.0 3.8 %moments.1 = (f32[2,2,32,128]{3,2,1,0:T(8,128)S(1)}, f32[2,32,128]{2,1,0:T(8,128)S(1)}, f32[4,2,64,128]{3,2,1,0:T(8,128)S(1)}, f32[2,64,768]{2,1,0:T(8,128)S(1)}...) custom-call(s32[8]{0:T(128)} %counts_ref.1, ...), custom_call_target="tpu_custom_call" | custom-call | tf_op jit(solution)/shard_map/moments/pallas_call | solution.py:285
  3.8 0.0 copy-start
  3.8 1.7 %copy-done = bf16[768,2048]{1,0:T(8,128)(2,1)} copy-done((bf16[768,2048]{1,0:T(8,128)(2,1)}, bf16[768,2048]{1,0:T(8,128)(2,1)S(1)}, u32[]{:S(2)}) %copy-start) | copy-done | bytes 3145752
  5.5 0.0 copy-start.2
  5.5 1.0 %copy-done.2 = f32[128,2048]{1,0:T(8,128)} copy-done((f32[128,2048]{1,0:T(8,128)}, f32[128,2048]{1,0:T(8,128)S(1)}, u32[]{:S(2)}) %copy-start.2) | copy-done | bytes 1048600
  6.5 0.0 copy-start.4
  6.5 0.7 %copy-done.4 = f32[4,2,64,128]{3,2,1,0:T(8,128)} copy-done((f32[4,2,64,128]{3,2,1,0:T(8,128)}, f32[4,2,64,128]{3,2,1,0:T(8,128)S(1)}, u32[]{:S(2)}) %copy-start.4) | copy-done | bytes 262168
  7.2 0.6 %copy-done.6 = f32[2,32,128]{2,1,0:T(8,128)} copy-done((f32[2,32,128]{2,1,0:T(8,128)}, f32[2,32,128]{2,1,0:T(8,128)S(1)}, u32[]{:S(2)}) %copy-start.6) | copy-done | bytes 32792
  7.8 7.6 %all-gather = f32[8,2,32,128]{3,2,1,0:T(8,128)} all-gather(f32[2,2,32,128]{3,2,1,0:T(8,128)S(1)} %get-tuple-element.13), channel_id=2, replica_groups=mesh['slab'=8,'mode'=4] {'mode'}, dimensions={0}, use_global_device_ids=true | all-gather | bytes 327680 | tf_op jit(solution)/shard_map/all_gather | solution.py:303
  15.4 1.6 %reduce_sum.45 = f32[2,2,32,128]{3,2,1,0:T(8,128)} reduce(f32[4,2,2,32,128]{4,3,2,1,0:T(8,128)} %bitcast.26, f32[]{:T(128)} %constant.12.clone.1), dimensions={0}, to_apply=%region_0.0 | reduce | flops 49152 | bytes 327684 | tf_op jit(solution)/shard_map/reduce_sum | solution.py:304
  17.0 0.8 %slice_bitcast_fusion.3 = (f32[2,32,128]{2,1,0:T(8,128)S(1)}, f32[2,32,128]{2,1,0:T(8,128)S(1)}) fusion(f32[2,2,32,128]{3,2,1,0:T(8,128)} %reduce_sum.45), kind=kLoop, calls=%fused_computation.12 | loop fusion | bytes 131072 | tf_op jit(solution)/shard_map/jit(_where)/broadcast_in_dim | solution.py:306
  17.8 0.8 %broadcast_select_fusion = f32[8,2,32,128]{3,2,1,0:T(8,128)} fusion(f32[2,32,128]{2,1,0:T(8,128)S(1)} %get-tuple-element.26, f32[2,32,128]{2,1,0:T(8,128)S(1)} %get-tuple-element.25, pred[8]{0:T(512)(128)(4,1)S(1)} %iota_compare_fusion.2), kind=kLoop, calls=%fused_computation.9 | loop fusion | flops 65536 | bytes 327688 | tf_op jit(solution)/shard_map/jit(_where)/select_n | solution.py:306
  18.6 5.9 %all-to-all-start = ((f32[8,2,32,128]{3,2,1,0:T(8,128)}), f32[8,2,32,128]{3,2,1,0:T(8,128)}, u32[]{:S(2)}, u32[]{:S(2)}) async-start(f32[8,2,32,128]{3,2,1,0:T(8,128)} %broadcast_select_fusion), calls=%async_computation | async-start | bytes 524288 | tf_op jit(solution)/shard_map/all_to_all | solution.py:307
  24.5 1.4 %neg.4 = f32[2,32,128]{2,1,0:T(8,128)} negate(f32[2,32,128]{2,1,0:T(8,128)} %copy-done.6) | non-fusion elementwise | flops 8192 | bytes 65536 | tf_op jit(solution)/shard_map/neg | solution.py:309
  25.9 0.6 %iota_compare_fusion.3 = pred[8]{0:T(512)(128)(4,1)} fusion(s32[]{:T(128)S(6)} %axis_index.23), kind=kLoop, calls=%fused_computation.19 | loop fusion | flops 8 | bytes 12 | tf_op jit(solution)/shard_map/lt | solution.py:312
  26.5 1.7 %fusion.3 = (f32[2,32,128]{2,1,0:T(8,128)}, f32[2,32,128]{2,1,0:T(8,128)}) fusion(f32[4,2,2,32,128]{4,3,2,1,0:T(8,128)} %bitcast.27, pred[4]{0:T(512)(128)(4,1)S(1)} %get-tuple-element.30, pred[4]{0:T(512)(128)(4,1)S(1)} %get-tuple-element.29), kind=kLoop, calls=%fused_computation.8 | loop fusion | flops 114688 | bytes 327688 | tf_op jit(solution)/shard_map/reduce_sum | solution.py:314
  28.1 5.9 %all-to-all-done = f32[8,2,32,128]{3,2,1,0:T(8,128)} async-done(((f32[8,2,32,128]{3,2,1,0:T(8,128)}), f32[8,2,32,128]{3,2,1,0:T(8,128)}, u32[]{:S(2)}, u32[]{:S(2)}) %all-to-all-start) | async-done | bytes 262176 | tf_op jit(solution)/shard_map/all_to_all | solution.py:307
  34.0 1.1 %select_reduce_fusion.1 = (f32[2,32,128]{2,1,0:T(8,128)S(1)}, f32[2,32,128]{2,1,0:T(8,128)S(1)}) fusion(f32[8,2,32,128]{3,2,1,0:T(8,128)} %all-to-all-done, f32[8]{0:T(128)S(1)} %maximum_convert_fusion, f32[2,32,128]{2,1,0:T(8,128)} %neg.4, pred[8]{0:T(512)(128)(4,1)} %iota_compare_fusion.3, pred[8]{0:T(512)(128)(4,1)S(1)} %iota_compare_fusion.2), kind=kLoop, calls=%fused_computation.1 | loop fusion | flops 376832 | bytes 360496 | tf_op jit(solution)/shard_map/reduce_sum | solution.py:312
  35.1 0.8 %add_bitcast_fusion.1 = (f32[2,1,32,128]{3,2,1,0:T(8,128)S(1)}, f32[2,1,32,128]{3,2,1,0:T(8,128)S(1)}) fusion(f32[2,32,128]{2,1,0:T(8,128)S(1)} %get-tuple-element.21, f32[2,32,128]{2,1,0:T(8,128)} %get-tuple-element.23, f32[2,32,128]{2,1,0:T(8,128)} %copy-done.6, f32[2,32,128]{2,1,0:T(8,128)S(1)} %get-tuple-element.22, f32[2,32,128]{2,1,0:T(8,128)} %get-tuple-element.24), kind=kLoop, calls=%fused_computation.14 | loop fusion | flops 32768 | bytes 229376 | tf_op jit(solution)/shard_map/stack | solution.py:316
  36.0 0.6 %pad_maximum_fusion.carry_ref = f32[2,2,32,128]{3,2,1,0:T(8,128)} fusion(f32[2,1,32,128]{3,2,1,0:T(8,128)S(1)} %get-tuple-element.28, f32[2,1,32,128]{3,2,1,0:T(8,128)S(1)} %get-tuple-element.27), kind=kLoop, calls=%fused_computation.10 | loop fusion | flops 16384 | bytes 131072 | tf_op jit(solution)/shard_map/stack | solution.py:316
  36.6 1.9 %copy-done.1 = bf16[768,2048]{1,0:T(8,128)(2,1)S(1)} copy-done((bf16[768,2048]{1,0:T(8,128)(2,1)S(1)}, bf16[768,2048]{1,0:T(8,128)(2,1)}, u32[]{:S(2)}) %copy-start.1) | copy-done | bytes 3145752
  38.5 1.2 %copy-done.3 = f32[128,2048]{1,0:T(8,128)S(1)} copy-done((f32[128,2048]{1,0:T(8,128)S(1)}, f32[128,2048]{1,0:T(8,128)}, u32[]{:S(2)}) %copy-start.3) | copy-done | bytes 1048600
  39.7 0.9 %copy-done.5 = f32[4,2,64,128]{3,2,1,0:T(8,128)S(1)} copy-done((f32[4,2,64,128]{3,2,1,0:T(8,128)S(1)}, f32[4,2,64,128]{3,2,1,0:T(8,128)}, u32[]{:S(2)}) %copy-start.5) | copy-done | bytes 262168
  40.6 6.6 %forces.1 = f32[3,2048]{1,0:T(4,128)} custom-call(f32[2]{0:T(128)} %box_ref.3, f32[2,2,32,128]{3,2,1,0:T(8,128)} %pad_maximum_fusion.carry_ref, f32[4,2,64,128]{3,2,1,0:T(8,128)S(1)} %copy-done.5, f32[2,64,768]{2,1,0:T(8,128)S(1)} %get-tuple-element.16.table_ref, bf16[768,2048]{1,0:T(8,128)(2,1)S(1)} %get-tuple-element.17.high_ref, ...), custom_call_target="tpu_custom_call" | custom-call | tf_op jit(solution)/shard_map/forces/pallas_call | solution.py:319
  (7 shorter events, 0.0 us)
Async XLA Ops:
  3.8 1.7 %copy-start = (bf16[768,2048]{1,0:T(8,128)(2,1)}, bf16[768,2048]{1,0:T(8,128)(2,1)S(1)}, u32[]{:S(2)}) copy-start(bf16[768,2048]{1,0:T(8,128)(2,1)S(1)} %get-tuple-element.18.low_ref) | copy-start | bytes 9437188
  5.5 1.0 %copy-start.2 = (f32[128,2048]{1,0:T(8,128)}, f32[128,2048]{1,0:T(8,128)S(1)}, u32[]{:S(2)}) copy-start(f32[128,2048]{1,0:T(8,128)S(1)} %get-tuple-element.19.phase_ref) | copy-start | bytes 3145732
  6.5 0.7 %copy-start.4 = (f32[4,2,64,128]{3,2,1,0:T(8,128)}, f32[4,2,64,128]{3,2,1,0:T(8,128)S(1)}, u32[]{:S(2)}) copy-start(f32[4,2,64,128]{3,2,1,0:T(8,128)S(1)} %get-tuple-element.15.before_ref) | copy-start | bytes 786436
  7.2 0.6 %copy-start.6 = (f32[2,32,128]{2,1,0:T(8,128)}, f32[2,32,128]{2,1,0:T(8,128)S(1)}, u32[]{:S(2)}) copy-start(f32[2,32,128]{2,1,0:T(8,128)S(1)} %get-tuple-element.14) | copy-start | bytes 98308
  18.6 15.4 %all-to-all-start = ((f32[8,2,32,128]{3,2,1,0:T(8,128)}), f32[8,2,32,128]{3,2,1,0:T(8,128)}, u32[]{:S(2)}, u32[]{:S(2)}) async-start(f32[8,2,32,128]{3,2,1,0:T(8,128)} %broadcast_select_fusion), calls=%async_computation | async-start | bytes 524288 | tf_op jit(solution)/shard_map/all_to_all | solution.py:307
  36.6 1.9 %copy-start.1 = (bf16[768,2048]{1,0:T(8,128)(2,1)S(1)}, bf16[768,2048]{1,0:T(8,128)(2,1)}, u32[]{:S(2)}) copy-start(bf16[768,2048]{1,0:T(8,128)(2,1)} %copy-done) | copy-start | bytes 9437188
  38.5 1.2 %copy-start.3 = (f32[128,2048]{1,0:T(8,128)S(1)}, f32[128,2048]{1,0:T(8,128)}, u32[]{:S(2)}) copy-start(f32[128,2048]{1,0:T(8,128)} %copy-done.2) | copy-start | bytes 3145732
  39.7 0.9 %copy-start.5 = (f32[4,2,64,128]{3,2,1,0:T(8,128)S(1)}, f32[4,2,64,128]{3,2,1,0:T(8,128)}, u32[]{:S(2)}) copy-start(f32[4,2,64,128]{3,2,1,0:T(8,128)} %copy-done.4) | copy-start | bytes 786436

commit v2 on v1

--- a/solution.py
+++ b/solution.py
@@ -114,7 +114,8 @@
 
 def moments_kernel(
     count, height, counts_ref, box_ref, positions_ref, charges_ref,
-    totals_ref, decay_ref, before_ref, table_ref, high_ref, low_ref, phase_ref, weight_ref,
+    totals_ref, decay_ref, before_ref, table_ref, weight_ref, high_out, low_out, phase_out,
+    high_ref, low_ref, phase_ref, sems,
 ):
     ions = positions_ref.shape[1]
     blocks = ions // BLOCK
@@ -137,7 +138,7 @@
     tile = (PDIM, LANES)
     sign = half_sign(tile)
     group_sign = jnp.where(even_group(tile), 1.0, -1.0)
-    found = []
+    found, copies = [], []
     for b in range(blocks):
         span = slice(b * BLOCK, (b + 1) * BLOCK)
         x = positions_ref[0:1, span]
@@ -159,7 +160,7 @@
             phase_c.append(base_c * c - base_s * s)
             phase_s.append(base_s * c + base_c * s)
         phase = jnp.concatenate(phase_c + phase_s, axis=0)
-        phase_ref[:, span] = phase
+        phase_ref[b] = phase
         base_c, base_s = turn((rows + 0.5) * y)
         step_c, step_s = turn(rows * y8)
         side_c, side_s = [base_c], [base_s]
@@ -177,14 +178,17 @@
                 for parity in range(2):
                     at = m * LANES + part * 2 * HALF + parity * HALF
                     high, low = split(powers[2 * m + parity] * sides[part])
-                    high_ref[at : at + HALF, span] = high
-                    low_ref[at : at + HALF, span] = low
+                    high_ref[b, at : at + HALF] = high
+                    low_ref[b, at : at + HALF] = low
+        for i, (held, out) in enumerate(((high_ref, high_out), (low_ref, low_out), (phase_ref, phase_out))):
+            copies.append(pltpu.make_async_copy(held.at[b], out.at[b], sems.at[i, b]))
+            copies[-1].start()
 
         heavy_high, heavy_low = split(phase * weight)
         both = jnp.concatenate([heavy_high, heavy_low], axis=0)
         across = (((1,), (1,)), ((), ()))
-        first = lax.dot_general(both, high_ref[:, span], across, preferred_element_type=jnp.float32)
-        second = lax.dot_general(heavy_high, low_ref[:, span], across, preferred_element_type=jnp.float32)
+        first = lax.dot_general(both, high_ref[b], across, preferred_element_type=jnp.float32)
+        second = lax.dot_general(heavy_high, low_ref[b], across, preferred_element_type=jnp.float32)
         moments = first[: 2 * PDIM] + first[2 * PDIM :] + second
 
         sums = [jnp.zeros(tile, jnp.float32) for _ in range(4)]
@@ -214,13 +218,20 @@
         totals_ref[kind, 1] = jnp.where(small, roll(top, -HALF), bottom)
         depth = wave_norm * height
         decay_ref[kind] = jnp.where(small, depth[: PDIM // 2], depth[PDIM // 2 :])
+    for copy in copies:
+        copy.wait()
 
 
 def forces_kernel(
-    count, box_ref, carry_ref, before_ref, table_ref, high_ref, low_ref, phase_ref, weight_ref,
-    forces_ref, coarse_ref, fine_ref,
+    count, box_ref, carry_ref, before_ref, table_ref, weight_ref, high_in, low_in, phase_in,
+    forces_ref, coarse_ref, fine_ref, high_ref, low_ref, phase_ref, sems,
 ):
     blocks = before_ref.shape[0]
+    copies = []
+    for b in range(blocks):
+        for i, (source, held) in enumerate(((high_in, high_ref), (low_in, low_ref), (phase_in, phase_ref))):
+            copies.append(pltpu.make_async_copy(source.at[b], held.at[b], sems.at[i, b]))
+            copies[-1].start()
     pairs = count // 2
     box_x = jnp.full((1, 1), box_ref[0], jnp.float32)
     box_y = jnp.full((1, 1), box_ref[1], jnp.float32)
@@ -259,75 +270,92 @@
                     high, low = split(table_plus * plus_rows[part] + table_minus * minus_rows[part])
                     coarse_ref[at : at + PDIM, lanes] = high
                     fine_ref[at : at + PDIM, lanes] = low
-        field = jnp.dot(coarse_ref[...], high_ref[:, span], preferred_element_type=jnp.float32)
-        field += jnp.dot(fine_ref[...], high_ref[:, span], preferred_element_type=jnp.float32)
-        field += jnp.dot(coarse_ref[...], low_ref[:, span], preferred_element_type=jnp.float32)
-        phase = phase_ref[:, span]
+        for copy in copies[3 * b : 3 * b + 3]:
+            copy.wait()
+        field = jnp.dot(coarse_ref[...], high_ref[b], preferred_element_type=jnp.float32)
+        field += jnp.dot(fine_ref[...], high_ref[b], preferred_element_type=jnp.float32)
+        field += jnp.dot(coarse_ref[...], low_ref[b], preferred_element_type=jnp.float32)
+        phase = phase_ref[b]
         for o in range(3):
             part = field[o * 2 * PDIM : (o + 1) * 2 * PDIM]
             forces_ref[o : o + 1, span] = jnp.sum(phase * part, axis=0, keepdims=True) * weight_ref[0:1, span]
 
 
+def exchange(totals, decay, parts, axis):
+    rank = lax.axis_index(axis)
+    part = jnp.arange(2, dtype=jnp.int32)[None, :, None, None]
+    outside = jnp.zeros_like(totals)
+    stride = 1
+    while stride < parts:
+        other = lax.ppermute(totals, axis, [(i, i ^ stride) for i in range(parts)])
+        upper = (rank // stride) % 2
+        ahead = part != upper
+        below = rank % stride
+        steps = jnp.where(part == 0, below, stride - 1 - below)
+        if decay is None:
+            outside = outside + jnp.where(ahead, other, 0.0)
+            totals = totals + other
+        else:
+            outside = outside + jnp.where(ahead, other * jnp.exp(-decay * steps.astype(jnp.float32)), 0.0)
+            fade = jnp.exp(-decay * float(stride))
+            totals = jnp.where(ahead, totals + fade * other, other + fade * totals)
+        stride *= 2
+    return outside, totals
+
+
 def shards(positions, charges, counts, box):
     slab_count = lax.axis_size("slab")
     mode_parts = lax.axis_size("mode")
-    slab_rank = lax.axis_index("slab")
-    mode_rank = lax.axis_index("mode")
     height = slab_span / slab_count
     count = series_terms(height)
     ions = positions.shape[1]
     blocks = ions // BLOCK
     terms = count * 2 * HALF
+    half = PDIM // 2
     scalar = pl.BlockSpec(memory_space=pltpu.SMEM)
     vector = pl.BlockSpec(memory_space=pltpu.VMEM)
-    params = pltpu.CompilerParams(vmem_limit_bytes=48 * 1024 * 1024)
-    half = PDIM // 2
-    totals, decay, before, table, high, low, phase, weight = pl.pallas_call(
+    apart = pl.BlockSpec(memory_space=pltpu.HBM)
+    params = pltpu.CompilerParams(vmem_limit_bytes=24 * 1024 * 1024)
+    kept = [((blocks, terms, BLOCK), jnp.bfloat16)] * 2 + [((blocks, 2 * PDIM, BLOCK), jnp.float32)]
+    held = [pltpu.VMEM(*v) for v in kept] + [pltpu.SemaphoreType.DMA((3, blocks))]
+    counts, box, positions, charges = [
+        pltpu.with_memory_space_constraint(v, pltpu.HBM) for v in (counts, box, positions, charges[None, :])
+    ]
+    totals, decay, *small, high, low, phase = pl.pallas_call(
         functools.partial(moments_kernel, count, height),
         out_shape=[
             pltpu.VMEM((2, 2, half, LANES), jnp.float32),
             pltpu.VMEM((2, half, LANES), jnp.float32),
             pltpu.VMEM((blocks, 2, PDIM, LANES), jnp.float32),
             pltpu.VMEM((2, PDIM, terms), jnp.float32),
-            pltpu.VMEM((terms, ions), jnp.bfloat16),
-            pltpu.VMEM((terms, ions), jnp.bfloat16),
-            pltpu.VMEM((2 * PDIM, ions), jnp.float32),
             pltpu.VMEM((1, ions), jnp.float32),
-        ],
+        ] + [pltpu.HBM(*v) for v in kept],
         in_specs=[scalar, scalar, vector, vector],
-        out_specs=[vector] * 8,
+        out_specs=[vector] * 5 + [apart] * 3,
+        scratch_shapes=held,
         compiler_params=params,
         name="moments",
-    )(counts, box, positions, charges[None, :])
-
-    gathered = lax.all_gather(totals, "mode", axis=0)
-    slab_totals = jnp.sum(gathered, axis=0)
-    slab_ids = jnp.arange(slab_count, dtype=jnp.int32)[:, None, None, None]
-    sent = jnp.where(slab_ids > slab_rank, slab_totals[None, :, 0], slab_totals[None, :, 1])
-    got = lax.all_to_all(sent, "slab", split_axis=0, concat_axis=0, tiled=True)
-    gap = jnp.maximum(jnp.abs(slab_ids - slab_rank) - 1, 0).astype(jnp.float32)
-    got = got * jnp.exp(-decay[None] * gap)
-    boost = jnp.exp(decay)
-    mode_ids = jnp.arange(mode_parts, dtype=jnp.int32)[:, None, None, None]
-    up = jnp.sum(jnp.where(slab_ids < slab_rank, got, 0.0), axis=0)
-    down = jnp.sum(jnp.where(slab_ids > slab_rank, got, 0.0), axis=0)
-    up += boost * jnp.sum(jnp.where(mode_ids < mode_rank, gathered[:, :, 0], 0.0), axis=0)
-    down += boost * jnp.sum(jnp.where(mode_ids > mode_rank, gathered[:, :, 1], 0.0), axis=0)
-    carry = jnp.stack([up, down], axis=1)
-
-    kept = [pltpu.with_memory_space_constraint(v, pltpu.VMEM) for v in (before, table, high, low, phase, weight)]
+    )(counts, box, positions, charges)
+
+    inside, slab_totals = exchange(totals, None, mode_parts, "mode")
+    depth = decay[:, None]
+    carry, _ = exchange(slab_totals, depth, slab_count, "slab")
+    carry = carry + jnp.exp(depth) * inside
+
+    carry, *small = [pltpu.with_memory_space_constraint(v, pltpu.VMEM) for v in (carry, *small)]
+    high, low, phase = [pltpu.with_memory_space_constraint(v, pltpu.HBM) for v in (high, low, phase)]
     return pl.pallas_call(
         functools.partial(forces_kernel, count),
         out_shape=jax.ShapeDtypeStruct((3, ions), jnp.float32),
-        in_specs=[scalar] + [vector] * 7,
+        in_specs=[scalar] + [vector] * 4 + [apart] * 3,
         out_specs=vector,
         scratch_shapes=[
             pltpu.VMEM((6 * PDIM, terms), jnp.bfloat16),
             pltpu.VMEM((6 * PDIM, terms), jnp.bfloat16),
-        ],
+        ] + held,
         compiler_params=params,
         name="forces",
-    )(box, carry, *kept)
+    )(box, carry, *small, high, low, phase)
 
 
 def solution(mesh):

time: 48 us -> 34.6 us (0.72); the launches traced: 47.2 us -> 34.4 us
  local copies, waits for them, and re-layouts: 8.78 us -> 0 us
  other arithmetic: 8.63 us -> 0.34 us
  blocking collectives: 7.63 us -> 0 us
  starting transfers between devices: 5.88 us -> 11 us
  waiting for transfers between devices: 5.87 us -> 10.2 us
  Pallas kernels: 10.4 us -> 12.9 us
    ppermute x0 -> x5, starting transfers between devices: none -> 11 us  [exchange(): other = lax.ppermute(totals, axis, [(i, i ^ stride) for i in range(parts)])]
    ppermute x0 -> x5, waiting for transfers between devices: none -> 10.2 us  [exchange(): other = lax.ppermute(totals, axis, [(i, i ^ stride) for i in range(parts)])]
    unnamed x14 -> x0, local copies, waits for them, and re-layouts: 8 us -> none
    all_gather x1 -> x0, blocking collectives: 7.63 us -> none  [shards(): gathered = lax.all_gather(totals, 'mode', axis=0)]
    all_to_all x1 -> x0, starting transfers between devices: 5.88 us -> none  [shards(): got = lax.all_to_all(sent, 'slab', split_axis=0, concat_axis=0, tiled=True)]
    all_to_all x1 -> x0, waiting for transfers between devices: 5.87 us -> none  [shards(): got = lax.all_to_all(sent, 'slab', split_axis=0, concat_axis=0, tiled=True)]
    reduce_sum x3 -> x0, other arithmetic: 4.4 us -> none  [the longest x1 1.68 us: shards(): jnp.sum(jnp.where(mode_ids < mode_rank, gathered[:, :, 0], 0.0), axis=0)]
    another operation x2 -> x0, other arithmetic: 1.44 us -> none  [shards(): carry = jnp.stack([up, down], axis=1)]
  transfers between devices with their start and end apart: 1 -> 5, of which waited for: 1 -> 5; matrix products, arithmetic and copies ran while one was open for 8% -> 0% of each run, Pallas kernels for 0% -> 0%
where the time goes in v2:
time: 34.6 us; the launch traced here: 34.4 us
  Pallas kernels  12.9 us (37%)
  starting transfers between devices  11 us (32%)
  waiting for transfers between devices  10.2 us (29%)
    ppermute x5, starting transfers between devices, exchange(): other = lax.ppermute(totals, axis, [(i, i ^ stride) for i in range(parts)])  11 us
    ppermute x5, waiting for transfers between devices, exchange(): other = lax.ppermute(totals, axis, [(i, i ^ stride) for i in range(parts)])  10.2 us
    pallas_call x1, Pallas kernels, shards(): pl.pallas_call(functools.partial(forces_kernel, count), out_shape=jax.Sha...  7.68 us
    pallas_call x1, Pallas kernels, shards(): pl.pallas_call(functools.partial(moments_kernel, count, height), out_shap...  5.18 us
  transfers between devices with their start and end apart: 5, of which 5 were waited for; matrix products, arithmetic and copies ran while one was open for 0% of the time, Pallas kernels for 0%

profile of v2, /device:TPU:0, one launch (start us, length us, event | category | flops | bytes accessed | tf_op | source)
XLA Modules:
  0.0 34.4 jit_solution(9655361412714893670)
XLA Ops:
  0.0 5.2 %moments.1 = (f32[2,2,32,128]{3,2,1,0:T(8,128)S(1)}, f32[2,32,128]{2,1,0:T(8,128)S(1)}, f32[4,2,64,128]{3,2,1,0:T(8,128)S(1)}, f32[2,64,768]{2,1,0:T(8,128)S(1)}...) custom-call(s32[8]{0:T(128)} %counts_ref.1, ...), custom_call_target="tpu_custom_call" | custom-call | tf_op jit(solution)/shard_map/moments/pallas_call | solution.py:324
  5.2 0.5 %collective-permute-start = (f32[2,2,32,128]{3,2,1,0:T(8,128)S(1)}, f32[2,2,32,128]{3,2,1,0:T(8,128)S(1)}, u32[]{:S(2)}, u32[]{:S(2)}) collective-permute-start(f32[2,2,32,128]{3,2,1,0:T(8,128)S(1)} %get-tuple-element.13), channel_id=1, source_target_pairs={{0,1},{1,0},{2,3},{3,2},{4,5},{5,4},{6,7},{7,6},{8,9},{9,8},{10,11... | collective-permute-start | bytes 196616 | tf_op jit(solution)/shard_map/ppermute | solution.py:290
  5.8 0.8 %collective-permute-done = f32[2,2,32,128]{3,2,1,0:T(8,128)S(1)} collective-permute-done((f32[2,2,32,128]{3,2,1,0:T(8,128)S(1)}, f32[2,2,32,128]{3,2,1,0:T(8,128)S(1)}, u32[]{:S(2)}, u32[]{:S(2)}) %collective-permute-start) | collective-permute-done | bytes 65568 | tf_op jit(solution)/shard_map/ppermute | solution.py:290
  6.6 2.9 %collective-permute-start.1 = (f32[2,2,32,128]{3,2,1,0:T(8,128)S(1)}, f32[2,2,32,128]{3,2,1,0:T(8,128)S(1)}, u32[]{:S(2)}, u32[]{:S(2)}) collective-permute-start(f32[2,2,32,128]{3,2,1,0:T(8,128)S(1)} %add.57), channel_id=1, source_target_pairs={{0,2},{1,3},{2,0},{3,1},{4,6},{5,7},{6,4},{7,5},{8,10},{9,11},{10,... | collective-permute-start | bytes 196616 | tf_op jit(solution)/shard_map/ppermute | solution.py:290
  9.5 2.4 %collective-permute-done.1 = f32[2,2,32,128]{3,2,1,0:T(8,128)S(1)} collective-permute-done((f32[2,2,32,128]{3,2,1,0:T(8,128)S(1)}, f32[2,2,32,128]{3,2,1,0:T(8,128)S(1)}, u32[]{:S(2)}, u32[]{:S(2)}) %collective-permute-start.1) | collective-permute-done | bytes 65568 | tf_op jit(solution)/shard_map/ppermute | solution.py:290
  12.0 1.9 %collective-permute-start.2 = (f32[2,2,32,128]{3,2,1,0:T(8,128)S(1)}, f32[2,2,32,128]{3,2,1,0:T(8,128)S(1)}, u32[]{:S(2)}, u32[]{:S(2)}) collective-permute-start(f32[2,2,32,128]{3,2,1,0:T(8,128)S(1)} %add.58), channel_id=1, source_target_pairs={{0,4},{4,0},{8,12},{12,8},{16,20},{20,16},{24,28},{28,24},{1,5},{5... | collective-permute-start | bytes 196616 | tf_op jit(solution)/shard_map/ppermute | solution.py:290
  13.9 2.4 %collective-permute-done.2 = f32[2,2,32,128]{3,2,1,0:T(8,128)S(1)} collective-permute-done((f32[2,2,32,128]{3,2,1,0:T(8,128)S(1)}, f32[2,2,32,128]{3,2,1,0:T(8,128)S(1)}, u32[]{:S(2)}, u32[]{:S(2)}) %collective-permute-start.2) | collective-permute-done | bytes 65568 | tf_op jit(solution)/shard_map/ppermute | solution.py:290
  16.3 0.1 add_select_fusion.1
  16.4 2.0 %collective-permute-start.3 = (f32[2,2,32,128]{3,2,1,0:T(8,128)S(1)}, f32[2,2,32,128]{3,2,1,0:T(8,128)S(1)}, u32[]{:S(2)}, u32[]{:S(2)}) collective-permute-start(f32[2,2,32,128]{3,2,1,0:T(8,128)S(1)} %add_select_fusion.1), channel_id=1, source_target_pairs={{0,8},{4,12},{8,0},{12,4},{16,24},{20,28},{24,16},{28,20},{1,9},{5... | collective-permute-start | bytes 196616 | tf_op jit(solution)/shard_map/ppermute | solution.py:290
  18.3 2.3 %collective-permute-done.3 = f32[2,2,32,128]{3,2,1,0:T(8,128)S(1)} collective-permute-done((f32[2,2,32,128]{3,2,1,0:T(8,128)S(1)}, f32[2,2,32,128]{3,2,1,0:T(8,128)S(1)}, u32[]{:S(2)}, u32[]{:S(2)}) %collective-permute-start.3) | collective-permute-done | bytes 65568 | tf_op jit(solution)/shard_map/ppermute | solution.py:290
  20.6 0.1 add_select_fusion
  20.7 3.6 %collective-permute-start.4 = (f32[2,2,32,128]{3,2,1,0:T(8,128)S(1)}, f32[2,2,32,128]{3,2,1,0:T(8,128)S(1)}, u32[]{:S(2)}, u32[]{:S(2)}) collective-permute-start(f32[2,2,32,128]{3,2,1,0:T(8,128)S(1)} %add_select_fusion), channel_id=1, source_target_pairs={{0,16},{4,20},{8,24},{12,28},{16,0},{20,4},{24,8},{28,12},{1,17},{... | collective-permute-start | bytes 196616 | tf_op jit(solution)/shard_map/ppermute | solution.py:290
  24.4 2.3 %collective-permute-done.4 = f32[2,2,32,128]{3,2,1,0:T(8,128)S(1)} collective-permute-done((f32[2,2,32,128]{3,2,1,0:T(8,128)S(1)}, f32[2,2,32,128]{3,2,1,0:T(8,128)S(1)}, u32[]{:S(2)}, u32[]{:S(2)}) %collective-permute-start.4) | collective-permute-done | bytes 65568 | tf_op jit(solution)/shard_map/ppermute | solution.py:290
  26.6 0.1 multiply_add_fusion.carry_ref
  26.7 7.7 %forces.1 = f32[3,2048]{1,0:T(4,128)} custom-call(f32[2]{0:T(128)} %box_ref.3, f32[2,2,32,128]{3,2,1,0:T(8,128)S(1)} %multiply_add_fusion.carry_ref, f32[4,2,64,128]{3,2,1,0:T(8,128)S(1)} %get-tuple-element.15.before_ref, f32[2,64,768]{2,1,0:T(8,128)S(1)} %get-tuple-element.16.table_ref, f32[1,2048]{1,0:T(1,128)S(1)} %get-tuple-element.17.weight_ref, ...), custom_call_target="tpu_custom_call" | custom-call | tf_op jit(solution)/shard_map/forces/pallas_call | solution.py:347
  (8 shorter events, 0.1 us)
Async XLA Ops:
  5.2 1.4 %collective-permute-start = (f32[2,2,32,128]{3,2,1,0:T(8,128)S(1)}, f32[2,2,32,128]{3,2,1,0:T(8,128)S(1)}, u32[]{:S(2)}, u32[]{:S(2)}) collective-permute-start(f32[2,2,32,128]{3,2,1,0:T(8,128)S(1)} %get-tuple-element.13), channel_id=1, source_target_pairs={{0,1},{1,0},{2,3},{3,2},{4,5},{5,4},{6,7},{7,6},{8,9},{9,8},{10,11... | collective-permute-start | bytes 196616 | tf_op jit(solution)/shard_map/ppermute | solution.py:290
  6.6 5.3 %collective-permute-start.1 = (f32[2,2,32,128]{3,2,1,0:T(8,128)S(1)}, f32[2,2,32,128]{3,2,1,0:T(8,128)S(1)}, u32[]{:S(2)}, u32[]{:S(2)}) collective-permute-start(f32[2,2,32,128]{3,2,1,0:T(8,128)S(1)} %add.57), channel_id=1, source_target_pairs={{0,2},{1,3},{2,0},{3,1},{4,6},{5,7},{6,4},{7,5},{8,10},{9,11},{10,... | collective-permute-start | bytes 196616 | tf_op jit(solution)/shard_map/ppermute | solution.py:290
  12.0 4.3 %collective-permute-start.2 = (f32[2,2,32,128]{3,2,1,0:T(8,128)S(1)}, f32[2,2,32,128]{3,2,1,0:T(8,128)S(1)}, u32[]{:S(2)}, u32[]{:S(2)}) collective-permute-start(f32[2,2,32,128]{3,2,1,0:T(8,128)S(1)} %add.58), channel_id=1, source_target_pairs={{0,4},{4,0},{8,12},{12,8},{16,20},{20,16},{24,28},{28,24},{1,5},{5... | collective-permute-start | bytes 196616 | tf_op jit(solution)/shard_map/ppermute | solution.py:290
  16.4 4.3 %collective-permute-start.3 = (f32[2,2,32,128]{3,2,1,0:T(8,128)S(1)}, f32[2,2,32,128]{3,2,1,0:T(8,128)S(1)}, u32[]{:S(2)}, u32[]{:S(2)}) collective-permute-start(f32[2,2,32,128]{3,2,1,0:T(8,128)S(1)} %add_select_fusion.1), channel_id=1, source_target_pairs={{0,8},{4,12},{8,0},{12,4},{16,24},{20,28},{24,16},{28,20},{1,9},{5... | collective-permute-start | bytes 196616 | tf_op jit(solution)/shard_map/ppermute | solution.py:290
  20.7 5.9 %collective-permute-start.4 = (f32[2,2,32,128]{3,2,1,0:T(8,128)S(1)}, f32[2,2,32,128]{3,2,1,0:T(8,128)S(1)}, u32[]{:S(2)}, u32[]{:S(2)}) collective-permute-start(f32[2,2,32,128]{3,2,1,0:T(8,128)S(1)} %add_select_fusion), channel_id=1, source_target_pairs={{0,16},{4,20},{8,24},{12,28},{16,0},{20,4},{24,8},{28,12},{1,17},{... | collective-permute-start | bytes 196616 | tf_op jit(solution)/shard_map/ppermute | solution.py:290

commit v3 on v2

--- a/solution.py
+++ b/solution.py
@@ -112,10 +112,21 @@
     return plus, minus
 
 
+def spread(count, powers, sides, high_ref, low_ref):
+    for m in range(count // 2):
+        for part in range(2):
+            for parity in range(2):
+                at = m * LANES + part * 2 * HALF + parity * HALF
+                n = 2 * m + parity
+                high, low = split(powers[n : n + 1] * sides[part * HALF : (part + 1) * HALF])
+                high_ref[at : at + HALF] = high
+                low_ref[at : at + HALF] = low
+
+
 def moments_kernel(
     count, height, counts_ref, box_ref, positions_ref, charges_ref,
-    totals_ref, decay_ref, before_ref, table_ref, weight_ref, high_out, low_out, phase_out,
-    high_ref, low_ref, phase_ref, sems,
+    totals_ref, decay_ref, before_ref, table_ref, weight_ref, phase_ref, sides_ref, powers_ref,
+    high_ref, low_ref,
 ):
     ions = positions_ref.shape[1]
     blocks = ions // BLOCK
@@ -138,7 +149,7 @@
     tile = (PDIM, LANES)
     sign = half_sign(tile)
     group_sign = jnp.where(even_group(tile), 1.0, -1.0)
-    found, copies = [], []
+    found = []
     for b in range(blocks):
         span = slice(b * BLOCK, (b + 1) * BLOCK)
         x = positions_ref[0:1, span]
@@ -168,21 +179,15 @@
             c, s = step_c[m : m + 1], step_s[m : m + 1]
             side_c.append(base_c * c - base_s * s)
             side_s.append(base_s * c + base_c * s)
-        sides = (jnp.concatenate(side_c, axis=0), jnp.concatenate(side_s, axis=0))
+        sides = jnp.concatenate(side_c + side_s, axis=0)
+        sides_ref[b] = sides
 
         powers = [jnp.ones_like(t), t]
         for n in range(2, count):
             powers.append(2.0 * t * powers[-1] - powers[-2])
-        for m in range(pairs):
-            for part in range(2):
-                for parity in range(2):
-                    at = m * LANES + part * 2 * HALF + parity * HALF
-                    high, low = split(powers[2 * m + parity] * sides[part])
-                    high_ref[b, at : at + HALF] = high
-                    low_ref[b, at : at + HALF] = low
-        for i, (held, out) in enumerate(((high_ref, high_out), (low_ref, low_out), (phase_ref, phase_out))):
-            copies.append(pltpu.make_async_copy(held.at[b], out.at[b], sems.at[i, b]))
-            copies[-1].start()
+        powers = jnp.concatenate(powers, axis=0)
+        powers_ref[b] = powers
+        spread(count, powers, sides, high_ref.at[b], low_ref.at[b])
 
         heavy_high, heavy_low = split(phase * weight)
         both = jnp.concatenate([heavy_high, heavy_low], axis=0)
@@ -218,20 +223,13 @@
         totals_ref[kind, 1] = jnp.where(small, roll(top, -HALF), bottom)
         depth = wave_norm * height
         decay_ref[kind] = jnp.where(small, depth[: PDIM // 2], depth[PDIM // 2 :])
-    for copy in copies:
-        copy.wait()
 
 
 def forces_kernel(
-    count, box_ref, carry_ref, before_ref, table_ref, weight_ref, high_in, low_in, phase_in,
-    forces_ref, coarse_ref, fine_ref, high_ref, low_ref, phase_ref, sems,
+    count, box_ref, carry_ref, before_ref, table_ref, weight_ref, phase_ref, sides_ref, powers_ref,
+    forces_ref, coarse_ref, fine_ref, high_ref, low_ref,
 ):
     blocks = before_ref.shape[0]
-    copies = []
-    for b in range(blocks):
-        for i, (source, held) in enumerate(((high_in, high_ref), (low_in, low_ref), (phase_in, phase_ref))):
-            copies.append(pltpu.make_async_copy(source.at[b], held.at[b], sems.at[i, b]))
-            copies[-1].start()
     pairs = count // 2
     box_x = jnp.full((1, 1), box_ref[0], jnp.float32)
     box_y = jnp.full((1, 1), box_ref[1], jnp.float32)
@@ -270,8 +268,7 @@
                     high, low = split(table_plus * plus_rows[part] + table_minus * minus_rows[part])
                     coarse_ref[at : at + PDIM, lanes] = high
                     fine_ref[at : at + PDIM, lanes] = low
-        for copy in copies[3 * b : 3 * b + 3]:
-            copy.wait()
+        spread(count, powers_ref[b], sides_ref[b], high_ref.at[b], low_ref.at[b])
         field = jnp.dot(coarse_ref[...], high_ref[b], preferred_element_type=jnp.float32)
         field += jnp.dot(fine_ref[...], high_ref[b], preferred_element_type=jnp.float32)
         field += jnp.dot(coarse_ref[...], low_ref[b], preferred_element_type=jnp.float32)
@@ -287,11 +284,15 @@
     outside = jnp.zeros_like(totals)
     stride = 1
     while stride < parts:
-        other = lax.ppermute(totals, axis, [(i, i ^ stride) for i in range(parts)])
         upper = (rank // stride) % 2
         ahead = part != upper
         below = rank % stride
         steps = jnp.where(part == 0, below, stride - 1 - below)
+        pairs = [(i, i ^ stride) for i in range(parts)]
+        if decay is not None and 2 * stride == parts:
+            other = lax.ppermute(jnp.where(upper == 0, totals[:, 0], totals[:, 1]), axis, pairs)[:, None]
+        else:
+            other = lax.ppermute(totals, axis, pairs)
         if decay is None:
             outside = outside + jnp.where(ahead, other, 0.0)
             totals = totals + other
@@ -314,14 +315,12 @@
     half = PDIM // 2
     scalar = pl.BlockSpec(memory_space=pltpu.SMEM)
     vector = pl.BlockSpec(memory_space=pltpu.VMEM)
-    apart = pl.BlockSpec(memory_space=pltpu.HBM)
     params = pltpu.CompilerParams(vmem_limit_bytes=24 * 1024 * 1024)
-    kept = [((blocks, terms, BLOCK), jnp.bfloat16)] * 2 + [((blocks, 2 * PDIM, BLOCK), jnp.float32)]
-    held = [pltpu.VMEM(*v) for v in kept] + [pltpu.SemaphoreType.DMA((3, blocks))]
+    work = [pltpu.VMEM((blocks, terms, BLOCK), jnp.bfloat16)] * 2
     counts, box, positions, charges = [
         pltpu.with_memory_space_constraint(v, pltpu.HBM) for v in (counts, box, positions, charges[None, :])
     ]
-    totals, decay, *small, high, low, phase = pl.pallas_call(
+    totals, decay, *kept = pl.pallas_call(
         functools.partial(moments_kernel, count, height),
         out_shape=[
             pltpu.VMEM((2, 2, half, LANES), jnp.float32),
@@ -329,10 +328,13 @@
             pltpu.VMEM((blocks, 2, PDIM, LANES), jnp.float32),
             pltpu.VMEM((2, PDIM, terms), jnp.float32),
             pltpu.VMEM((1, ions), jnp.float32),
-        ] + [pltpu.HBM(*v) for v in kept],
+            pltpu.VMEM((blocks, 2 * PDIM, BLOCK), jnp.float32),
+            pltpu.VMEM((blocks, 2 * HALF, BLOCK), jnp.float32),
+            pltpu.VMEM((blocks, count, BLOCK), jnp.float32),
+        ],
         in_specs=[scalar, scalar, vector, vector],
-        out_specs=[vector] * 5 + [apart] * 3,
-        scratch_shapes=held,
+        out_specs=[vector] * 8,
+        scratch_shapes=work,
         compiler_params=params,
         name="moments",
     )(counts, box, positions, charges)
@@ -342,20 +344,19 @@
     carry, _ = exchange(slab_totals, depth, slab_count, "slab")
     carry = carry + jnp.exp(depth) * inside
 
-    carry, *small = [pltpu.with_memory_space_constraint(v, pltpu.VMEM) for v in (carry, *small)]
-    high, low, phase = [pltpu.with_memory_space_constraint(v, pltpu.HBM) for v in (high, low, phase)]
+    carry, *kept = [pltpu.with_memory_space_constraint(v, pltpu.VMEM) for v in (carry, *kept)]
     return pl.pallas_call(
         functools.partial(forces_kernel, count),
         out_shape=jax.ShapeDtypeStruct((3, ions), jnp.float32),
-        in_specs=[scalar] + [vector] * 4 + [apart] * 3,
+        in_specs=[scalar] + [vector] * 7,
         out_specs=vector,
         scratch_shapes=[
             pltpu.VMEM((6 * PDIM, terms), jnp.bfloat16),
             pltpu.VMEM((6 * PDIM, terms), jnp.bfloat16),
-        ] + held,
+        ] + work,
         compiler_params=params,
         name="forces",
-    )(box, carry, *small, high, low, phase)
+    )(box, carry, *kept)
 
 
 def solution(mesh):

time: 34.6 us -> 31.3 us (0.905)
  Pallas kernels: 12.9 us -> 10.2 us
  waiting for transfers between devices: 10.2 us -> 9.8 us
    pallas_call x1, Pallas kernels: 5.18 us -> 3.59 us  [shards(): pl.pallas_call(functools.partial(moments_kernel, count, height), out_shap...]
    pallas_call x1, Pallas kernels: 7.68 us -> 6.61 us  [shards(): pl.pallas_call(functools.partial(forces_kernel, count), out_shape=jax.Sha...]
    ppermute x5, waiting for transfers between devices: 10.2 us -> 9.8 us  [the longest x4 7.91 us: exchange(): other = lax.ppermute(totals, axis, pairs)]
where the time goes in v3:
time: 31.3 us; the launch traced here: 31.1 us
  starting transfers between devices  10.7 us (34%)
  Pallas kernels  10.2 us (33%)
  waiting for transfers between devices  9.8 us (31%)
  other arithmetic  0.35 us (1%)
    ppermute x4, waiting for transfers between devices, exchange(): other = lax.ppermute(totals, axis, pairs)  7.91 us
    ppermute x4, starting transfers between devices, exchange(): other = lax.ppermute(totals, axis, pairs)  7.32 us
    pallas_call x1, Pallas kernels, shards(): pl.pallas_call(functools.partial(forces_kernel, count), out_shape=jax.Sha...  6.61 us
    pallas_call x1, Pallas kernels, shards(): pl.pallas_call(functools.partial(moments_kernel, count, height), out_shap...  3.59 us
    ppermute x1, starting transfers between devices, exchange(): lax.ppermute(jnp.where(upper == 0, totals[:, 0], totals[:, 1]), axis, pairs)  3.37 us
    ppermute x1, waiting for transfers between devices, exchange(): lax.ppermute(jnp.where(upper == 0, totals[:, 0], totals[:, 1]), axis, pairs)  1.89 us
  transfers between devices with their start and end apart: 5, of which 5 were waited for; matrix products, arithmetic and copies ran while one was open for 0% of the time, Pallas kernels for 0%

profile of v3, /device:TPU:0, one launch (start us, length us, event | category | flops | bytes accessed | tf_op | source)
XLA Modules:
  0.0 31.1 jit_solution(11148771308627262232)
XLA Ops:
  0.0 3.6 %moments.1 = (f32[2,2,32,128]{3,2,1,0:T(8,128)S(1)}, f32[2,32,128]{2,1,0:T(8,128)S(1)}, f32[4,2,64,128]{3,2,1,0:T(8,128)S(1)}, f32[2,64,768]{2,1,0:T(8,128)S(1)}...) custom-call(s32[8]{0:T(128)} %counts_ref.1, ...), custom_call_target="tpu_custom_call" | custom-call | tf_op jit(solution)/shard_map/moments/pallas_call | solution.py:323
  3.6 0.5 %collective-permute-start = (f32[2,2,32,128]{3,2,1,0:T(8,128)S(1)}, f32[2,2,32,128]{3,2,1,0:T(8,128)S(1)}, u32[]{:S(2)}, u32[]{:S(2)}) collective-permute-start(f32[2,2,32,128]{3,2,1,0:T(8,128)S(1)} %get-tuple-element.13), channel_id=1, source_target_pairs={{0,1},{1,0},{2,3},{3,2},{4,5},{5,4},{6,7},{7,6},{8,9},{9,8},{10,11... | collective-permute-start | bytes 196616 | tf_op jit(solution)/shard_map/ppermute | solution.py:295
  4.2 0.8 %collective-permute-done = f32[2,2,32,128]{3,2,1,0:T(8,128)S(1)} collective-permute-done((f32[2,2,32,128]{3,2,1,0:T(8,128)S(1)}, f32[2,2,32,128]{3,2,1,0:T(8,128)S(1)}, u32[]{:S(2)}, u32[]{:S(2)}) %collective-permute-start) | collective-permute-done | bytes 65568 | tf_op jit(solution)/shard_map/ppermute | solution.py:295
  5.0 2.9 %collective-permute-start.1 = (f32[2,2,32,128]{3,2,1,0:T(8,128)S(1)}, f32[2,2,32,128]{3,2,1,0:T(8,128)S(1)}, u32[]{:S(2)}, u32[]{:S(2)}) collective-permute-start(f32[2,2,32,128]{3,2,1,0:T(8,128)S(1)} %add.57), channel_id=1, source_target_pairs={{0,2},{1,3},{2,0},{3,1},{4,6},{5,7},{6,4},{7,5},{8,10},{9,11},{10,... | collective-permute-start | bytes 196616 | tf_op jit(solution)/shard_map/ppermute | solution.py:295
  7.9 2.4 %collective-permute-done.1 = f32[2,2,32,128]{3,2,1,0:T(8,128)S(1)} collective-permute-done((f32[2,2,32,128]{3,2,1,0:T(8,128)S(1)}, f32[2,2,32,128]{3,2,1,0:T(8,128)S(1)}, u32[]{:S(2)}, u32[]{:S(2)}) %collective-permute-start.1) | collective-permute-done | bytes 65568 | tf_op jit(solution)/shard_map/ppermute | solution.py:295
  10.3 2.0 %collective-permute-start.2 = (f32[2,2,32,128]{3,2,1,0:T(8,128)S(1)}, f32[2,2,32,128]{3,2,1,0:T(8,128)S(1)}, u32[]{:S(2)}, u32[]{:S(2)}) collective-permute-start(f32[2,2,32,128]{3,2,1,0:T(8,128)S(1)} %add.58), channel_id=1, source_target_pairs={{0,4},{4,0},{8,12},{12,8},{16,20},{20,16},{24,28},{28,24},{1,5},{5... | collective-permute-start | bytes 196616 | tf_op jit(solution)/shard_map/ppermute | solution.py:295
  12.3 2.4 %collective-permute-done.2 = f32[2,2,32,128]{3,2,1,0:T(8,128)S(1)} collective-permute-done((f32[2,2,32,128]{3,2,1,0:T(8,128)S(1)}, f32[2,2,32,128]{3,2,1,0:T(8,128)S(1)}, u32[]{:S(2)}, u32[]{:S(2)}) %collective-permute-start.2) | collective-permute-done | bytes 65568 | tf_op jit(solution)/shard_map/ppermute | solution.py:295
  14.7 0.1 add_select_fusion.1
  14.8 1.9 %collective-permute-start.3 = (f32[2,2,32,128]{3,2,1,0:T(8,128)S(1)}, f32[2,2,32,128]{3,2,1,0:T(8,128)S(1)}, u32[]{:S(2)}, u32[]{:S(2)}) collective-permute-start(f32[2,2,32,128]{3,2,1,0:T(8,128)S(1)} %add_select_fusion.1), channel_id=1, source_target_pairs={{0,8},{4,12},{8,0},{12,4},{16,24},{20,28},{24,16},{28,20},{1,9},{5... | collective-permute-start | bytes 196616 | tf_op jit(solution)/shard_map/ppermute | solution.py:295
  16.7 2.3 %collective-permute-done.3 = f32[2,2,32,128]{3,2,1,0:T(8,128)S(1)} collective-permute-done((f32[2,2,32,128]{3,2,1,0:T(8,128)S(1)}, f32[2,2,32,128]{3,2,1,0:T(8,128)S(1)}, u32[]{:S(2)}, u32[]{:S(2)}) %collective-permute-start.3) | collective-permute-done | bytes 65568 | tf_op jit(solution)/shard_map/ppermute | solution.py:295
  19.0 0.1 add_select_fusion
  19.1 3.4 %collective-permute-start.4 = (f32[2,32,128]{2,1,0:T(8,128)S(1)}, f32[2,32,128]{2,1,0:T(8,128)S(1)}, u32[]{:S(2)}, u32[]{:S(2)}) collective-permute-start(f32[2,32,128]{2,1,0:T(8,128)S(1)} %fusion), channel_id=1, source_target_pairs={{0,16},{4,20},{8,24},{12,28},{16,0},{20,4},{24,8},{28,12},{1,17},{... | collective-permute-start | bytes 98312 | tf_op jit(solution)/shard_map/ppermute | solution.py:293
  22.5 1.9 %collective-permute-done.4 = f32[2,32,128]{2,1,0:T(8,128)S(1)} collective-permute-done((f32[2,32,128]{2,1,0:T(8,128)S(1)}, f32[2,32,128]{2,1,0:T(8,128)S(1)}, u32[]{:S(2)}, u32[]{:S(2)}) %collective-permute-start.4) | collective-permute-done | bytes 32800 | tf_op jit(solution)/shard_map/ppermute | solution.py:293
  24.4 0.1 multiply_add_fusion.carry_ref
  24.5 6.6 %forces.1 = f32[3,2048]{1,0:T(4,128)} custom-call(f32[2]{0:T(128)} %box_ref.3, f32[2,2,32,128]{3,2,1,0:T(8,128)S(1)} %multiply_add_fusion.carry_ref, f32[4,2,64,128]{3,2,1,0:T(8,128)S(1)} %get-tuple-element.15.before_ref, f32[2,64,768]{2,1,0:T(8,128)S(1)} %get-tuple-element.16.table_ref, f32[1,2048]{1,0:T(1,128)S(1)} %get-tuple-element.17.weight_ref, ...), custom_call_target="tpu_custom_call" | custom-call | tf_op jit(solution)/shard_map/forces/pallas_call | solution.py:348
  (9 shorter events, 0.1 us)
Async XLA Ops:
  3.6 1.4 %collective-permute-start = (f32[2,2,32,128]{3,2,1,0:T(8,128)S(1)}, f32[2,2,32,128]{3,2,1,0:T(8,128)S(1)}, u32[]{:S(2)}, u32[]{:S(2)}) collective-permute-start(f32[2,2,32,128]{3,2,1,0:T(8,128)S(1)} %get-tuple-element.13), channel_id=1, source_target_pairs={{0,1},{1,0},{2,3},{3,2},{4,5},{5,4},{6,7},{7,6},{8,9},{9,8},{10,11... | collective-permute-start | bytes 196616 | tf_op jit(solution)/shard_map/ppermute | solution.py:295
  5.0 5.3 %collective-permute-start.1 = (f32[2,2,32,128]{3,2,1,0:T(8,128)S(1)}, f32[2,2,32,128]{3,2,1,0:T(8,128)S(1)}, u32[]{:S(2)}, u32[]{:S(2)}) collective-permute-start(f32[2,2,32,128]{3,2,1,0:T(8,128)S(1)} %add.57), channel_id=1, source_target_pairs={{0,2},{1,3},{2,0},{3,1},{4,6},{5,7},{6,4},{7,5},{8,10},{9,11},{10,... | collective-permute-start | bytes 196616 | tf_op jit(solution)/shard_map/ppermute | solution.py:295
  10.3 4.3 %collective-permute-start.2 = (f32[2,2,32,128]{3,2,1,0:T(8,128)S(1)}, f32[2,2,32,128]{3,2,1,0:T(8,128)S(1)}, u32[]{:S(2)}, u32[]{:S(2)}) collective-permute-start(f32[2,2,32,128]{3,2,1,0:T(8,128)S(1)} %add.58), channel_id=1, source_target_pairs={{0,4},{4,0},{8,12},{12,8},{16,20},{20,16},{24,28},{28,24},{1,5},{5... | collective-permute-start | bytes 196616 | tf_op jit(solution)/shard_map/ppermute | solution.py:295
  14.8 4.3 %collective-permute-start.3 = (f32[2,2,32,128]{3,2,1,0:T(8,128)S(1)}, f32[2,2,32,128]{3,2,1,0:T(8,128)S(1)}, u32[]{:S(2)}, u32[]{:S(2)}) collective-permute-start(f32[2,2,32,128]{3,2,1,0:T(8,128)S(1)} %add_select_fusion.1), channel_id=1, source_target_pairs={{0,8},{4,12},{8,0},{12,4},{16,24},{20,28},{24,16},{28,20},{1,9},{5... | collective-permute-start | bytes 196616 | tf_op jit(solution)/shard_map/ppermute | solution.py:295
  19.1 5.3 %collective-permute-start.4 = (f32[2,32,128]{2,1,0:T(8,128)S(1)}, f32[2,32,128]{2,1,0:T(8,128)S(1)}, u32[]{:S(2)}, u32[]{:S(2)}) collective-permute-start(f32[2,32,128]{2,1,0:T(8,128)S(1)} %fusion), channel_id=1, source_target_pairs={{0,16},{4,20},{8,24},{12,28},{16,0},{20,4},{24,8},{28,12},{1,17},{... | collective-permute-start | bytes 98312 | tf_op jit(solution)/shard_map/ppermute | solution.py:293

commit v4 on v3

--- a/solution.py
+++ b/solution.py
@@ -92,18 +92,19 @@
     p, q_plus, q_minus = tile_orders()
     even = even_group(p.shape)
     a = (0.5 * height) * wave(p, jnp.where(even, q_plus, q_minus), box_x, box_y)[2]
-    ratio = jnp.zeros_like(a)
-    ratios = {}
-    for n in range(count + 6, 0, -1):
-        ratio = a / (2.0 * n + a * ratio)
-        ratios[n] = ratio
-    products = [jnp.ones_like(a)]
-    total = jnp.ones_like(a)
-    for n in range(1, count + 7):
-        products.append(products[-1] * ratios[n])
-        total = total + 2.0 * products[n]
+    square = 0.25 * a * a
+    last = count + 8
+    scaled = {last + 1: jnp.ones_like(a), last: jnp.ones_like(a)}
+    for n in range(last, 0, -1):
+        scaled[n - 1] = scaled[n] + square * (scaled[n + 1] * (1.0 / (n * (n + 1))))
+    power, total = jnp.ones_like(a), scaled[0]
+    parts = [scaled[0]]
+    for n in range(1, last + 1):
+        power = power * (a * (0.5 / n))
+        parts.append(2.0 * (power * scaled[n]))
+        total = total + parts[n]
     first = 1.0 / total
-    terms = [first] + [(2.0 * first) * products[n] for n in range(1, count)]
+    terms = [first * part for part in parts[:count]]
     plus, minus = [], []
     for m in range(count // 2):
         low, high = terms[2 * m], terms[2 * m + 1]
@@ -125,7 +126,7 @@
 
 def moments_kernel(
     count, height, counts_ref, box_ref, positions_ref, charges_ref,
-    totals_ref, decay_ref, before_ref, table_ref, weight_ref, phase_ref, sides_ref, powers_ref,
+    totals_ref, decay_ref, unit_ref, before_ref, table_ref, weight_ref, phase_ref, sides_ref, powers_ref,
     high_ref, low_ref,
 ):
     ions = positions_ref.shape[1]
@@ -209,7 +210,10 @@
     p, q_plus, q_minus = tile_orders()
     even = even_group(tile)
     for kind, order_q in enumerate((q_plus, q_minus)):
-        wave_norm = wave(p, order_q, box_x, box_y)[2]
+        wave_x, wave_y, wave_norm = wave(p, order_q, box_x, box_y)
+        inverse = 1.0 / wave_norm
+        unit_ref[kind, 0] = wave_x * inverse
+        unit_ref[kind, 1] = wave_y * inverse
         boost = jnp.exp(wave_norm * height)
         prefix = [jnp.zeros(tile, jnp.float32)]
         for b in range(blocks):
@@ -226,26 +230,21 @@
 
 
 def forces_kernel(
-    count, box_ref, carry_ref, before_ref, table_ref, weight_ref, phase_ref, sides_ref, powers_ref,
-    forces_ref, coarse_ref, fine_ref, high_ref, low_ref,
+    count, carry_ref, unit_ref, before_ref, table_ref, weight_ref, phase_ref, sides_ref, powers_ref,
+    forces_ref, coarse_ref, high_ref, low_ref,
 ):
     blocks = before_ref.shape[0]
     pairs = count // 2
-    box_x = jnp.full((1, 1), box_ref[0], jnp.float32)
-    box_y = jnp.full((1, 1), box_ref[1], jnp.float32)
     tile = (PDIM, LANES)
     sign = half_sign(tile)
     group_sign = jnp.where(even_group(tile), 1.0, -1.0)
-    p, q_plus, q_minus = tile_orders()
-    base, units = [], []
+    base = []
     small = even_group((PDIM // 2, LANES))
-    for kind, order_q in enumerate((q_plus, q_minus)):
+    for kind in range(2):
         up, down = carry_ref[kind, 0], carry_ref[kind, 1]
         top = jnp.where(small, up, roll(down, HALF))
         bottom = jnp.where(small, roll(up, -HALF), down)
         base.append(jnp.concatenate([top, bottom], axis=0))
-        wave_x, wave_y, wave_norm = wave(p, order_q, box_x, box_y)
-        units.append((wave_x / wave_norm, wave_y / wave_norm))
 
     for b in range(blocks):
         span = slice(b * BLOCK, (b + 1) * BLOCK)
@@ -254,7 +253,7 @@
             held = base[kind] + before_ref[b, kind]
             mixed = held + group_sign * swap_groups(held)
             turned = sign * roll(mixed, LANES // 2)
-            sides.append((units[kind][0] * turned, units[kind][1] * turned, -swap_groups(mixed)))
+            sides.append((unit_ref[kind, 0] * turned, unit_ref[kind, 1] * turned, -swap_groups(mixed)))
         for o in range(3):
             plus, minus = sides[0][o], sides[1][o]
             plus_rows = (plus, -sign * roll(plus, LANES // 2))
@@ -266,42 +265,59 @@
                 for part in range(2):
                     at = (2 * o + part) * PDIM
                     high, low = split(table_plus * plus_rows[part] + table_minus * minus_rows[part])
-                    coarse_ref[at : at + PDIM, lanes] = high
-                    fine_ref[at : at + PDIM, lanes] = low
+                    coarse_ref[b, at : at + PDIM, lanes] = high
+                    coarse_ref[b, 6 * PDIM + at : 6 * PDIM + at + PDIM, lanes] = low
         spread(count, powers_ref[b], sides_ref[b], high_ref.at[b], low_ref.at[b])
-        field = jnp.dot(coarse_ref[...], high_ref[b], preferred_element_type=jnp.float32)
-        field += jnp.dot(fine_ref[...], high_ref[b], preferred_element_type=jnp.float32)
-        field += jnp.dot(coarse_ref[...], low_ref[b], preferred_element_type=jnp.float32)
+        field = jnp.dot(coarse_ref[b], high_ref[b], preferred_element_type=jnp.float32)
+        field = field[: 6 * PDIM] + field[6 * PDIM :]
+        field += jnp.dot(coarse_ref[b, : 6 * PDIM], low_ref[b], preferred_element_type=jnp.float32)
         phase = phase_ref[b]
         for o in range(3):
             part = field[o * 2 * PDIM : (o + 1) * 2 * PDIM]
             forces_ref[o : o + 1, span] = jnp.sum(phase * part, axis=0, keepdims=True) * weight_ref[0:1, span]
 
 
-def exchange(totals, decay, parts, axis):
-    rank = lax.axis_index(axis)
+def doublings(first, size):
+    return [first << i for i in range(32) if first << i < size]
+
+
+def carries(totals, decay, slabs, modes):
+    slab, mode = lax.axis_index("slab"), lax.axis_index("mode")
     part = jnp.arange(2, dtype=jnp.int32)[None, :, None, None]
-    outside = jnp.zeros_like(totals)
-    stride = 1
-    while stride < parts:
-        upper = (rank // stride) % 2
-        ahead = part != upper
-        below = rank % stride
-        steps = jnp.where(part == 0, below, stride - 1 - below)
-        pairs = [(i, i ^ stride) for i in range(parts)]
-        if decay is not None and 2 * stride == parts:
-            other = lax.ppermute(jnp.where(upper == 0, totals[:, 0], totals[:, 1]), axis, pairs)[:, None]
-        else:
-            other = lax.ppermute(totals, axis, pairs)
-        if decay is None:
-            outside = outside + jnp.where(ahead, other, 0.0)
-            totals = totals + other
-        else:
-            outside = outside + jnp.where(ahead, other * jnp.exp(-decay * steps.astype(jnp.float32)), 0.0)
-            fade = jnp.exp(-decay * float(stride))
-            totals = jnp.where(ahead, totals + fade * other, other + fade * totals)
-        stride *= 2
-    return outside, totals
+    depth = decay[:, None]
+
+    def swap(value, mask):
+        return lax.ppermute(value, ("slab", "mode"), [(i, i ^ mask) for i in range(slabs * modes)])
+
+    def ahead(rank, stride):
+        return part != (rank // stride) % 2
+
+    other = swap(totals, 1)
+    inside = jnp.where(ahead(mode, 1), other, 0.0)
+    totals = totals + other
+    strides = doublings(2, modes)
+    for stride in strides[:-1]:
+        other = swap(totals, stride ^ 1)
+        inside = inside + jnp.where(ahead(mode, stride), other, 0.0)
+        totals = totals + other
+    across, along, both = [swap(totals, mask) for mask in (strides[-1] ^ 1, modes ^ 1, modes ^ strides[-1] ^ 1)]
+    inside = inside + jnp.where(ahead(mode, strides[-1]), across, 0.0)
+    totals = totals + across
+    other = along + both
+    outside = jnp.exp(depth) * inside
+    for stride in doublings(1, slabs):
+        first = ahead(slab, stride)
+        if stride > 1 and 2 * stride < slabs:
+            other = swap(totals, (stride * modes) ^ 1)
+        elif stride > 1:
+            sent = jnp.where((slab // stride) % 2 == 0, totals[:, 0], totals[:, 1])
+            other = swap(sent, (stride * modes) ^ 1)[:, None]
+        below = slab % stride
+        steps = jnp.where(part == 0, below, stride - 1 - below).astype(jnp.float32)
+        outside = outside + jnp.where(first, other * jnp.exp(-depth * steps), 0.0)
+        fade = jnp.exp(-depth * float(stride))
+        totals = jnp.where(first, totals + fade * other, other + fade * totals)
+    return outside
 
 
 def shards(positions, charges, counts, box):
@@ -315,9 +331,9 @@
     half = PDIM // 2
     scalar = pl.BlockSpec(memory_space=pltpu.SMEM)
     vector = pl.BlockSpec(memory_space=pltpu.VMEM)
-    params = pltpu.CompilerParams(vmem_limit_bytes=24 * 1024 * 1024)
+    params = pltpu.CompilerParams(vmem_limit_bytes=40 * 1024 * 1024)
     work = [pltpu.VMEM((blocks, terms, BLOCK), jnp.bfloat16)] * 2
-    counts, box, positions, charges = [
+    inputs = [
         pltpu.with_memory_space_constraint(v, pltpu.HBM) for v in (counts, box, positions, charges[None, :])
     ]
     totals, decay, *kept = pl.pallas_call(
@@ -325,6 +341,7 @@
         out_shape=[
             pltpu.VMEM((2, 2, half, LANES), jnp.float32),
             pltpu.VMEM((2, half, LANES), jnp.float32),
+            pltpu.VMEM((2, 2, PDIM, LANES), jnp.float32),
             pltpu.VMEM((blocks, 2, PDIM, LANES), jnp.float32),
             pltpu.VMEM((2, PDIM, terms), jnp.float32),
             pltpu.VMEM((1, ions), jnp.float32),
@@ -333,30 +350,26 @@
             pltpu.VMEM((blocks, count, BLOCK), jnp.float32),
         ],
         in_specs=[scalar, scalar, vector, vector],
-        out_specs=[vector] * 8,
+        out_specs=[vector] * 9,
         scratch_shapes=work,
         compiler_params=params,
         name="moments",
-    )(counts, box, positions, charges)
-
-    inside, slab_totals = exchange(totals, None, mode_parts, "mode")
-    depth = decay[:, None]
-    carry, _ = exchange(slab_totals, depth, slab_count, "slab")
-    carry = carry + jnp.exp(depth) * inside
+    )(*inputs)
+
+    carry = carries(totals, decay, slab_count, mode_parts)
 
     carry, *kept = [pltpu.with_memory_space_constraint(v, pltpu.VMEM) for v in (carry, *kept)]
     return pl.pallas_call(
         functools.partial(forces_kernel, count),
         out_shape=jax.ShapeDtypeStruct((3, ions), jnp.float32),
-        in_specs=[scalar] + [vector] * 7,
+        in_specs=[vector] * 8,
         out_specs=vector,
         scratch_shapes=[
-            pltpu.VMEM((6 * PDIM, terms), jnp.bfloat16),
-            pltpu.VMEM((6 * PDIM, terms), jnp.bfloat16),
+            pltpu.VMEM((blocks, 12 * PDIM, terms), jnp.bfloat16),
         ] + work,
         compiler_params=params,
         name="forces",
-    )(box, carry, *kept)
+    )(carry, *kept)
 
 
 def solution(mesh):

time: 31.3 us -> 28.4 us (0.907)
  starting transfers between devices: 10.7 us -> 8.45 us
  Pallas kernels: 10.2 us -> 9.02 us
  waiting for transfers between devices: 9.8 us -> 10.3 us
    ppermute x5 -> x6, starting transfers between devices: 10.7 us -> 8.45 us  [swap(): lax.ppermute(value, ('slab', 'mode'), [(i, i ^ mask) for i in range(slabs...]
    pallas_call x1, Pallas kernels: 6.61 us -> 5.46 us  [shards(): pl.pallas_call(functools.partial(forces_kernel, count), out_shape=jax.Sha...]
    ppermute x5 -> x6, waiting for transfers between devices: 9.8 us -> 10.3 us  [swap(): lax.ppermute(value, ('slab', 'mode'), [(i, i ^ mask) for i in range(slabs...]
  transfers between devices with their start and end apart: 5 -> 6, of which waited for: 5 -> 6; matrix products, arithmetic and copies ran while one was open for 0% -> 0% of each run, Pallas kernels for 0% -> 0%
where the time goes in v4:
time: 28.4 us; the launch traced here: 28.2 us
  waiting for transfers between devices  10.3 us (36%)
  Pallas kernels  9.02 us (32%)
  starting transfers between devices  8.45 us (30%)
  other arithmetic  0.33 us (1%)
    ppermute x6, waiting for transfers between devices, swap(): lax.ppermute(value, ('slab', 'mode'), [(i, i ^ mask) for i in range(slabs...  10.3 us
    ppermute x6, starting transfers between devices, swap(): lax.ppermute(value, ('slab', 'mode'), [(i, i ^ mask) for i in range(slabs...  8.45 us
    pallas_call x1, Pallas kernels, shards(): pl.pallas_call(functools.partial(forces_kernel, count), out_shape=jax.Sha...  5.46 us
    pallas_call x1, Pallas kernels, shards(): pl.pallas_call(functools.partial(moments_kernel, count, height), out_shap...  3.56 us
  transfers between devices with their start and end apart: 6, of which 6 were waited for; matrix products, arithmetic and copies ran while one was open for 0% of the time, Pallas kernels for 0%

profile of v4, /device:TPU:0, one launch (start us, length us, event | category | flops | bytes accessed | tf_op | source)
XLA Modules:
  0.0 28.2 jit_solution(2112123051695501821)
XLA Ops:
  0.0 3.6 %moments.1 = (f32[2,2,32,128]{3,2,1,0:T(8,128)S(1)}, f32[2,32,128]{2,1,0:T(8,128)S(1)}, f32[2,2,64,128]{3,2,1,0:T(8,128)S(1)}, f32[4,2,64,128]{3,2,1,0:T(8,128)S...) custom-call(s32[8]{0:T(128)} %counts_ref.1, ...), custom_call_target="tpu_custom_call" | custom-call | tf_op jit(solution)/shard_map/moments/pallas_call | solution.py:339
  3.6 0.5 %collective-permute-start = (f32[2,2,32,128]{3,2,1,0:T(8,128)S(1)}, f32[2,2,32,128]{3,2,1,0:T(8,128)S(1)}, u32[]{:S(2)}, u32[]{:S(2)}) collective-permute-start(f32[2,2,32,128]{3,2,1,0:T(8,128)S(1)} %get-tuple-element.15), channel_id=1, source_target_pairs={{0,1},{1,0},{2,3},{3,2},{4,5},{5,4},{6,7},{7,6},{8,9},{9,8},{10,11... | collective-permute-start | bytes 196616 | tf_op jit(solution)/shard_map/ppermute | solution.py:290
  4.2 0.8 %collective-permute-done = f32[2,2,32,128]{3,2,1,0:T(8,128)S(1)} collective-permute-done((f32[2,2,32,128]{3,2,1,0:T(8,128)S(1)}, f32[2,2,32,128]{3,2,1,0:T(8,128)S(1)}, u32[]{:S(2)}, u32[]{:S(2)}) %collective-permute-start) | collective-permute-done | bytes 65568 | tf_op jit(solution)/shard_map/ppermute | solution.py:290
  5.0 2.7 %collective-permute-start.1 = (f32[2,2,32,128]{3,2,1,0:T(8,128)S(1)}, f32[2,2,32,128]{3,2,1,0:T(8,128)S(1)}, u32[]{:S(2)}, u32[]{:S(2)}) collective-permute-start(f32[2,2,32,128]{3,2,1,0:T(8,128)S(1)} %add.62), channel_id=1, source_target_pairs={{0,3},{1,2},{2,1},{3,0},{4,7},{5,6},{6,5},{7,4},{8,11},{9,10},{10,... | collective-permute-start | bytes 196616 | tf_op jit(solution)/shard_map/ppermute | solution.py:290
  7.7 1.5 %collective-permute-start.2 = (f32[2,2,32,128]{3,2,1,0:T(8,128)S(1)}, f32[2,2,32,128]{3,2,1,0:T(8,128)S(1)}, u32[]{:S(2)}, u32[]{:S(2)}) collective-permute-start(f32[2,2,32,128]{3,2,1,0:T(8,128)S(1)} %add.62), channel_id=1, source_target_pairs={{0,5},{1,4},{2,7},{3,6},{4,1},{5,0},{6,3},{7,2},{8,13},{9,12},{10,... | collective-permute-start | bytes 196616 | tf_op jit(solution)/shard_map/ppermute | solution.py:290
  9.1 0.0 collective-permute-start.3
  9.2 0.7 %collective-permute-done.1 = f32[2,2,32,128]{3,2,1,0:T(8,128)S(1)} collective-permute-done((f32[2,2,32,128]{3,2,1,0:T(8,128)S(1)}, f32[2,2,32,128]{3,2,1,0:T(8,128)S(1)}, u32[]{:S(2)}, u32[]{:S(2)}) %collective-permute-start.1) | collective-permute-done | bytes 65568 | tf_op jit(solution)/shard_map/ppermute | solution.py:290
  9.9 1.7 %collective-permute-done.2 = f32[2,2,32,128]{3,2,1,0:T(8,128)S(1)} collective-permute-done((f32[2,2,32,128]{3,2,1,0:T(8,128)S(1)}, f32[2,2,32,128]{3,2,1,0:T(8,128)S(1)}, u32[]{:S(2)}, u32[]{:S(2)}) %collective-permute-start.2) | collective-permute-done | bytes 65568 | tf_op jit(solution)/shard_map/ppermute | solution.py:290
  11.6 2.5 %collective-permute-done.3 = f32[2,2,32,128]{3,2,1,0:T(8,128)S(1)} collective-permute-done((f32[2,2,32,128]{3,2,1,0:T(8,128)S(1)}, f32[2,2,32,128]{3,2,1,0:T(8,128)S(1)}, u32[]{:S(2)}, u32[]{:S(2)}) %collective-permute-start.3) | collective-permute-done | bytes 65568 | tf_op jit(solution)/shard_map/ppermute | solution.py:290
  14.1 0.1 add_select_fusion.1
  14.2 1.4 %collective-permute-start.4 = (f32[2,2,32,128]{3,2,1,0:T(8,128)S(1)}, f32[2,2,32,128]{3,2,1,0:T(8,128)S(1)}, u32[]{:S(2)}, u32[]{:S(2)}) collective-permute-start(f32[2,2,32,128]{3,2,1,0:T(8,128)S(1)} %add_select_fusion.1), channel_id=1, source_target_pairs={{0,9},{1,8},{2,11},{3,10},{4,13},{5,12},{6,15},{7,14},{8,1},{9,0},... | collective-permute-start | bytes 196616 | tf_op jit(solution)/shard_map/ppermute | solution.py:290
  15.5 2.7 %collective-permute-done.4 = f32[2,2,32,128]{3,2,1,0:T(8,128)S(1)} collective-permute-done((f32[2,2,32,128]{3,2,1,0:T(8,128)S(1)}, f32[2,2,32,128]{3,2,1,0:T(8,128)S(1)}, u32[]{:S(2)}, u32[]{:S(2)}) %collective-permute-start.4) | collective-permute-done | bytes 65568 | tf_op jit(solution)/shard_map/ppermute | solution.py:290
  18.2 0.1 add_select_fusion
  18.3 2.4 %collective-permute-start.5 = (f32[2,32,128]{2,1,0:T(8,128)S(1)}, f32[2,32,128]{2,1,0:T(8,128)S(1)}, u32[]{:S(2)}, u32[]{:S(2)}) collective-permute-start(f32[2,32,128]{2,1,0:T(8,128)S(1)} %fusion), channel_id=1, source_target_pairs={{0,17},{1,16},{2,19},{3,18},{4,21},{5,20},{6,23},{7,22},{8,25},{9,... | collective-permute-start | bytes 98312 | tf_op jit(solution)/shard_map/ppermute | solution.py:290
  20.8 1.9 %collective-permute-done.5 = f32[2,32,128]{2,1,0:T(8,128)S(1)} collective-permute-done((f32[2,32,128]{2,1,0:T(8,128)S(1)}, f32[2,32,128]{2,1,0:T(8,128)S(1)}, u32[]{:S(2)}, u32[]{:S(2)}) %collective-permute-start.5) | collective-permute-done | bytes 32800 | tf_op jit(solution)/shard_map/ppermute | solution.py:290
  22.6 0.1 select_add_fusion.carry_ref
  22.8 5.5 %forces.1 = f32[3,2048]{1,0:T(4,128)} custom-call(f32[2,2,32,128]{3,2,1,0:T(8,128)S(1)} %select_add_fusion.carry_ref, f32[2,2,64,128]{3,2,1,0:T(8,128)S(1)} %get-tuple-element.16.unit_ref, f32[4,2,64,128]{3,2,1,0:T(8,128)S(1)} %get-tuple-element.17.before_ref, f32[2,64,768]{2,1,0:T(8,128)S(1)} %get-tuple-element.18.table_ref, ...), custom_call_target="tpu_custom_call" | custom-call | tf_op jit(solution)/shard_map/forces/pallas_call | solution.py:362
  (8 shorter events, 0.1 us)
Async XLA Ops:
  3.6 1.4 %collective-permute-start = (f32[2,2,32,128]{3,2,1,0:T(8,128)S(1)}, f32[2,2,32,128]{3,2,1,0:T(8,128)S(1)}, u32[]{:S(2)}, u32[]{:S(2)}) collective-permute-start(f32[2,2,32,128]{3,2,1,0:T(8,128)S(1)} %get-tuple-element.15), channel_id=1, source_target_pairs={{0,1},{1,0},{2,3},{3,2},{4,5},{5,4},{6,7},{7,6},{8,9},{9,8},{10,11... | collective-permute-start | bytes 196616 | tf_op jit(solution)/shard_map/ppermute | solution.py:290
  5.0 4.9 %collective-permute-start.1 = (f32[2,2,32,128]{3,2,1,0:T(8,128)S(1)}, f32[2,2,32,128]{3,2,1,0:T(8,128)S(1)}, u32[]{:S(2)}, u32[]{:S(2)}) collective-permute-start(f32[2,2,32,128]{3,2,1,0:T(8,128)S(1)} %add.62), channel_id=1, source_target_pairs={{0,3},{1,2},{2,1},{3,0},{4,7},{5,6},{6,5},{7,4},{8,11},{9,10},{10,... | collective-permute-start | bytes 196616 | tf_op jit(solution)/shard_map/ppermute | solution.py:290
  7.7 3.9 %collective-permute-start.2 = (f32[2,2,32,128]{3,2,1,0:T(8,128)S(1)}, f32[2,2,32,128]{3,2,1,0:T(8,128)S(1)}, u32[]{:S(2)}, u32[]{:S(2)}) collective-permute-start(f32[2,2,32,128]{3,2,1,0:T(8,128)S(1)} %add.62), channel_id=1, source_target_pairs={{0,5},{1,4},{2,7},{3,6},{4,1},{5,0},{6,3},{7,2},{8,13},{9,12},{10,... | collective-permute-start | bytes 196616 | tf_op jit(solution)/shard_map/ppermute | solution.py:290
  9.1 5.0 %collective-permute-start.3 = (f32[2,2,32,128]{3,2,1,0:T(8,128)S(1)}, f32[2,2,32,128]{3,2,1,0:T(8,128)S(1)}, u32[]{:S(2)}, u32[]{:S(2)}) collective-permute-start(f32[2,2,32,128]{3,2,1,0:T(8,128)S(1)} %add.62), channel_id=1, source_target_pairs={{0,7},{1,6},{2,5},{3,4},{4,3},{5,2},{6,1},{7,0},{8,15},{9,14},{10,... | collective-permute-start | bytes 196616 | tf_op jit(solution)/shard_map/ppermute | solution.py:290
  14.2 4.1 %collective-permute-start.4 = (f32[2,2,32,128]{3,2,1,0:T(8,128)S(1)}, f32[2,2,32,128]{3,2,1,0:T(8,128)S(1)}, u32[]{:S(2)}, u32[]{:S(2)}) collective-permute-start(f32[2,2,32,128]{3,2,1,0:T(8,128)S(1)} %add_select_fusion.1), channel_id=1, source_target_pairs={{0,9},{1,8},{2,11},{3,10},{4,13},{5,12},{6,15},{7,14},{8,1},{9,0},... | collective-permute-start | bytes 196616 | tf_op jit(solution)/shard_map/ppermute | solution.py:290
  18.3 4.3 %collective-permute-start.5 = (f32[2,32,128]{2,1,0:T(8,128)S(1)}, f32[2,32,128]{2,1,0:T(8,128)S(1)}, u32[]{:S(2)}, u32[]{:S(2)}) collective-permute-start(f32[2,32,128]{2,1,0:T(8,128)S(1)} %fusion), channel_id=1, source_target_pairs={{0,17},{1,16},{2,19},{3,18},{4,21},{5,20},{6,23},{7,22},{8,25},{9,... | collective-permute-start | bytes 98312 | tf_op jit(solution)/shard_map/ppermute | solution.py:290

commit v5 on v4

--- a/solution.py
+++ b/solution.py
@@ -305,18 +305,25 @@
     totals = totals + across
     other = along + both
     outside = jnp.exp(depth) * inside
-    for stride in doublings(1, slabs):
+    for stride in doublings(1, slabs // 4):
         first = ahead(slab, stride)
-        if stride > 1 and 2 * stride < slabs:
+        if stride > 1:
             other = swap(totals, (stride * modes) ^ 1)
-        elif stride > 1:
-            sent = jnp.where((slab // stride) % 2 == 0, totals[:, 0], totals[:, 1])
-            other = swap(sent, (stride * modes) ^ 1)[:, None]
         below = slab % stride
         steps = jnp.where(part == 0, below, stride - 1 - below).astype(jnp.float32)
         outside = outside + jnp.where(first, other * jnp.exp(-depth * steps), 0.0)
         fade = jnp.exp(-depth * float(stride))
         totals = jnp.where(first, totals + fade * other, other + fade * totals)
+    stride = slabs // 4
+    group, below = slab // stride, slab % stride
+    for mask in range(1, 4):
+        partner = group ^ mask
+        lower = partner < group
+        sent = jnp.where(lower, totals[:, 1], totals[:, 0])
+        other = swap(sent, (mask * stride * modes) ^ 1)[:, None]
+        steps = jnp.where(lower, below, stride - 1 - below) + stride * (jnp.abs(group - partner) - 1)
+        heard = other * jnp.exp(-depth * steps.astype(jnp.float32))
+        outside = outside + jnp.where(part == jnp.where(lower, 0, 1), heard, 0.0)
     return outside
 
 

time: 28.4 us -> 27.6 us (0.972)
  waiting for transfers between devices: 10.3 us -> 9.37 us
    ppermute x6 -> x7, waiting for transfers between devices: 10.3 us -> 9.37 us  [swap(): lax.ppermute(value, ('slab', 'mode'), [(i, i ^ mask) for i in range(slabs...]
    ppermute x6 -> x7, starting transfers between devices: 8.45 us -> 8.71 us  [swap(): lax.ppermute(value, ('slab', 'mode'), [(i, i ^ mask) for i in range(slabs...]
  transfers between devices with their start and end apart: 6 -> 7, of which waited for: 6 -> 7; matrix products, arithmetic and copies ran while one was open for 0% -> 0% of each run, Pallas kernels for 0% -> 0%
where the time goes in v5:
time: 27.6 us; the launch traced here: 27.5 us
  waiting for transfers between devices  9.37 us (34%)
  Pallas kernels  9.01 us (33%)
  starting transfers between devices  8.71 us (32%)
  other arithmetic  0.28 us (1%)
    ppermute x7, waiting for transfers between devices, swap(): lax.ppermute(value, ('slab', 'mode'), [(i, i ^ mask) for i in range(slabs...  9.37 us
    ppermute x7, starting transfers between devices, swap(): lax.ppermute(value, ('slab', 'mode'), [(i, i ^ mask) for i in range(slabs...  8.71 us
    pallas_call x1, Pallas kernels, shards(): pl.pallas_call(functools.partial(forces_kernel, count), out_shape=jax.Sha...  5.45 us
    pallas_call x1, Pallas kernels, shards(): pl.pallas_call(functools.partial(moments_kernel, count, height), out_shap...  3.56 us
  transfers between devices with their start and end apart: 7, of which 7 were waited for; matrix products, arithmetic and copies ran while one was open for 0% of the time, Pallas kernels for 0%

profile of v5, /device:TPU:0, one launch (start us, length us, event | category | flops | bytes accessed | tf_op | source)
XLA Modules:
  0.0 27.5 jit_solution(1858749500102295972)
XLA Ops:
  0.0 3.6 %moments.1 = (f32[2,2,32,128]{3,2,1,0:T(8,128)S(1)}, f32[2,32,128]{2,1,0:T(8,128)S(1)}, f32[2,2,64,128]{3,2,1,0:T(8,128)S(1)}, f32[4,2,64,128]{3,2,1,0:T(8,128)S...) custom-call(s32[8]{0:T(128)} %counts_ref.1, ...), custom_call_target="tpu_custom_call" | custom-call | tf_op jit(solution)/shard_map/moments/pallas_call | solution.py:346
  3.6 0.5 %collective-permute-start = (f32[2,2,32,128]{3,2,1,0:T(8,128)S(1)}, f32[2,2,32,128]{3,2,1,0:T(8,128)S(1)}, u32[]{:S(2)}, u32[]{:S(2)}) collective-permute-start(f32[2,2,32,128]{3,2,1,0:T(8,128)S(1)} %get-tuple-element.15), channel_id=1, source_target_pairs={{0,1},{1,0},{2,3},{3,2},{4,5},{5,4},{6,7},{7,6},{8,9},{9,8},{10,11... | collective-permute-start | bytes 196616 | tf_op jit(solution)/shard_map/ppermute | solution.py:290
  4.2 0.8 %collective-permute-done = f32[2,2,32,128]{3,2,1,0:T(8,128)S(1)} collective-permute-done((f32[2,2,32,128]{3,2,1,0:T(8,128)S(1)}, f32[2,2,32,128]{3,2,1,0:T(8,128)S(1)}, u32[]{:S(2)}, u32[]{:S(2)}) %collective-permute-start) | collective-permute-done | bytes 65568 | tf_op jit(solution)/shard_map/ppermute | solution.py:290
  5.0 2.7 %collective-permute-start.1 = (f32[2,2,32,128]{3,2,1,0:T(8,128)S(1)}, f32[2,2,32,128]{3,2,1,0:T(8,128)S(1)}, u32[]{:S(2)}, u32[]{:S(2)}) collective-permute-start(f32[2,2,32,128]{3,2,1,0:T(8,128)S(1)} %add.60), channel_id=1, source_target_pairs={{0,3},{1,2},{2,1},{3,0},{4,7},{5,6},{6,5},{7,4},{8,11},{9,10},{10,... | collective-permute-start | bytes 196616 | tf_op jit(solution)/shard_map/ppermute | solution.py:290
  7.7 1.5 %collective-permute-start.2 = (f32[2,2,32,128]{3,2,1,0:T(8,128)S(1)}, f32[2,2,32,128]{3,2,1,0:T(8,128)S(1)}, u32[]{:S(2)}, u32[]{:S(2)}) collective-permute-start(f32[2,2,32,128]{3,2,1,0:T(8,128)S(1)} %add.60), channel_id=1, source_target_pairs={{0,5},{1,4},{2,7},{3,6},{4,1},{5,0},{6,3},{7,2},{8,13},{9,12},{10,... | collective-permute-start | bytes 196616 | tf_op jit(solution)/shard_map/ppermute | solution.py:290
  9.1 0.0 collective-permute-start.3
  9.2 0.7 %collective-permute-done.1 = f32[2,2,32,128]{3,2,1,0:T(8,128)S(1)} collective-permute-done((f32[2,2,32,128]{3,2,1,0:T(8,128)S(1)}, f32[2,2,32,128]{3,2,1,0:T(8,128)S(1)}, u32[]{:S(2)}, u32[]{:S(2)}) %collective-permute-start.1) | collective-permute-done | bytes 65568 | tf_op jit(solution)/shard_map/ppermute | solution.py:290
  9.9 1.7 %collective-permute-done.2 = f32[2,2,32,128]{3,2,1,0:T(8,128)S(1)} collective-permute-done((f32[2,2,32,128]{3,2,1,0:T(8,128)S(1)}, f32[2,2,32,128]{3,2,1,0:T(8,128)S(1)}, u32[]{:S(2)}, u32[]{:S(2)}) %collective-permute-start.2) | collective-permute-done | bytes 65568 | tf_op jit(solution)/shard_map/ppermute | solution.py:290
  11.6 2.5 %collective-permute-done.3 = f32[2,2,32,128]{3,2,1,0:T(8,128)S(1)} collective-permute-done((f32[2,2,32,128]{3,2,1,0:T(8,128)S(1)}, f32[2,2,32,128]{3,2,1,0:T(8,128)S(1)}, u32[]{:S(2)}, u32[]{:S(2)}) %collective-permute-start.3) | collective-permute-done | bytes 65568 | tf_op jit(solution)/shard_map/ppermute | solution.py:290
  14.1 0.1 add_select_fusion
  14.2 3.4 %collective-permute-start.6 = (f32[2,32,128]{2,1,0:T(8,128)S(1)}, f32[2,32,128]{2,1,0:T(8,128)S(1)}, u32[]{:S(2)}, u32[]{:S(2)}) collective-permute-start(f32[2,32,128]{2,1,0:T(8,128)S(1)} %select_bitcast_fusion), channel_id=1, source_target_pairs={{0,25},{1,24},{2,27},{3,26},{4,29},{5,28},{6,31},{7,30},{8,17},{9,... | collective-permute-start | bytes 98312 | tf_op jit(solution)/shard_map/ppermute | solution.py:290
  17.6 0.0 collective-permute-start.4
  17.6 0.6 %collective-permute-start.5 = (f32[2,32,128]{2,1,0:T(8,128)S(1)}, f32[2,32,128]{2,1,0:T(8,128)S(1)}, u32[]{:S(2)}, u32[]{:S(2)}) collective-permute-start(f32[2,32,128]{2,1,0:T(8,128)S(1)} %get-tuple-element.24), channel_id=1, source_target_pairs={{0,17},{1,16},{2,19},{3,18},{4,21},{5,20},{6,23},{7,22},{8,25},{9,... | collective-permute-start | bytes 98312 | tf_op jit(solution)/shard_map/ppermute | solution.py:290
  18.2 1.2 %collective-permute-done.6 = f32[2,32,128]{2,1,0:T(8,128)S(1)} collective-permute-done((f32[2,32,128]{2,1,0:T(8,128)S(1)}, f32[2,32,128]{2,1,0:T(8,128)S(1)}, u32[]{:S(2)}, u32[]{:S(2)}) %collective-permute-start.6) | collective-permute-done | bytes 32800 | tf_op jit(solution)/shard_map/ppermute | solution.py:290
  19.4 1.6 %collective-permute-done.4 = f32[2,32,128]{2,1,0:T(8,128)S(1)} collective-permute-done((f32[2,32,128]{2,1,0:T(8,128)S(1)}, f32[2,32,128]{2,1,0:T(8,128)S(1)}, u32[]{:S(2)}, u32[]{:S(2)}) %collective-permute-start.4) | collective-permute-done | bytes 32800 | tf_op jit(solution)/shard_map/ppermute | solution.py:290
  21.0 0.9 %collective-permute-done.5 = f32[2,32,128]{2,1,0:T(8,128)S(1)} collective-permute-done((f32[2,32,128]{2,1,0:T(8,128)S(1)}, f32[2,32,128]{2,1,0:T(8,128)S(1)}, u32[]{:S(2)}, u32[]{:S(2)}) %collective-permute-start.5) | collective-permute-done | bytes 32800 | tf_op jit(solution)/shard_map/ppermute | solution.py:290
  21.9 0.1 select_add_fusion.carry_ref
  22.0 5.5 %forces.1 = f32[3,2048]{1,0:T(4,128)} custom-call(f32[2,2,32,128]{3,2,1,0:T(8,128)S(1)} %select_add_fusion.carry_ref, f32[2,2,64,128]{3,2,1,0:T(8,128)S(1)} %get-tuple-element.16.unit_ref, f32[4,2,64,128]{3,2,1,0:T(8,128)S(1)} %get-tuple-element.17.before_ref, f32[2,64,768]{2,1,0:T(8,128)S(1)} %get-tuple-element.18.table_ref, ...), custom_call_target="tpu_custom_call" | custom-call | tf_op jit(solution)/shard_map/forces/pallas_call | solution.py:369
  (9 shorter events, 0.1 us)
Async XLA Ops:
  3.6 1.4 %collective-permute-start = (f32[2,2,32,128]{3,2,1,0:T(8,128)S(1)}, f32[2,2,32,128]{3,2,1,0:T(8,128)S(1)}, u32[]{:S(2)}, u32[]{:S(2)}) collective-permute-start(f32[2,2,32,128]{3,2,1,0:T(8,128)S(1)} %get-tuple-element.15), channel_id=1, source_target_pairs={{0,1},{1,0},{2,3},{3,2},{4,5},{5,4},{6,7},{7,6},{8,9},{9,8},{10,11... | collective-permute-start | bytes 196616 | tf_op jit(solution)/shard_map/ppermute | solution.py:290
  5.0 4.9 %collective-permute-start.1 = (f32[2,2,32,128]{3,2,1,0:T(8,128)S(1)}, f32[2,2,32,128]{3,2,1,0:T(8,128)S(1)}, u32[]{:S(2)}, u32[]{:S(2)}) collective-permute-start(f32[2,2,32,128]{3,2,1,0:T(8,128)S(1)} %add.60), channel_id=1, source_target_pairs={{0,3},{1,2},{2,1},{3,0},{4,7},{5,6},{6,5},{7,4},{8,11},{9,10},{10,... | collective-permute-start | bytes 196616 | tf_op jit(solution)/shard_map/ppermute | solution.py:290
  7.7 3.9 %collective-permute-start.2 = (f32[2,2,32,128]{3,2,1,0:T(8,128)S(1)}, f32[2,2,32,128]{3,2,1,0:T(8,128)S(1)}, u32[]{:S(2)}, u32[]{:S(2)}) collective-permute-start(f32[2,2,32,128]{3,2,1,0:T(8,128)S(1)} %add.60), channel_id=1, source_target_pairs={{0,5},{1,4},{2,7},{3,6},{4,1},{5,0},{6,3},{7,2},{8,13},{9,12},{10,... | collective-permute-start | bytes 196616 | tf_op jit(solution)/shard_map/ppermute | solution.py:290
  9.1 5.0 %collective-permute-start.3 = (f32[2,2,32,128]{3,2,1,0:T(8,128)S(1)}, f32[2,2,32,128]{3,2,1,0:T(8,128)S(1)}, u32[]{:S(2)}, u32[]{:S(2)}) collective-permute-start(f32[2,2,32,128]{3,2,1,0:T(8,128)S(1)} %add.60), channel_id=1, source_target_pairs={{0,7},{1,6},{2,5},{3,4},{4,3},{5,2},{6,1},{7,0},{8,15},{9,14},{10,... | collective-permute-start | bytes 196616 | tf_op jit(solution)/shard_map/ppermute | solution.py:290
  14.2 5.2 %collective-permute-start.6 = (f32[2,32,128]{2,1,0:T(8,128)S(1)}, f32[2,32,128]{2,1,0:T(8,128)S(1)}, u32[]{:S(2)}, u32[]{:S(2)}) collective-permute-start(f32[2,32,128]{2,1,0:T(8,128)S(1)} %select_bitcast_fusion), channel_id=1, source_target_pairs={{0,25},{1,24},{2,27},{3,26},{4,29},{5,28},{6,31},{7,30},{8,17},{9,... | collective-permute-start | bytes 98312 | tf_op jit(solution)/shard_map/ppermute | solution.py:290
  17.6 3.3 %collective-permute-start.4 = (f32[2,32,128]{2,1,0:T(8,128)S(1)}, f32[2,32,128]{2,1,0:T(8,128)S(1)}, u32[]{:S(2)}, u32[]{:S(2)}) collective-permute-start(f32[2,32,128]{2,1,0:T(8,128)S(1)} %get-tuple-element.23), channel_id=1, source_target_pairs={{0,9},{1,8},{2,11},{3,10},{4,13},{5,12},{6,15},{7,14},{8,1},{9,0},... | collective-permute-start | bytes 98312 | tf_op jit(solution)/shard_map/ppermute | solution.py:290
  17.6 4.2 %collective-permute-start.5 = (f32[2,32,128]{2,1,0:T(8,128)S(1)}, f32[2,32,128]{2,1,0:T(8,128)S(1)}, u32[]{:S(2)}, u32[]{:S(2)}) collective-permute-start(f32[2,32,128]{2,1,0:T(8,128)S(1)} %get-tuple-element.24), channel_id=1, source_target_pairs={{0,17},{1,16},{2,19},{3,18},{4,21},{5,20},{6,23},{7,22},{8,25},{9,... | collective-permute-start | bytes 98312 | tf_op jit(solution)/shard_map/ppermute | solution.py:290

commit v6 on v5

--- a/solution.py
+++ b/solution.py
@@ -124,6 +124,38 @@
                 low_ref[at : at + HALF] = low
 
 
+def coefficients(pairs, held, unit_ref, table_ref, coarse_ref):
+    tile = (PDIM, LANES)
+    sign = half_sign(tile)
+    group_sign = jnp.where(even_group(tile), 1.0, -1.0)
+    sides = []
+    for kind in range(2):
+        mixed = held[kind] + group_sign * swap_groups(held[kind])
+        turned = sign * roll(mixed, LANES // 2)
+        sides.append((unit_ref[kind, 0] * turned, unit_ref[kind, 1] * turned, -swap_groups(mixed)))
+    for o in range(3):
+        plus, minus = sides[0][o], sides[1][o]
+        plus_rows = (plus, -sign * roll(plus, LANES // 2))
+        minus_rows = (-sign * minus, roll(minus, LANES // 2))
+        for m in range(pairs):
+            lanes = slice(m * LANES, (m + 1) * LANES)
+            table_plus = table_ref[0, :, lanes]
+            table_minus = table_ref[1, :, lanes]
+            for part in range(2):
+                at = (2 * o + part) * PDIM
+                high, low = split(table_plus * plus_rows[part] + table_minus * minus_rows[part])
+                coarse_ref[at : at + PDIM, lanes] = high
+                coarse_ref[6 * PDIM + at : 6 * PDIM + at + PDIM, lanes] = low
+
+
+def fields(coarse_ref, high_ref, low_ref, phase):
+    field = jnp.dot(coarse_ref[...], high_ref[...], preferred_element_type=jnp.float32)
+    field = field[: 6 * PDIM] + field[6 * PDIM :]
+    field += jnp.dot(coarse_ref[: 6 * PDIM], low_ref[...], preferred_element_type=jnp.float32)
+    parts = [field[o * 2 * PDIM : (o + 1) * 2 * PDIM] for o in range(3)]
+    return jnp.concatenate([jnp.sum(phase * part, axis=0, keepdims=True) for part in parts], axis=0)
+
+
 def moments_kernel(
     count, height, counts_ref, box_ref, positions_ref, charges_ref,
     totals_ref, decay_ref, unit_ref, before_ref, table_ref, weight_ref, phase_ref, sides_ref, powers_ref,
@@ -229,59 +261,45 @@
         decay_ref[kind] = jnp.where(small, depth[: PDIM // 2], depth[PDIM // 2 :])
 
 
-def forces_kernel(
-    count, carry_ref, unit_ref, before_ref, table_ref, weight_ref, phase_ref, sides_ref, powers_ref,
+def near_kernel(
+    count, chosen, before_ref, unit_ref, table_ref, phase_ref, sides_ref, powers_ref,
     forces_ref, coarse_ref, high_ref, low_ref,
 ):
-    blocks = before_ref.shape[0]
-    pairs = count // 2
-    tile = (PDIM, LANES)
-    sign = half_sign(tile)
-    group_sign = jnp.where(even_group(tile), 1.0, -1.0)
-    base = []
+    for i, b in enumerate(chosen):
+        held = [before_ref[b, kind] for kind in range(2)]
+        coefficients(count // 2, held, unit_ref, table_ref, coarse_ref.at[i])
+        spread(count, powers_ref[b], sides_ref[b], high_ref.at[i], low_ref.at[i])
+        forces_ref[:, i * BLOCK : (i + 1) * BLOCK] = fields(coarse_ref.at[i], high_ref.at[i], low_ref.at[i], phase_ref[b])
+
+
+def forces_kernel(
+    count, carry_ref, early_ref, late_ref, unit_ref, table_ref, weight_ref, phase_ref, sides_ref, powers_ref,
+    forces_ref, coarse_ref, high_ref, low_ref,
+):
+    blocks = phase_ref.shape[0]
+    held = []
     small = even_group((PDIM // 2, LANES))
     for kind in range(2):
         up, down = carry_ref[kind, 0], carry_ref[kind, 1]
         top = jnp.where(small, up, roll(down, HALF))
         bottom = jnp.where(small, roll(up, -HALF), down)
-        base.append(jnp.concatenate([top, bottom], axis=0))
-
+        held.append(jnp.concatenate([top, bottom], axis=0))
+    coefficients(count // 2, held, unit_ref, table_ref, coarse_ref)
+    first = early_ref.shape[1] // BLOCK
     for b in range(blocks):
         span = slice(b * BLOCK, (b + 1) * BLOCK)
-        sides = []
-        for kind in range(2):
-            held = base[kind] + before_ref[b, kind]
-            mixed = held + group_sign * swap_groups(held)
-            turned = sign * roll(mixed, LANES // 2)
-            sides.append((unit_ref[kind, 0] * turned, unit_ref[kind, 1] * turned, -swap_groups(mixed)))
-        for o in range(3):
-            plus, minus = sides[0][o], sides[1][o]
-            plus_rows = (plus, -sign * roll(plus, LANES // 2))
-            minus_rows = (-sign * minus, roll(minus, LANES // 2))
-            for m in range(pairs):
-                lanes = slice(m * LANES, (m + 1) * LANES)
-                table_plus = table_ref[0, :, lanes]
-                table_minus = table_ref[1, :, lanes]
-                for part in range(2):
-                    at = (2 * o + part) * PDIM
-                    high, low = split(table_plus * plus_rows[part] + table_minus * minus_rows[part])
-                    coarse_ref[b, at : at + PDIM, lanes] = high
-                    coarse_ref[b, 6 * PDIM + at : 6 * PDIM + at + PDIM, lanes] = low
         spread(count, powers_ref[b], sides_ref[b], high_ref.at[b], low_ref.at[b])
-        field = jnp.dot(coarse_ref[b], high_ref[b], preferred_element_type=jnp.float32)
-        field = field[: 6 * PDIM] + field[6 * PDIM :]
-        field += jnp.dot(coarse_ref[b, : 6 * PDIM], low_ref[b], preferred_element_type=jnp.float32)
-        phase = phase_ref[b]
-        for o in range(3):
-            part = field[o * 2 * PDIM : (o + 1) * 2 * PDIM]
-            forces_ref[o : o + 1, span] = jnp.sum(phase * part, axis=0, keepdims=True) * weight_ref[0:1, span]
+        near_ref, at = (early_ref, b) if b < first else (late_ref, b - first)
+        near = near_ref[:, at * BLOCK : (at + 1) * BLOCK]
+        far = fields(coarse_ref, high_ref.at[b], low_ref.at[b], phase_ref[b])
+        forces_ref[:, span] = (far + near) * weight_ref[0:1, span]
 
 
 def doublings(first, size):
     return [first << i for i in range(32) if first << i < size]
 
 
-def carries(totals, decay, slabs, modes):
+def carries(totals, decay, slabs, modes, early, late):
     slab, mode = lax.axis_index("slab"), lax.axis_index("mode")
     part = jnp.arange(2, dtype=jnp.int32)[None, :, None, None]
     depth = decay[:, None]
@@ -301,6 +319,7 @@
         inside = inside + jnp.where(ahead(mode, stride), other, 0.0)
         totals = totals + other
     across, along, both = [swap(totals, mask) for mask in (strides[-1] ^ 1, modes ^ 1, modes ^ strides[-1] ^ 1)]
+    near = early()
     inside = inside + jnp.where(ahead(mode, strides[-1]), across, 0.0)
     totals = totals + across
     other = along + both
@@ -314,6 +333,8 @@
         outside = outside + jnp.where(first, other * jnp.exp(-depth * steps), 0.0)
         fade = jnp.exp(-depth * float(stride))
         totals = jnp.where(first, totals + fade * other, other + fade * totals)
+    totals, near = lax.optimization_barrier((totals, near))
+    near = near[0], late(near[1])
     stride = slabs // 4
     group, below = slab // stride, slab % stride
     for mask in range(1, 4):
@@ -324,7 +345,7 @@
         steps = jnp.where(lower, below, stride - 1 - below) + stride * (jnp.abs(group - partner) - 1)
         heard = other * jnp.exp(-depth * steps.astype(jnp.float32))
         outside = outside + jnp.where(part == jnp.where(lower, 0, 1), heard, 0.0)
-    return outside
+    return outside, near
 
 
 def shards(positions, charges, counts, box):
@@ -363,20 +384,40 @@
         name="moments",
     )(*inputs)
 
-    carry = carries(totals, decay, slab_count, mode_parts)
-
-    carry, *kept = [pltpu.with_memory_space_constraint(v, pltpu.VMEM) for v in (carry, *kept)]
+    fast = lambda values: [pltpu.with_memory_space_constraint(v, pltpu.VMEM) for v in values]
+    unit, before, table, weight, phase, sides, powers = kept
+    halves = [range(0, blocks // 2), range(blocks // 2, blocks)]
+
+    def near(before, chosen):
+        operands = fast((before, unit, table, phase, sides, powers))
+        return pl.pallas_call(
+            functools.partial(near_kernel, count, chosen),
+            out_shape=pltpu.VMEM((3, len(chosen) * BLOCK), jnp.float32),
+            in_specs=[vector] * 6,
+            out_specs=vector,
+            scratch_shapes=[
+                pltpu.VMEM((len(chosen), 12 * PDIM, terms), jnp.bfloat16),
+                pltpu.VMEM((len(chosen), terms, BLOCK), jnp.bfloat16),
+                pltpu.VMEM((len(chosen), terms, BLOCK), jnp.bfloat16),
+            ],
+            compiler_params=params,
+            cost_estimate=pl.CostEstimate(flops=12 * PDIM * terms * BLOCK * len(chosen) * 3 // 2, bytes_accessed=1 << 20, transcendentals=0),
+            name="near",
+        )(*operands)
+
+    carry, (early, late) = carries(
+        totals, decay, slab_count, mode_parts,
+        lambda: (near(before, halves[0]), before), lambda held: near(held, halves[1]),
+    )
     return pl.pallas_call(
         functools.partial(forces_kernel, count),
         out_shape=jax.ShapeDtypeStruct((3, ions), jnp.float32),
-        in_specs=[vector] * 8,
+        in_specs=[vector] * 9,
         out_specs=vector,
-        scratch_shapes=[
-            pltpu.VMEM((blocks, 12 * PDIM, terms), jnp.bfloat16),
-        ] + work,
+        scratch_shapes=[pltpu.VMEM((12 * PDIM, terms), jnp.bfloat16)] + work,
         compiler_params=params,
         name="forces",
-    )(carry, *kept)
+    )(*fast((carry, early, late, unit, table, weight, phase, sides, powers)))
 
 
 def solution(mesh):

time: 27.6 us -> 27.1 us (0.982)
  waiting for transfers between devices: 9.37 us -> 4.04 us
  Pallas kernels: 9.01 us -> 13.8 us
    ppermute x7, waiting for transfers between devices: 9.37 us -> 4.04 us  [swap(): lax.ppermute(value, ('slab', 'mode'), [(i, i ^ mask) for i in range(slabs...]
    pallas_call x0 -> x2, Pallas kernels: none -> 5.27 us  [near(): pl.pallas_call(functools.partial(near_kernel, count, chosen), out_shape=p...]
    pallas_call x1, Pallas kernels: 5.45 us -> 4.95 us  [shards(): pl.pallas_call(functools.partial(forces_kernel, count), out_shape=jax.Sha...]
  transfers between devices with their start and end apart: 7 -> 7, of which waited for: 7 -> 4; matrix products, arithmetic and copies ran while one was open for 0% -> 0% of each run, Pallas kernels for 0% -> 20%
where the time goes in v6:
time: 27.1 us; the launch traced here: 27 us
  Pallas kernels  13.8 us (51%)
  starting transfers between devices  8.71 us (32%)
  waiting for transfers between devices  4.04 us (15%)
  other arithmetic  0.29 us (1%)
    ppermute x7, starting transfers between devices, swap(): lax.ppermute(value, ('slab', 'mode'), [(i, i ^ mask) for i in range(slabs...  8.71 us
    pallas_call x2, Pallas kernels, near(): pl.pallas_call(functools.partial(near_kernel, count, chosen), out_shape=p...  5.27 us
    pallas_call x1, Pallas kernels, shards(): pl.pallas_call(functools.partial(forces_kernel, count), out_shape=jax.Sha...  4.95 us
    ppermute x7, waiting for transfers between devices, swap(): lax.ppermute(value, ('slab', 'mode'), [(i, i ^ mask) for i in range(slabs...  4.04 us
    pallas_call x1, Pallas kernels, shards(): pl.pallas_call(functools.partial(moments_kernel, count, height), out_shap...  3.56 us
  transfers between devices with their start and end apart: 7, of which 4 were waited for; matrix products, arithmetic and copies ran while one was open for 0% of the time, Pallas kernels for 20%

profile of v6, /device:TPU:0, one launch (start us, length us, event | category | flops | bytes accessed | tf_op | source)
XLA Modules:
  0.0 27.0 jit_solution(2825236769710190880)
XLA Ops:
  0.0 3.6 %moments.1 = (f32[2,2,32,128]{3,2,1,0:T(8,128)S(1)}, f32[2,32,128]{2,1,0:T(8,128)S(1)}, f32[2,2,64,128]{3,2,1,0:T(8,128)S(1)}, f32[4,2,64,128]{3,2,1,0:T(8,128)S...) custom-call(s32[8]{0:T(128)} %counts_ref.1, ...), custom_call_target="tpu_custom_call" | custom-call | tf_op jit(solution)/shard_map/moments/pallas_call | solution.py:367
  3.6 0.5 %collective-permute-start = (f32[2,2,32,128]{3,2,1,0:T(8,128)S(1)}, f32[2,2,32,128]{3,2,1,0:T(8,128)S(1)}, u32[]{:S(2)}, u32[]{:S(2)}) collective-permute-start(f32[2,2,32,128]{3,2,1,0:T(8,128)S(1)} %get-tuple-element.18), channel_id=1, source_target_pairs={{0,1},{1,0},{2,3},{3,2},{4,5},{5,4},{6,7},{7,6},{8,9},{9,8},{10,11... | collective-permute-start | bytes 196616 | tf_op jit(solution)/shard_map/ppermute | solution.py:308
  4.2 0.8 %collective-permute-done = f32[2,2,32,128]{3,2,1,0:T(8,128)S(1)} collective-permute-done((f32[2,2,32,128]{3,2,1,0:T(8,128)S(1)}, f32[2,2,32,128]{3,2,1,0:T(8,128)S(1)}, u32[]{:S(2)}, u32[]{:S(2)}) %collective-permute-start) | collective-permute-done | bytes 65568 | tf_op jit(solution)/shard_map/ppermute | solution.py:308
  5.0 2.7 %collective-permute-start.1 = (f32[2,2,32,128]{3,2,1,0:T(8,128)S(1)}, f32[2,2,32,128]{3,2,1,0:T(8,128)S(1)}, u32[]{:S(2)}, u32[]{:S(2)}) collective-permute-start(f32[2,2,32,128]{3,2,1,0:T(8,128)S(1)} %add.60), channel_id=1, source_target_pairs={{0,3},{1,2},{2,1},{3,0},{4,7},{5,6},{6,5},{7,4},{8,11},{9,10},{10,... | collective-permute-start | bytes 196616 | tf_op jit(solution)/shard_map/ppermute | solution.py:308
  7.7 1.5 %collective-permute-start.2 = (f32[2,2,32,128]{3,2,1,0:T(8,128)S(1)}, f32[2,2,32,128]{3,2,1,0:T(8,128)S(1)}, u32[]{:S(2)}, u32[]{:S(2)}) collective-permute-start(f32[2,2,32,128]{3,2,1,0:T(8,128)S(1)} %add.60), channel_id=1, source_target_pairs={{0,5},{1,4},{2,7},{3,6},{4,1},{5,0},{6,3},{7,2},{8,13},{9,12},{10,... | collective-permute-start | bytes 196616 | tf_op jit(solution)/shard_map/ppermute | solution.py:308
  9.1 0.0 collective-permute-start.3
  9.2 2.6 %near.2.early_ref = f32[3,1024]{1,0:T(4,128)S(1)} custom-call(f32[4,2,64,128]{3,2,1,0:T(8,128)S(1)} %get-tuple-element.27.before_ref, f32[2,2,64,128]{3,2,1,0:T(8,128)S(1)} %get-tuple-element.20.unit_ref, f32[2,64,768]{2,1,0:T(8,128)S(1)} %get-tuple-element.21.table_ref, f32[4,128,512]{2,1,0:T(8,128)S(1)} %get-tuple-element.22.phase_ref, ...), custom_call_target="tpu_custom_call" | custom-call | flops 905969664 | bytes 1048576 | tf_op jit(solution)/shard_map/near/pallas_call | solution.py:393
  11.8 0.0 collective-permute-done.1
  11.8 0.0 collective-permute-done.2
  11.8 2.3 %collective-permute-done.3 = f32[2,2,32,128]{3,2,1,0:T(8,128)S(1)} collective-permute-done((f32[2,2,32,128]{3,2,1,0:T(8,128)S(1)}, f32[2,2,32,128]{3,2,1,0:T(8,128)S(1)}, u32[]{:S(2)}, u32[]{:S(2)}) %collective-permute-start.3) | collective-permute-done | bytes 65568 | tf_op jit(solution)/shard_map/ppermute | solution.py:308
  14.1 0.1 add_select_fusion
  14.2 3.4 %collective-permute-start.6 = (f32[2,32,128]{2,1,0:T(8,128)S(1)}, f32[2,32,128]{2,1,0:T(8,128)S(1)}, u32[]{:S(2)}, u32[]{:S(2)}) collective-permute-start(f32[2,32,128]{2,1,0:T(8,128)S(1)} %fusion), channel_id=1, source_target_pairs={{0,25},{1,24},{2,27},{3,26},{4,29},{5,28},{6,31},{7,30},{8,17},{9,... | collective-permute-start | bytes 98312 | tf_op jit(solution)/shard_map/ppermute | solution.py:308
  17.6 0.0 collective-permute-start.4
  17.6 0.6 %collective-permute-start.5 = (f32[2,32,128]{2,1,0:T(8,128)S(1)}, f32[2,32,128]{2,1,0:T(8,128)S(1)}, u32[]{:S(2)}, u32[]{:S(2)}) collective-permute-start(f32[2,32,128]{2,1,0:T(8,128)S(1)} %get-tuple-element.30), channel_id=1, source_target_pairs={{0,17},{1,16},{2,19},{3,18},{4,21},{5,20},{6,23},{7,22},{8,25},{9,... | collective-permute-start | bytes 98312 | tf_op jit(solution)/shard_map/ppermute | solution.py:308
  18.2 2.6 %near.3.late_ref = f32[3,1024]{1,0:T(4,128)S(1)} custom-call(f32[4,2,64,128]{3,2,1,0:T(8,128)S(1)} %get-tuple-element.27.before_ref, f32[2,2,64,128]{3,2,1,0:T(8,128)S(1)} %get-tuple-element.20.unit_ref, f32[2,64,768]{2,1,0:T(8,128)S(1)} %get-tuple-element.21.table_ref, f32[4,128,512]{2,1,0:T(8,128)S(1)} %get-tuple-element.22.phase_ref, ...), custom_call_target="tpu_custom_call" | custom-call | flops 905969664 | bytes 1048576 | tf_op jit(solution)/shard_map/near/pallas_call | solution.py:393
  20.9 0.0 collective-permute-done.6
  20.9 0.1 collective-permute-done.4
  21.0 0.9 %collective-permute-done.5 = f32[2,32,128]{2,1,0:T(8,128)S(1)} collective-permute-done((f32[2,32,128]{2,1,0:T(8,128)S(1)}, f32[2,32,128]{2,1,0:T(8,128)S(1)}, u32[]{:S(2)}, u32[]{:S(2)}) %collective-permute-start.5) | collective-permute-done | bytes 32800 | tf_op jit(solution)/shard_map/ppermute | solution.py:308
  21.9 0.1 select_add_fusion.carry_ref
  22.0 5.0 %forces.1 = f32[3,2048]{1,0:T(4,128)} custom-call(f32[2,2,32,128]{3,2,1,0:T(8,128)S(1)} %select_add_fusion.carry_ref, f32[3,1024]{1,0:T(4,128)S(1)} %near.2.early_ref, f32[3,1024]{1,0:T(4,128)S(1)} %near.3.late_ref, f32[2,2,64,128]{3,2,1,0:T(8,128)S(1)} %get-tuple-element.20.unit_ref, f32[2,64,768]{2,1,0:T(8,128)S(1)} %get-tuple-element.21.table_ref, ...), custom_call_target="tpu_custom_call" | custom-call | tf_op jit(solution)/shard_map/forces/pallas_call | solution.py:412
  (9 shorter events, 0.1 us)
Async XLA Ops:
  3.6 1.4 %collective-permute-start = (f32[2,2,32,128]{3,2,1,0:T(8,128)S(1)}, f32[2,2,32,128]{3,2,1,0:T(8,128)S(1)}, u32[]{:S(2)}, u32[]{:S(2)}) collective-permute-start(f32[2,2,32,128]{3,2,1,0:T(8,128)S(1)} %get-tuple-element.18), channel_id=1, source_target_pairs={{0,1},{1,0},{2,3},{3,2},{4,5},{5,4},{6,7},{7,6},{8,9},{9,8},{10,11... | collective-permute-start | bytes 196616 | tf_op jit(solution)/shard_map/ppermute | solution.py:308
  5.0 6.8 %collective-permute-start.1 = (f32[2,2,32,128]{3,2,1,0:T(8,128)S(1)}, f32[2,2,32,128]{3,2,1,0:T(8,128)S(1)}, u32[]{:S(2)}, u32[]{:S(2)}) collective-permute-start(f32[2,2,32,128]{3,2,1,0:T(8,128)S(1)} %add.60), channel_id=1, source_target_pairs={{0,3},{1,2},{2,1},{3,0},{4,7},{5,6},{6,5},{7,4},{8,11},{9,10},{10,... | collective-permute-start | bytes 196616 | tf_op jit(solution)/shard_map/ppermute | solution.py:308
  7.7 4.2 %collective-permute-start.2 = (f32[2,2,32,128]{3,2,1,0:T(8,128)S(1)}, f32[2,2,32,128]{3,2,1,0:T(8,128)S(1)}, u32[]{:S(2)}, u32[]{:S(2)}) collective-permute-start(f32[2,2,32,128]{3,2,1,0:T(8,128)S(1)} %add.60), channel_id=1, source_target_pairs={{0,5},{1,4},{2,7},{3,6},{4,1},{5,0},{6,3},{7,2},{8,13},{9,12},{10,... | collective-permute-start | bytes 196616 | tf_op jit(solution)/shard_map/ppermute | solution.py:308
  9.1 5.0 %collective-permute-start.3 = (f32[2,2,32,128]{3,2,1,0:T(8,128)S(1)}, f32[2,2,32,128]{3,2,1,0:T(8,128)S(1)}, u32[]{:S(2)}, u32[]{:S(2)}) collective-permute-start(f32[2,2,32,128]{3,2,1,0:T(8,128)S(1)} %add.60), channel_id=1, source_target_pairs={{0,7},{1,6},{2,5},{3,4},{4,3},{5,2},{6,1},{7,0},{8,15},{9,14},{10,... | collective-permute-start | bytes 196616 | tf_op jit(solution)/shard_map/ppermute | solution.py:308
  14.2 6.7 %collective-permute-start.6 = (f32[2,32,128]{2,1,0:T(8,128)S(1)}, f32[2,32,128]{2,1,0:T(8,128)S(1)}, u32[]{:S(2)}, u32[]{:S(2)}) collective-permute-start(f32[2,32,128]{2,1,0:T(8,128)S(1)} %fusion), channel_id=1, source_target_pairs={{0,25},{1,24},{2,27},{3,26},{4,29},{5,28},{6,31},{7,30},{8,17},{9,... | collective-permute-start | bytes 98312 | tf_op jit(solution)/shard_map/ppermute | solution.py:308
  17.6 3.3 %collective-permute-start.4 = (f32[2,32,128]{2,1,0:T(8,128)S(1)}, f32[2,32,128]{2,1,0:T(8,128)S(1)}, u32[]{:S(2)}, u32[]{:S(2)}) collective-permute-start(f32[2,32,128]{2,1,0:T(8,128)S(1)} %get-tuple-element.29), channel_id=1, source_target_pairs={{0,9},{1,8},{2,11},{3,10},{4,13},{5,12},{6,15},{7,14},{8,1},{9,0},... | collective-permute-start | bytes 98312 | tf_op jit(solution)/shard_map/ppermute | solution.py:308
  17.6 4.2 %collective-permute-start.5 = (f32[2,32,128]{2,1,0:T(8,128)S(1)}, f32[2,32,128]{2,1,0:T(8,128)S(1)}, u32[]{:S(2)}, u32[]{:S(2)}) collective-permute-start(f32[2,32,128]{2,1,0:T(8,128)S(1)} %get-tuple-element.30), channel_id=1, source_target_pairs={{0,17},{1,16},{2,19},{3,18},{4,21},{5,20},{6,23},{7,22},{8,25},{9,... | collective-permute-start | bytes 98312 | tf_op jit(solution)/shard_map/ppermute | solution.py:308

commit v7 on v6

--- a/solution.py
+++ b/solution.py
@@ -28,11 +28,14 @@
     a = 0.5 * height * two_pi * math.hypot(PDIM, HALF) / box_low
     nodes = np.cos(np.pi * (np.arange(64) + 0.5) / 64)
     order = np.arange(32)[:, None]
-    coefficients = np.abs((np.exp(-a * (1.0 + nodes)) * np.cos(order * np.arccos(nodes))).sum(1) / 32.0)
-    count = 4
-    while coefficients[count:].sum() > 2.0**-24:
+    parts = np.abs((np.exp(-a * (1.0 + nodes)) * np.cos(order * np.arccos(nodes))).sum(1) / 32.0)
+    parts[0] *= 0.5
+    count = exact = 4
+    while parts[count:].sum() > 2.0**-24:
         count += 4
-    return count
+    while exact < count and parts[exact:].max() > 2.0**-9 * parts.max():
+        exact += 4
+    return count, exact
 
 
 def poly(terms, u):
@@ -113,18 +116,20 @@
     return plus, minus
 
 
-def spread(count, powers, sides, high_ref, low_ref):
+def spread(count, exact, powers, sides, spread_ref):
     for m in range(count // 2):
         for part in range(2):
             for parity in range(2):
                 at = m * LANES + part * 2 * HALF + parity * HALF
                 n = 2 * m + parity
-                high, low = split(powers[n : n + 1] * sides[part * HALF : (part + 1) * HALF])
-                high_ref[at : at + HALF] = high
-                low_ref[at : at + HALF] = low
-
-
-def coefficients(pairs, held, unit_ref, table_ref, coarse_ref):
+                value = powers[n : n + 1] * sides[part * HALF : (part + 1) * HALF]
+                if n < exact:
+                    value, low = split(value)
+                    spread_ref[count * 2 * HALF + at : count * 2 * HALF + at + HALF] = low
+                spread_ref[at : at + HALF] = value.astype(jnp.bfloat16)
+
+
+def coefficients(count, exact, held, unit_ref, table_ref, coarse_ref):
     tile = (PDIM, LANES)
     sign = half_sign(tile)
     group_sign = jnp.where(even_group(tile), 1.0, -1.0)
@@ -137,29 +142,34 @@
         plus, minus = sides[0][o], sides[1][o]
         plus_rows = (plus, -sign * roll(plus, LANES // 2))
         minus_rows = (-sign * minus, roll(minus, LANES // 2))
-        for m in range(pairs):
+        for m in range(count // 2):
             lanes = slice(m * LANES, (m + 1) * LANES)
             table_plus = table_ref[0, :, lanes]
             table_minus = table_ref[1, :, lanes]
             for part in range(2):
                 at = (2 * o + part) * PDIM
-                high, low = split(table_plus * plus_rows[part] + table_minus * minus_rows[part])
-                coarse_ref[at : at + PDIM, lanes] = high
-                coarse_ref[6 * PDIM + at : 6 * PDIM + at + PDIM, lanes] = low
-
-
-def fields(coarse_ref, high_ref, low_ref, phase):
-    field = jnp.dot(coarse_ref[...], high_ref[...], preferred_element_type=jnp.float32)
+                value = table_plus * plus_rows[part] + table_minus * minus_rows[part]
+                if 2 * m < exact:
+                    value, low = split(value)
+                    coarse_ref[6 * PDIM + at : 6 * PDIM + at + PDIM, lanes] = low
+                    again = slice(count * 2 * HALF + m * LANES, count * 2 * HALF + (m + 1) * LANES)
+                    coarse_ref[at : at + PDIM, again] = value
+                coarse_ref[at : at + PDIM, lanes] = value.astype(jnp.bfloat16)
+
+
+def fields(exact, coarse_ref, spread_ref, phase):
+    cut = exact * 2 * HALF
+    field = jnp.dot(coarse_ref[:, :cut], spread_ref[:cut], preferred_element_type=jnp.float32)
     field = field[: 6 * PDIM] + field[6 * PDIM :]
-    field += jnp.dot(coarse_ref[: 6 * PDIM], low_ref[...], preferred_element_type=jnp.float32)
+    field += jnp.dot(coarse_ref[: 6 * PDIM, cut:], spread_ref[cut:], preferred_element_type=jnp.float32)
     parts = [field[o * 2 * PDIM : (o + 1) * 2 * PDIM] for o in range(3)]
     return jnp.concatenate([jnp.sum(phase * part, axis=0, keepdims=True) for part in parts], axis=0)
 
 
 def moments_kernel(
-    count, height, counts_ref, box_ref, positions_ref, charges_ref,
+    count, exact, height, counts_ref, box_ref, positions_ref, charges_ref,
     totals_ref, decay_ref, unit_ref, before_ref, table_ref, weight_ref, phase_ref, sides_ref, powers_ref,
-    high_ref, low_ref,
+    spread_ref,
 ):
     ions = positions_ref.shape[1]
     blocks = ions // BLOCK
@@ -220,18 +230,21 @@
             powers.append(2.0 * t * powers[-1] - powers[-2])
         powers = jnp.concatenate(powers, axis=0)
         powers_ref[b] = powers
-        spread(count, powers, sides, high_ref.at[b], low_ref.at[b])
+        spread(count, exact, powers, sides, spread_ref.at[b])
 
         heavy_high, heavy_low = split(phase * weight)
         both = jnp.concatenate([heavy_high, heavy_low], axis=0)
         across = (((1,), (1,)), ((), ()))
-        first = lax.dot_general(both, high_ref[b], across, preferred_element_type=jnp.float32)
-        second = lax.dot_general(heavy_high, low_ref[b], across, preferred_element_type=jnp.float32)
-        moments = first[: 2 * PDIM] + first[2 * PDIM :] + second
+        cut, rest = exact * 2 * HALF, (count - exact) * 2 * HALF
+        first = lax.dot_general(both, spread_ref[b, :cut], across, preferred_element_type=jnp.float32)
+        second = lax.dot_general(heavy_high, spread_ref[b, cut:], across, preferred_element_type=jnp.float32)
+        moments = first[: 2 * PDIM] + first[2 * PDIM :] + second[:, rest:]
+        moments = [moments[:, m * LANES : (m + 1) * LANES] for m in range(exact // 2)]
+        moments += [second[:, m * LANES : (m + 1) * LANES] for m in range((count - exact) // 2)]
 
         sums = [jnp.zeros(tile, jnp.float32) for _ in range(4)]
         for m in range(pairs):
-            piece = moments[:, m * LANES : (m + 1) * LANES]
+            piece = moments[m]
             for kind, values in enumerate((plus[m], minus[m])):
                 sums[2 * kind] += values * piece[:PDIM]
                 sums[2 * kind + 1] += values * piece[PDIM:]
@@ -262,19 +275,20 @@
 
 
 def near_kernel(
-    count, chosen, before_ref, unit_ref, table_ref, phase_ref, sides_ref, powers_ref,
-    forces_ref, coarse_ref, high_ref, low_ref,
+    count, exact, chosen, before_ref, unit_ref, table_ref, phase_ref, sides_ref, powers_ref,
+    forces_ref, coarse_ref, spread_ref,
 ):
     for i, b in enumerate(chosen):
         held = [before_ref[b, kind] for kind in range(2)]
-        coefficients(count // 2, held, unit_ref, table_ref, coarse_ref.at[i])
-        spread(count, powers_ref[b], sides_ref[b], high_ref.at[i], low_ref.at[i])
-        forces_ref[:, i * BLOCK : (i + 1) * BLOCK] = fields(coarse_ref.at[i], high_ref.at[i], low_ref.at[i], phase_ref[b])
+        coefficients(count, exact, held, unit_ref, table_ref, coarse_ref.at[i])
+        spread(count, exact, powers_ref[b], sides_ref[b], spread_ref.at[i])
+        found = fields(exact, coarse_ref.at[i], spread_ref.at[i], phase_ref[b])
+        forces_ref[:, i * BLOCK : (i + 1) * BLOCK] = found
 
 
 def forces_kernel(
-    count, carry_ref, early_ref, late_ref, unit_ref, table_ref, weight_ref, phase_ref, sides_ref, powers_ref,
-    forces_ref, coarse_ref, high_ref, low_ref,
+    count, exact, carry_ref, early_ref, late_ref, unit_ref, table_ref, weight_ref, phase_ref, sides_ref, powers_ref,
+    forces_ref, coarse_ref, spread_ref,
 ):
     blocks = phase_ref.shape[0]
     held = []
@@ -284,14 +298,14 @@
         top = jnp.where(small, up, roll(down, HALF))
         bottom = jnp.where(small, roll(up, -HALF), down)
         held.append(jnp.concatenate([top, bottom], axis=0))
-    coefficients(count // 2, held, unit_ref, table_ref, coarse_ref)
+    coefficients(count, exact, held, unit_ref, table_ref, coarse_ref)
     first = early_ref.shape[1] // BLOCK
     for b in range(blocks):
         span = slice(b * BLOCK, (b + 1) * BLOCK)
-        spread(count, powers_ref[b], sides_ref[b], high_ref.at[b], low_ref.at[b])
+        spread(count, exact, powers_ref[b], sides_ref[b], spread_ref.at[b])
         near_ref, at = (early_ref, b) if b < first else (late_ref, b - first)
         near = near_ref[:, at * BLOCK : (at + 1) * BLOCK]
-        far = fields(coarse_ref, high_ref.at[b], low_ref.at[b], phase_ref[b])
+        far = fields(exact, coarse_ref, spread_ref.at[b], phase_ref[b])
         forces_ref[:, span] = (far + near) * weight_ref[0:1, span]
 
 
@@ -352,20 +366,20 @@
     slab_count = lax.axis_size("slab")
     mode_parts = lax.axis_size("mode")
     height = slab_span / slab_count
-    count = series_terms(height)
+    count, exact = series_terms(height)
     ions = positions.shape[1]
     blocks = ions // BLOCK
-    terms = count * 2 * HALF
+    terms, all_terms = count * 2 * HALF, (count + exact) * 2 * HALF
     half = PDIM // 2
     scalar = pl.BlockSpec(memory_space=pltpu.SMEM)
     vector = pl.BlockSpec(memory_space=pltpu.VMEM)
     params = pltpu.CompilerParams(vmem_limit_bytes=40 * 1024 * 1024)
-    work = [pltpu.VMEM((blocks, terms, BLOCK), jnp.bfloat16)] * 2
+    work = [pltpu.VMEM((blocks, all_terms, BLOCK), jnp.bfloat16)]
     inputs = [
         pltpu.with_memory_space_constraint(v, pltpu.HBM) for v in (counts, box, positions, charges[None, :])
     ]
     totals, decay, *kept = pl.pallas_call(
-        functools.partial(moments_kernel, count, height),
+        functools.partial(moments_kernel, count, exact, height),
         out_shape=[
             pltpu.VMEM((2, 2, half, LANES), jnp.float32),
             pltpu.VMEM((2, half, LANES), jnp.float32),
@@ -391,14 +405,13 @@
     def near(before, chosen):
         operands = fast((before, unit, table, phase, sides, powers))
         return pl.pallas_call(
-            functools.partial(near_kernel, count, chosen),
+            functools.partial(near_kernel, count, exact, chosen),
             out_shape=pltpu.VMEM((3, len(chosen) * BLOCK), jnp.float32),
             in_specs=[vector] * 6,
             out_specs=vector,
             scratch_shapes=[
-                pltpu.VMEM((len(chosen), 12 * PDIM, terms), jnp.bfloat16),
-                pltpu.VMEM((len(chosen), terms, BLOCK), jnp.bfloat16),
-                pltpu.VMEM((len(chosen), terms, BLOCK), jnp.bfloat16),
+                pltpu.VMEM((len(chosen), 12 * PDIM, all_terms), jnp.bfloat16),
+                pltpu.VMEM((len(chosen), all_terms, BLOCK), jnp.bfloat16),
             ],
             compiler_params=params,
             cost_estimate=pl.CostEstimate(flops=12 * PDIM * terms * BLOCK * len(chosen) * 3 // 2, bytes_accessed=1 << 20, transcendentals=0),
@@ -410,11 +423,11 @@
         lambda: (near(before, halves[0]), before), lambda held: near(held, halves[1]),
     )
     return pl.pallas_call(
-        functools.partial(forces_kernel, count),
+        functools.partial(forces_kernel, count, exact),
         out_shape=jax.ShapeDtypeStruct((3, ions), jnp.float32),
         in_specs=[vector] * 9,
         out_specs=vector,
-        scratch_shapes=[pltpu.VMEM((12 * PDIM, terms), jnp.bfloat16)] + work,
+        scratch_shapes=[pltpu.VMEM((12 * PDIM, all_terms), jnp.bfloat16)] + work,
         compiler_params=params,
         name="forces",
     )(*fast((carry, early, late, unit, table, weight, phase, sides, powers)))

time: 27.1 us -> 26.1 us (0.963)
  Pallas kernels: 13.8 us -> 11.8 us
  waiting for transfers between devices: 4.04 us -> 5 us
    pallas_call x4, Pallas kernels: 13.8 us -> 11.8 us  [the longest x2 4.33 us: near(): pl.pallas_call(functools.partial(near_kernel, count, exact, chosen), out_...]
    ppermute x7, waiting for transfers between devices: 4.04 us -> 5 us  [swap(): lax.ppermute(value, ('slab', 'mode'), [(i, i ^ mask) for i in range(slabs...]
  transfers between devices with their start and end apart: 7 -> 7, of which waited for: 4 -> 5; matrix products, arithmetic and copies ran while one was open for 0% -> 0% of each run, Pallas kernels for 20% -> 17%
where the time goes in v7:
time: 26.1 us; the launch traced here: 25.9 us
  Pallas kernels  11.8 us (45%)
  starting transfers between devices  8.7 us (33%)
  waiting for transfers between devices  5 us (19%)
  other arithmetic  0.29 us (1%)
    ppermute x7, starting transfers between devices, swap(): lax.ppermute(value, ('slab', 'mode'), [(i, i ^ mask) for i in range(slabs...  8.7 us
    ppermute x7, waiting for transfers between devices, swap(): lax.ppermute(value, ('slab', 'mode'), [(i, i ^ mask) for i in range(slabs...  5 us
    pallas_call x2, Pallas kernels, near(): pl.pallas_call(functools.partial(near_kernel, count, exact, chosen), out_...  4.33 us
    pallas_call x1, Pallas kernels, shards(): pl.pallas_call(functools.partial(forces_kernel, count, exact), out_shape=...  4.1 us
    pallas_call x1, Pallas kernels, shards(): pl.pallas_call(functools.partial(moments_kernel, count, exact, height), o...  3.34 us
  transfers between devices with their start and end apart: 7, of which 5 were waited for; matrix products, arithmetic and copies ran while one was open for 0% of the time, Pallas kernels for 17%

profile of v7, /device:TPU:0, one launch (start us, length us, event | category | flops | bytes accessed | tf_op | source)
XLA Modules:
  0.0 25.9 jit_solution(13320845734955513780)
XLA Ops:
  0.0 3.3 %moments.1 = (f32[2,2,32,128]{3,2,1,0:T(8,128)S(1)}, f32[2,32,128]{2,1,0:T(8,128)S(1)}, f32[2,2,64,128]{3,2,1,0:T(8,128)S(1)}, f32[4,2,64,128]{3,2,1,0:T(8,128)S...) custom-call(s32[8]{0:T(128)} %counts_ref.1, ...), custom_call_target="tpu_custom_call" | custom-call | tf_op jit(solution)/shard_map/moments/pallas_call | solution.py:381
  3.3 0.5 %collective-permute-start = (f32[2,2,32,128]{3,2,1,0:T(8,128)S(1)}, f32[2,2,32,128]{3,2,1,0:T(8,128)S(1)}, u32[]{:S(2)}, u32[]{:S(2)}) collective-permute-start(f32[2,2,32,128]{3,2,1,0:T(8,128)S(1)} %get-tuple-element.18), channel_id=1, source_target_pairs={{0,1},{1,0},{2,3},{3,2},{4,5},{5,4},{6,7},{7,6},{8,9},{9,8},{10,11... | collective-permute-start | bytes 196616 | tf_op jit(solution)/shard_map/ppermute | solution.py:322
  4.0 0.8 %collective-permute-done = f32[2,2,32,128]{3,2,1,0:T(8,128)S(1)} collective-permute-done((f32[2,2,32,128]{3,2,1,0:T(8,128)S(1)}, f32[2,2,32,128]{3,2,1,0:T(8,128)S(1)}, u32[]{:S(2)}, u32[]{:S(2)}) %collective-permute-start) | collective-permute-done | bytes 65568 | tf_op jit(solution)/shard_map/ppermute | solution.py:322
  4.8 2.7 %collective-permute-start.1 = (f32[2,2,32,128]{3,2,1,0:T(8,128)S(1)}, f32[2,2,32,128]{3,2,1,0:T(8,128)S(1)}, u32[]{:S(2)}, u32[]{:S(2)}) collective-permute-start(f32[2,2,32,128]{3,2,1,0:T(8,128)S(1)} %add.60), channel_id=1, source_target_pairs={{0,3},{1,2},{2,1},{3,0},{4,7},{5,6},{6,5},{7,4},{8,11},{9,10},{10,... | collective-permute-start | bytes 196616 | tf_op jit(solution)/shard_map/ppermute | solution.py:322
  7.4 1.5 %collective-permute-start.2 = (f32[2,2,32,128]{3,2,1,0:T(8,128)S(1)}, f32[2,2,32,128]{3,2,1,0:T(8,128)S(1)}, u32[]{:S(2)}, u32[]{:S(2)}) collective-permute-start(f32[2,2,32,128]{3,2,1,0:T(8,128)S(1)} %add.60), channel_id=1, source_target_pairs={{0,5},{1,4},{2,7},{3,6},{4,1},{5,0},{6,3},{7,2},{8,13},{9,12},{10,... | collective-permute-start | bytes 196616 | tf_op jit(solution)/shard_map/ppermute | solution.py:322
  8.9 0.0 collective-permute-start.3
  8.9 2.2 %near.2.early_ref = f32[3,1024]{1,0:T(4,128)S(1)} custom-call(f32[4,2,64,128]{3,2,1,0:T(8,128)S(1)} %get-tuple-element.27.before_ref, f32[2,2,64,128]{3,2,1,0:T(8,128)S(1)} %get-tuple-element.20.unit_ref, f32[2,64,768]{2,1,0:T(8,128)S(1)} %get-tuple-element.21.table_ref, f32[4,128,512]{2,1,0:T(8,128)S(1)} %get-tuple-element.22.phase_ref, ...), custom_call_target="tpu_custom_call" | custom-call | flops 905969664 | bytes 1048576 | tf_op jit(solution)/shard_map/near/pallas_call | solution.py:407
  11.1 0.0 collective-permute-done.1
  11.1 0.2 collective-permute-done.2
  11.4 2.5 %collective-permute-done.3 = f32[2,2,32,128]{3,2,1,0:T(8,128)S(1)} collective-permute-done((f32[2,2,32,128]{3,2,1,0:T(8,128)S(1)}, f32[2,2,32,128]{3,2,1,0:T(8,128)S(1)}, u32[]{:S(2)}, u32[]{:S(2)}) %collective-permute-start.3) | collective-permute-done | bytes 65568 | tf_op jit(solution)/shard_map/ppermute | solution.py:322
  13.9 0.1 add_select_fusion
  14.0 3.4 %collective-permute-start.6 = (f32[2,32,128]{2,1,0:T(8,128)S(1)}, f32[2,32,128]{2,1,0:T(8,128)S(1)}, u32[]{:S(2)}, u32[]{:S(2)}) collective-permute-start(f32[2,32,128]{2,1,0:T(8,128)S(1)} %fusion), channel_id=1, source_target_pairs={{0,25},{1,24},{2,27},{3,26},{4,29},{5,28},{6,31},{7,30},{8,17},{9,... | collective-permute-start | bytes 98312 | tf_op jit(solution)/shard_map/ppermute | solution.py:322
  17.4 0.0 collective-permute-start.4
  17.4 0.6 %collective-permute-start.5 = (f32[2,32,128]{2,1,0:T(8,128)S(1)}, f32[2,32,128]{2,1,0:T(8,128)S(1)}, u32[]{:S(2)}, u32[]{:S(2)}) collective-permute-start(f32[2,32,128]{2,1,0:T(8,128)S(1)} %get-tuple-element.30), channel_id=1, source_target_pairs={{0,17},{1,16},{2,19},{3,18},{4,21},{5,20},{6,23},{7,22},{8,25},{9,... | collective-permute-start | bytes 98312 | tf_op jit(solution)/shard_map/ppermute | solution.py:322
  18.0 2.2 %near.3.late_ref = f32[3,1024]{1,0:T(4,128)S(1)} custom-call(f32[4,2,64,128]{3,2,1,0:T(8,128)S(1)} %get-tuple-element.27.before_ref, f32[2,2,64,128]{3,2,1,0:T(8,128)S(1)} %get-tuple-element.20.unit_ref, f32[2,64,768]{2,1,0:T(8,128)S(1)} %get-tuple-element.21.table_ref, f32[4,128,512]{2,1,0:T(8,128)S(1)} %get-tuple-element.22.phase_ref, ...), custom_call_target="tpu_custom_call" | custom-call | flops 905969664 | bytes 1048576 | tf_op jit(solution)/shard_map/near/pallas_call | solution.py:407
  20.2 0.0 collective-permute-done.6
  20.2 0.6 %collective-permute-done.4 = f32[2,32,128]{2,1,0:T(8,128)S(1)} collective-permute-done((f32[2,32,128]{2,1,0:T(8,128)S(1)}, f32[2,32,128]{2,1,0:T(8,128)S(1)}, u32[]{:S(2)}, u32[]{:S(2)}) %collective-permute-start.4) | collective-permute-done | bytes 32800 | tf_op jit(solution)/shard_map/ppermute | solution.py:322
  20.7 0.9 %collective-permute-done.5 = f32[2,32,128]{2,1,0:T(8,128)S(1)} collective-permute-done((f32[2,32,128]{2,1,0:T(8,128)S(1)}, f32[2,32,128]{2,1,0:T(8,128)S(1)}, u32[]{:S(2)}, u32[]{:S(2)}) %collective-permute-start.5) | collective-permute-done | bytes 32800 | tf_op jit(solution)/shard_map/ppermute | solution.py:322
  21.7 0.1 select_add_fusion.carry_ref
  21.8 4.1 %forces.1 = f32[3,2048]{1,0:T(4,128)} custom-call(f32[2,2,32,128]{3,2,1,0:T(8,128)S(1)} %select_add_fusion.carry_ref, f32[3,1024]{1,0:T(4,128)S(1)} %near.2.early_ref, f32[3,1024]{1,0:T(4,128)S(1)} %near.3.late_ref, f32[2,2,64,128]{3,2,1,0:T(8,128)S(1)} %get-tuple-element.20.unit_ref, f32[2,64,768]{2,1,0:T(8,128)S(1)} %get-tuple-element.21.table_ref, ...), custom_call_target="tpu_custom_call" | custom-call | tf_op jit(solution)/shard_map/forces/pallas_call | solution.py:425
  (9 shorter events, 0.1 us)
Async XLA Ops:
  3.3 1.4 %collective-permute-start = (f32[2,2,32,128]{3,2,1,0:T(8,128)S(1)}, f32[2,2,32,128]{3,2,1,0:T(8,128)S(1)}, u32[]{:S(2)}, u32[]{:S(2)}) collective-permute-start(f32[2,2,32,128]{3,2,1,0:T(8,128)S(1)} %get-tuple-element.18), channel_id=1, source_target_pairs={{0,1},{1,0},{2,3},{3,2},{4,5},{5,4},{6,7},{7,6},{8,9},{9,8},{10,11... | collective-permute-start | bytes 196616 | tf_op jit(solution)/shard_map/ppermute | solution.py:322
  4.8 6.3 %collective-permute-start.1 = (f32[2,2,32,128]{3,2,1,0:T(8,128)S(1)}, f32[2,2,32,128]{3,2,1,0:T(8,128)S(1)}, u32[]{:S(2)}, u32[]{:S(2)}) collective-permute-start(f32[2,2,32,128]{3,2,1,0:T(8,128)S(1)} %add.60), channel_id=1, source_target_pairs={{0,3},{1,2},{2,1},{3,0},{4,7},{5,6},{6,5},{7,4},{8,11},{9,10},{10,... | collective-permute-start | bytes 196616 | tf_op jit(solution)/shard_map/ppermute | solution.py:322
  7.4 3.9 %collective-permute-start.2 = (f32[2,2,32,128]{3,2,1,0:T(8,128)S(1)}, f32[2,2,32,128]{3,2,1,0:T(8,128)S(1)}, u32[]{:S(2)}, u32[]{:S(2)}) collective-permute-start(f32[2,2,32,128]{3,2,1,0:T(8,128)S(1)} %add.60), channel_id=1, source_target_pairs={{0,5},{1,4},{2,7},{3,6},{4,1},{5,0},{6,3},{7,2},{8,13},{9,12},{10,... | collective-permute-start | bytes 196616 | tf_op jit(solution)/shard_map/ppermute | solution.py:322
  8.9 5.0 %collective-permute-start.3 = (f32[2,2,32,128]{3,2,1,0:T(8,128)S(1)}, f32[2,2,32,128]{3,2,1,0:T(8,128)S(1)}, u32[]{:S(2)}, u32[]{:S(2)}) collective-permute-start(f32[2,2,32,128]{3,2,1,0:T(8,128)S(1)} %add.60), channel_id=1, source_target_pairs={{0,7},{1,6},{2,5},{3,4},{4,3},{5,2},{6,1},{7,0},{8,15},{9,14},{10,... | collective-permute-start | bytes 196616 | tf_op jit(solution)/shard_map/ppermute | solution.py:322
  14.0 6.2 %collective-permute-start.6 = (f32[2,32,128]{2,1,0:T(8,128)S(1)}, f32[2,32,128]{2,1,0:T(8,128)S(1)}, u32[]{:S(2)}, u32[]{:S(2)}) collective-permute-start(f32[2,32,128]{2,1,0:T(8,128)S(1)} %fusion), channel_id=1, source_target_pairs={{0,25},{1,24},{2,27},{3,26},{4,29},{5,28},{6,31},{7,30},{8,17},{9,... | collective-permute-start | bytes 98312 | tf_op jit(solution)/shard_map/ppermute | solution.py:322
  17.4 3.3 %collective-permute-start.4 = (f32[2,32,128]{2,1,0:T(8,128)S(1)}, f32[2,32,128]{2,1,0:T(8,128)S(1)}, u32[]{:S(2)}, u32[]{:S(2)}) collective-permute-start(f32[2,32,128]{2,1,0:T(8,128)S(1)} %get-tuple-element.29), channel_id=1, source_target_pairs={{0,9},{1,8},{2,11},{3,10},{4,13},{5,12},{6,15},{7,14},{8,1},{9,0},... | collective-permute-start | bytes 98312 | tf_op jit(solution)/shard_map/ppermute | solution.py:322
  17.4 4.2 %collective-permute-start.5 = (f32[2,32,128]{2,1,0:T(8,128)S(1)}, f32[2,32,128]{2,1,0:T(8,128)S(1)}, u32[]{:S(2)}, u32[]{:S(2)}) collective-permute-start(f32[2,32,128]{2,1,0:T(8,128)S(1)} %get-tuple-element.30), channel_id=1, source_target_pairs={{0,17},{1,16},{2,19},{3,18},{4,21},{5,20},{6,23},{7,22},{8,25},{9,... | collective-permute-start | bytes 98312 | tf_op jit(solution)/shard_map/ppermute | solution.py:322

commit v8 on v7

--- a/solution.py
+++ b/solution.py
@@ -96,7 +96,7 @@
     even = even_group(p.shape)
     a = (0.5 * height) * wave(p, jnp.where(even, q_plus, q_minus), box_x, box_y)[2]
     square = 0.25 * a * a
-    last = count + 8
+    last = count + 3
     scaled = {last + 1: jnp.ones_like(a), last: jnp.ones_like(a)}
     for n in range(last, 0, -1):
         scaled[n - 1] = scaled[n] + square * (scaled[n + 1] * (1.0 / (n * (n + 1))))
@@ -236,9 +236,10 @@
         both = jnp.concatenate([heavy_high, heavy_low], axis=0)
         across = (((1,), (1,)), ((), ()))
         cut, rest = exact * 2 * HALF, (count - exact) * 2 * HALF
-        first = lax.dot_general(both, spread_ref[b, :cut], across, preferred_element_type=jnp.float32)
-        second = lax.dot_general(heavy_high, spread_ref[b, cut:], across, preferred_element_type=jnp.float32)
-        moments = first[: 2 * PDIM] + first[2 * PDIM :] + second[:, rest:]
+        found_parts = lax.dot_general(both, spread_ref[b], across, preferred_element_type=jnp.float32)
+        second = found_parts[: 2 * PDIM] + found_parts[2 * PDIM :]
+        moments = second[:, :cut] + found_parts[: 2 * PDIM, cut + rest :]
+        second = second[:, cut : cut + rest]
         moments = [moments[:, m * LANES : (m + 1) * LANES] for m in range(exact // 2)]
         moments += [second[:, m * LANES : (m + 1) * LANES] for m in range((count - exact) // 2)]
 
@@ -332,7 +333,7 @@
         other = swap(totals, stride ^ 1)
         inside = inside + jnp.where(ahead(mode, stride), other, 0.0)
         totals = totals + other
-    across, along, both = [swap(totals, mask) for mask in (strides[-1] ^ 1, modes ^ 1, modes ^ strides[-1] ^ 1)]
+    across, both, along = [swap(totals, mask) for mask in (strides[-1] ^ 1, modes ^ strides[-1] ^ 1, modes ^ 1)]
     near = early()
     inside = inside + jnp.where(ahead(mode, strides[-1]), across, 0.0)
     totals = totals + across

time: 26.1 us -> 26 us (level)
  no operation moved by 1% of the time
where the time goes in v8:
time: 26 us; the launch traced here: 25.8 us
  Pallas kernels  11.7 us (45%)
  starting transfers between devices  8.72 us (34%)
  waiting for transfers between devices  4.98 us (19%)
  other arithmetic  0.29 us (1%)
    ppermute x7, starting transfers between devices, swap(): lax.ppermute(value, ('slab', 'mode'), [(i, i ^ mask) for i in range(slabs...  8.72 us
    ppermute x7, waiting for transfers between devices, swap(): lax.ppermute(value, ('slab', 'mode'), [(i, i ^ mask) for i in range(slabs...  4.98 us
    pallas_call x2, Pallas kernels, near(): pl.pallas_call(functools.partial(near_kernel, count, exact, chosen), out_...  4.33 us
    pallas_call x1, Pallas kernels, shards(): pl.pallas_call(functools.partial(forces_kernel, count, exact), out_shape=...  4.1 us
    pallas_call x1, Pallas kernels, shards(): pl.pallas_call(functools.partial(moments_kernel, count, exact, height), o...  3.26 us
  transfers between devices with their start and end apart: 7, of which 5 were waited for; matrix products, arithmetic and copies ran while one was open for 0% of the time, Pallas kernels for 17%

profile of v8, /device:TPU:0, one launch (start us, length us, event | category | flops | bytes accessed | tf_op | source)
XLA Modules:
  0.0 25.8 jit_solution(14314134741023149342)
XLA Ops:
  0.0 3.3 %moments.1 = (f32[2,2,32,128]{3,2,1,0:T(8,128)S(1)}, f32[2,32,128]{2,1,0:T(8,128)S(1)}, f32[2,2,64,128]{3,2,1,0:T(8,128)S(1)}, f32[4,2,64,128]{3,2,1,0:T(8,128)S...) custom-call(s32[8]{0:T(128)} %counts_ref.1, ...), custom_call_target="tpu_custom_call" | custom-call | tf_op jit(solution)/shard_map/moments/pallas_call | solution.py:382
  3.3 0.5 %collective-permute-start = (f32[2,2,32,128]{3,2,1,0:T(8,128)S(1)}, f32[2,2,32,128]{3,2,1,0:T(8,128)S(1)}, u32[]{:S(2)}, u32[]{:S(2)}) collective-permute-start(f32[2,2,32,128]{3,2,1,0:T(8,128)S(1)} %get-tuple-element.18), channel_id=1, source_target_pairs={{0,1},{1,0},{2,3},{3,2},{4,5},{5,4},{6,7},{7,6},{8,9},{9,8},{10,11... | collective-permute-start | bytes 196616 | tf_op jit(solution)/shard_map/ppermute | solution.py:323
  3.9 0.8 %collective-permute-done = f32[2,2,32,128]{3,2,1,0:T(8,128)S(1)} collective-permute-done((f32[2,2,32,128]{3,2,1,0:T(8,128)S(1)}, f32[2,2,32,128]{3,2,1,0:T(8,128)S(1)}, u32[]{:S(2)}, u32[]{:S(2)}) %collective-permute-start) | collective-permute-done | bytes 65568 | tf_op jit(solution)/shard_map/ppermute | solution.py:323
  4.7 2.7 %collective-permute-start.1 = (f32[2,2,32,128]{3,2,1,0:T(8,128)S(1)}, f32[2,2,32,128]{3,2,1,0:T(8,128)S(1)}, u32[]{:S(2)}, u32[]{:S(2)}) collective-permute-start(f32[2,2,32,128]{3,2,1,0:T(8,128)S(1)} %add.60), channel_id=1, source_target_pairs={{0,3},{1,2},{2,1},{3,0},{4,7},{5,6},{6,5},{7,4},{8,11},{9,10},{10,... | collective-permute-start | bytes 196616 | tf_op jit(solution)/shard_map/ppermute | solution.py:323
  7.4 1.5 %collective-permute-start.2 = (f32[2,2,32,128]{3,2,1,0:T(8,128)S(1)}, f32[2,2,32,128]{3,2,1,0:T(8,128)S(1)}, u32[]{:S(2)}, u32[]{:S(2)}) collective-permute-start(f32[2,2,32,128]{3,2,1,0:T(8,128)S(1)} %add.60), channel_id=1, source_target_pairs={{0,5},{1,4},{2,7},{3,6},{4,1},{5,0},{6,3},{7,2},{8,13},{9,12},{10,... | collective-permute-start | bytes 196616 | tf_op jit(solution)/shard_map/ppermute | solution.py:323
  8.8 0.0 collective-permute-start.3
  8.9 2.2 %near.2.early_ref = f32[3,1024]{1,0:T(4,128)S(1)} custom-call(f32[4,2,64,128]{3,2,1,0:T(8,128)S(1)} %get-tuple-element.27.before_ref, f32[2,2,64,128]{3,2,1,0:T(8,128)S(1)} %get-tuple-element.20.unit_ref, f32[2,64,768]{2,1,0:T(8,128)S(1)} %get-tuple-element.21.table_ref, f32[4,128,512]{2,1,0:T(8,128)S(1)} %get-tuple-element.22.phase_ref, ...), custom_call_target="tpu_custom_call" | custom-call | flops 905969664 | bytes 1048576 | tf_op jit(solution)/shard_map/near/pallas_call | solution.py:408
  11.0 0.0 collective-permute-done.1
  11.0 0.2 collective-permute-done.2
  11.3 2.5 %collective-permute-done.3 = f32[2,2,32,128]{3,2,1,0:T(8,128)S(1)} collective-permute-done((f32[2,2,32,128]{3,2,1,0:T(8,128)S(1)}, f32[2,2,32,128]{3,2,1,0:T(8,128)S(1)}, u32[]{:S(2)}, u32[]{:S(2)}) %collective-permute-start.3) | collective-permute-done | bytes 65568 | tf_op jit(solution)/shard_map/ppermute | solution.py:323
  13.8 0.1 add_select_fusion
  13.9 3.4 %collective-permute-start.6 = (f32[2,32,128]{2,1,0:T(8,128)S(1)}, f32[2,32,128]{2,1,0:T(8,128)S(1)}, u32[]{:S(2)}, u32[]{:S(2)}) collective-permute-start(f32[2,32,128]{2,1,0:T(8,128)S(1)} %fusion), channel_id=1, source_target_pairs={{0,25},{1,24},{2,27},{3,26},{4,29},{5,28},{6,31},{7,30},{8,17},{9,... | collective-permute-start | bytes 98312 | tf_op jit(solution)/shard_map/ppermute | solution.py:323
  17.3 0.0 collective-permute-start.4
  17.3 0.6 %collective-permute-start.5 = (f32[2,32,128]{2,1,0:T(8,128)S(1)}, f32[2,32,128]{2,1,0:T(8,128)S(1)}, u32[]{:S(2)}, u32[]{:S(2)}) collective-permute-start(f32[2,32,128]{2,1,0:T(8,128)S(1)} %get-tuple-element.30), channel_id=1, source_target_pairs={{0,17},{1,16},{2,19},{3,18},{4,21},{5,20},{6,23},{7,22},{8,25},{9,... | collective-permute-start | bytes 98312 | tf_op jit(solution)/shard_map/ppermute | solution.py:323
  17.9 2.2 %near.3.late_ref = f32[3,1024]{1,0:T(4,128)S(1)} custom-call(f32[4,2,64,128]{3,2,1,0:T(8,128)S(1)} %get-tuple-element.27.before_ref, f32[2,2,64,128]{3,2,1,0:T(8,128)S(1)} %get-tuple-element.20.unit_ref, f32[2,64,768]{2,1,0:T(8,128)S(1)} %get-tuple-element.21.table_ref, f32[4,128,512]{2,1,0:T(8,128)S(1)} %get-tuple-element.22.phase_ref, ...), custom_call_target="tpu_custom_call" | custom-call | flops 905969664 | bytes 1048576 | tf_op jit(solution)/shard_map/near/pallas_call | solution.py:408
  20.1 0.0 collective-permute-done.6
  20.1 0.6 %collective-permute-done.4 = f32[2,32,128]{2,1,0:T(8,128)S(1)} collective-permute-done((f32[2,32,128]{2,1,0:T(8,128)S(1)}, f32[2,32,128]{2,1,0:T(8,128)S(1)}, u32[]{:S(2)}, u32[]{:S(2)}) %collective-permute-start.4) | collective-permute-done | bytes 32800 | tf_op jit(solution)/shard_map/ppermute | solution.py:323
  20.7 0.9 %collective-permute-done.5 = f32[2,32,128]{2,1,0:T(8,128)S(1)} collective-permute-done((f32[2,32,128]{2,1,0:T(8,128)S(1)}, f32[2,32,128]{2,1,0:T(8,128)S(1)}, u32[]{:S(2)}, u32[]{:S(2)}) %collective-permute-start.5) | collective-permute-done | bytes 32800 | tf_op jit(solution)/shard_map/ppermute | solution.py:323
  21.6 0.1 select_add_fusion.carry_ref
  21.7 4.1 %forces.1 = f32[3,2048]{1,0:T(4,128)} custom-call(f32[2,2,32,128]{3,2,1,0:T(8,128)S(1)} %select_add_fusion.carry_ref, f32[3,1024]{1,0:T(4,128)S(1)} %near.2.early_ref, f32[3,1024]{1,0:T(4,128)S(1)} %near.3.late_ref, f32[2,2,64,128]{3,2,1,0:T(8,128)S(1)} %get-tuple-element.20.unit_ref, f32[2,64,768]{2,1,0:T(8,128)S(1)} %get-tuple-element.21.table_ref, ...), custom_call_target="tpu_custom_call" | custom-call | tf_op jit(solution)/shard_map/forces/pallas_call | solution.py:426
  (9 shorter events, 0.1 us)
Async XLA Ops:
  3.3 1.4 %collective-permute-start = (f32[2,2,32,128]{3,2,1,0:T(8,128)S(1)}, f32[2,2,32,128]{3,2,1,0:T(8,128)S(1)}, u32[]{:S(2)}, u32[]{:S(2)}) collective-permute-start(f32[2,2,32,128]{3,2,1,0:T(8,128)S(1)} %get-tuple-element.18), channel_id=1, source_target_pairs={{0,1},{1,0},{2,3},{3,2},{4,5},{5,4},{6,7},{7,6},{8,9},{9,8},{10,11... | collective-permute-start | bytes 196616 | tf_op jit(solution)/shard_map/ppermute | solution.py:323
  4.7 6.3 %collective-permute-start.1 = (f32[2,2,32,128]{3,2,1,0:T(8,128)S(1)}, f32[2,2,32,128]{3,2,1,0:T(8,128)S(1)}, u32[]{:S(2)}, u32[]{:S(2)}) collective-permute-start(f32[2,2,32,128]{3,2,1,0:T(8,128)S(1)} %add.60), channel_id=1, source_target_pairs={{0,3},{1,2},{2,1},{3,0},{4,7},{5,6},{6,5},{7,4},{8,11},{9,10},{10,... | collective-permute-start | bytes 196616 | tf_op jit(solution)/shard_map/ppermute | solution.py:323
  7.4 3.9 %collective-permute-start.2 = (f32[2,2,32,128]{3,2,1,0:T(8,128)S(1)}, f32[2,2,32,128]{3,2,1,0:T(8,128)S(1)}, u32[]{:S(2)}, u32[]{:S(2)}) collective-permute-start(f32[2,2,32,128]{3,2,1,0:T(8,128)S(1)} %add.60), channel_id=1, source_target_pairs={{0,5},{1,4},{2,7},{3,6},{4,1},{5,0},{6,3},{7,2},{8,13},{9,12},{10,... | collective-permute-start | bytes 196616 | tf_op jit(solution)/shard_map/ppermute | solution.py:323
  8.8 5.0 %collective-permute-start.3 = (f32[2,2,32,128]{3,2,1,0:T(8,128)S(1)}, f32[2,2,32,128]{3,2,1,0:T(8,128)S(1)}, u32[]{:S(2)}, u32[]{:S(2)}) collective-permute-start(f32[2,2,32,128]{3,2,1,0:T(8,128)S(1)} %add.60), channel_id=1, source_target_pairs={{0,7},{1,6},{2,5},{3,4},{4,3},{5,2},{6,1},{7,0},{8,15},{9,14},{10,... | collective-permute-start | bytes 196616 | tf_op jit(solution)/shard_map/ppermute | solution.py:323
  13.9 6.2 %collective-permute-start.6 = (f32[2,32,128]{2,1,0:T(8,128)S(1)}, f32[2,32,128]{2,1,0:T(8,128)S(1)}, u32[]{:S(2)}, u32[]{:S(2)}) collective-permute-start(f32[2,32,128]{2,1,0:T(8,128)S(1)} %fusion), channel_id=1, source_target_pairs={{0,25},{1,24},{2,27},{3,26},{4,29},{5,28},{6,31},{7,30},{8,17},{9,... | collective-permute-start | bytes 98312 | tf_op jit(solution)/shard_map/ppermute | solution.py:323
  17.3 3.3 %collective-permute-start.4 = (f32[2,32,128]{2,1,0:T(8,128)S(1)}, f32[2,32,128]{2,1,0:T(8,128)S(1)}, u32[]{:S(2)}, u32[]{:S(2)}) collective-permute-start(f32[2,32,128]{2,1,0:T(8,128)S(1)} %get-tuple-element.29), channel_id=1, source_target_pairs={{0,9},{1,8},{2,11},{3,10},{4,13},{5,12},{6,15},{7,14},{8,1},{9,0},... | collective-permute-start | bytes 98312 | tf_op jit(solution)/shard_map/ppermute | solution.py:323
  17.3 4.2 %collective-permute-start.5 = (f32[2,32,128]{2,1,0:T(8,128)S(1)}, f32[2,32,128]{2,1,0:T(8,128)S(1)}, u32[]{:S(2)}, u32[]{:S(2)}) collective-permute-start(f32[2,32,128]{2,1,0:T(8,128)S(1)} %get-tuple-element.30), channel_id=1, source_target_pairs={{0,17},{1,16},{2,19},{3,18},{4,21},{5,20},{6,23},{7,22},{8,25},{9,... | collective-permute-start | bytes 98312 | tf_op jit(solution)/shard_map/ppermute | solution.py:323

commit v9 on v8

--- a/solution.py
+++ b/solution.py
@@ -122,7 +122,8 @@
             for parity in range(2):
                 at = m * LANES + part * 2 * HALF + parity * HALF
                 n = 2 * m + parity
-                value = powers[n : n + 1] * sides[part * HALF : (part + 1) * HALF]
+                value = sides[part * HALF : (part + 1) * HALF]
+                value = powers[n : n + 1] * value if n else value
                 if n < exact:
                     value, low = split(value)
                     spread_ref[count * 2 * HALF + at : count * 2 * HALF + at + HALF] = low

time: 26 us -> 25.9 us (level)
  no operation moved by 1% of the time
where the time goes in v9:
time: 25.9 us; the launch traced here: 25.7 us
  Pallas kernels  11.5 us (44%)
  starting transfers between devices  8.71 us (34%)
  waiting for transfers between devices  5.04 us (19%)
  other arithmetic  0.29 us (1%)
    ppermute x7, starting transfers between devices, swap(): lax.ppermute(value, ('slab', 'mode'), [(i, i ^ mask) for i in range(slabs...  8.71 us
    ppermute x7, waiting for transfers between devices, swap(): lax.ppermute(value, ('slab', 'mode'), [(i, i ^ mask) for i in range(slabs...  5.04 us
    pallas_call x2, Pallas kernels, near(): pl.pallas_call(functools.partial(near_kernel, count, exact, chosen), out_...  4.27 us
    pallas_call x1, Pallas kernels, shards(): pl.pallas_call(functools.partial(forces_kernel, count, exact), out_shape=...  4.09 us
    pallas_call x1, Pallas kernels, shards(): pl.pallas_call(functools.partial(moments_kernel, count, exact, height), o...  3.17 us
  transfers between devices with their start and end apart: 7, of which 5 were waited for; matrix products, arithmetic and copies ran while one was open for 0% of the time, Pallas kernels for 17%

profile of v9, /device:TPU:0, one launch (start us, length us, event | category | flops | bytes accessed | tf_op | source)
XLA Modules:
  0.0 25.7 jit_solution(10164071544070029437)
XLA Ops:
  0.0 3.2 %moments.1 = (f32[2,2,32,128]{3,2,1,0:T(8,128)S(1)}, f32[2,32,128]{2,1,0:T(8,128)S(1)}, f32[2,2,64,128]{3,2,1,0:T(8,128)S(1)}, f32[4,2,64,128]{3,2,1,0:T(8,128)S...) custom-call(s32[8]{0:T(128)} %counts_ref.1, ...), custom_call_target="tpu_custom_call" | custom-call | tf_op jit(solution)/shard_map/moments/pallas_call | solution.py:383
  3.2 0.5 %collective-permute-start = (f32[2,2,32,128]{3,2,1,0:T(8,128)S(1)}, f32[2,2,32,128]{3,2,1,0:T(8,128)S(1)}, u32[]{:S(2)}, u32[]{:S(2)}) collective-permute-start(f32[2,2,32,128]{3,2,1,0:T(8,128)S(1)} %get-tuple-element.18), channel_id=1, source_target_pairs={{0,1},{1,0},{2,3},{3,2},{4,5},{5,4},{6,7},{7,6},{8,9},{9,8},{10,11... | collective-permute-start | bytes 196616 | tf_op jit(solution)/shard_map/ppermute | solution.py:324
  3.8 0.8 %collective-permute-done = f32[2,2,32,128]{3,2,1,0:T(8,128)S(1)} collective-permute-done((f32[2,2,32,128]{3,2,1,0:T(8,128)S(1)}, f32[2,2,32,128]{3,2,1,0:T(8,128)S(1)}, u32[]{:S(2)}, u32[]{:S(2)}) %collective-permute-start) | collective-permute-done | bytes 65568 | tf_op jit(solution)/shard_map/ppermute | solution.py:324
  4.6 2.7 %collective-permute-start.1 = (f32[2,2,32,128]{3,2,1,0:T(8,128)S(1)}, f32[2,2,32,128]{3,2,1,0:T(8,128)S(1)}, u32[]{:S(2)}, u32[]{:S(2)}) collective-permute-start(f32[2,2,32,128]{3,2,1,0:T(8,128)S(1)} %add.60), channel_id=1, source_target_pairs={{0,3},{1,2},{2,1},{3,0},{4,7},{5,6},{6,5},{7,4},{8,11},{9,10},{10,... | collective-permute-start | bytes 196616 | tf_op jit(solution)/shard_map/ppermute | solution.py:324
  7.3 1.5 %collective-permute-start.2 = (f32[2,2,32,128]{3,2,1,0:T(8,128)S(1)}, f32[2,2,32,128]{3,2,1,0:T(8,128)S(1)}, u32[]{:S(2)}, u32[]{:S(2)}) collective-permute-start(f32[2,2,32,128]{3,2,1,0:T(8,128)S(1)} %add.60), channel_id=1, source_target_pairs={{0,5},{1,4},{2,7},{3,6},{4,1},{5,0},{6,3},{7,2},{8,13},{9,12},{10,... | collective-permute-start | bytes 196616 | tf_op jit(solution)/shard_map/ppermute | solution.py:324
  8.8 0.0 collective-permute-start.3
  8.8 2.1 %near.2.early_ref = f32[3,1024]{1,0:T(4,128)S(1)} custom-call(f32[4,2,64,128]{3,2,1,0:T(8,128)S(1)} %get-tuple-element.27.before_ref, f32[2,2,64,128]{3,2,1,0:T(8,128)S(1)} %get-tuple-element.20.unit_ref, f32[2,64,768]{2,1,0:T(8,128)S(1)} %get-tuple-element.21.table_ref, f32[4,128,512]{2,1,0:T(8,128)S(1)} %get-tuple-element.22.phase_ref, ...), custom_call_target="tpu_custom_call" | custom-call | flops 905969664 | bytes 1048576 | tf_op jit(solution)/shard_map/near/pallas_call | solution.py:409
  10.9 0.0 collective-permute-done.1
  10.9 0.3 %collective-permute-done.2 = f32[2,2,32,128]{3,2,1,0:T(8,128)S(1)} collective-permute-done((f32[2,2,32,128]{3,2,1,0:T(8,128)S(1)}, f32[2,2,32,128]{3,2,1,0:T(8,128)S(1)}, u32[]{:S(2)}, u32[]{:S(2)}) %collective-permute-start.2) | collective-permute-done | bytes 65568 | tf_op jit(solution)/shard_map/ppermute | solution.py:324
  11.2 2.5 %collective-permute-done.3 = f32[2,2,32,128]{3,2,1,0:T(8,128)S(1)} collective-permute-done((f32[2,2,32,128]{3,2,1,0:T(8,128)S(1)}, f32[2,2,32,128]{3,2,1,0:T(8,128)S(1)}, u32[]{:S(2)}, u32[]{:S(2)}) %collective-permute-start.3) | collective-permute-done | bytes 65568 | tf_op jit(solution)/shard_map/ppermute | solution.py:324
  13.7 0.1 add_select_fusion
  13.8 3.4 %collective-permute-start.6 = (f32[2,32,128]{2,1,0:T(8,128)S(1)}, f32[2,32,128]{2,1,0:T(8,128)S(1)}, u32[]{:S(2)}, u32[]{:S(2)}) collective-permute-start(f32[2,32,128]{2,1,0:T(8,128)S(1)} %fusion), channel_id=1, source_target_pairs={{0,25},{1,24},{2,27},{3,26},{4,29},{5,28},{6,31},{7,30},{8,17},{9,... | collective-permute-start | bytes 98312 | tf_op jit(solution)/shard_map/ppermute | solution.py:324
  17.2 0.0 collective-permute-start.4
  17.2 0.6 %collective-permute-start.5 = (f32[2,32,128]{2,1,0:T(8,128)S(1)}, f32[2,32,128]{2,1,0:T(8,128)S(1)}, u32[]{:S(2)}, u32[]{:S(2)}) collective-permute-start(f32[2,32,128]{2,1,0:T(8,128)S(1)} %get-tuple-element.30), channel_id=1, source_target_pairs={{0,17},{1,16},{2,19},{3,18},{4,21},{5,20},{6,23},{7,22},{8,25},{9,... | collective-permute-start | bytes 98312 | tf_op jit(solution)/shard_map/ppermute | solution.py:324
  17.8 2.1 %near.3.late_ref = f32[3,1024]{1,0:T(4,128)S(1)} custom-call(f32[4,2,64,128]{3,2,1,0:T(8,128)S(1)} %get-tuple-element.27.before_ref, f32[2,2,64,128]{3,2,1,0:T(8,128)S(1)} %get-tuple-element.20.unit_ref, f32[2,64,768]{2,1,0:T(8,128)S(1)} %get-tuple-element.21.table_ref, f32[4,128,512]{2,1,0:T(8,128)S(1)} %get-tuple-element.22.phase_ref, ...), custom_call_target="tpu_custom_call" | custom-call | flops 905969664 | bytes 1048576 | tf_op jit(solution)/shard_map/near/pallas_call | solution.py:409
  20.0 0.0 collective-permute-done.6
  20.0 0.6 %collective-permute-done.4 = f32[2,32,128]{2,1,0:T(8,128)S(1)} collective-permute-done((f32[2,32,128]{2,1,0:T(8,128)S(1)}, f32[2,32,128]{2,1,0:T(8,128)S(1)}, u32[]{:S(2)}, u32[]{:S(2)}) %collective-permute-start.4) | collective-permute-done | bytes 32800 | tf_op jit(solution)/shard_map/ppermute | solution.py:324
  20.6 0.9 %collective-permute-done.5 = f32[2,32,128]{2,1,0:T(8,128)S(1)} collective-permute-done((f32[2,32,128]{2,1,0:T(8,128)S(1)}, f32[2,32,128]{2,1,0:T(8,128)S(1)}, u32[]{:S(2)}, u32[]{:S(2)}) %collective-permute-start.5) | collective-permute-done | bytes 32800 | tf_op jit(solution)/shard_map/ppermute | solution.py:324
  21.5 0.1 select_add_fusion.carry_ref
  21.6 4.1 %forces.1 = f32[3,2048]{1,0:T(4,128)} custom-call(f32[2,2,32,128]{3,2,1,0:T(8,128)S(1)} %select_add_fusion.carry_ref, f32[3,1024]{1,0:T(4,128)S(1)} %near.2.early_ref, f32[3,1024]{1,0:T(4,128)S(1)} %near.3.late_ref, f32[2,2,64,128]{3,2,1,0:T(8,128)S(1)} %get-tuple-element.20.unit_ref, f32[2,64,768]{2,1,0:T(8,128)S(1)} %get-tuple-element.21.table_ref, ...), custom_call_target="tpu_custom_call" | custom-call | tf_op jit(solution)/shard_map/forces/pallas_call | solution.py:427
  (9 shorter events, 0.1 us)
Async XLA Ops:
  3.2 1.4 %collective-permute-start = (f32[2,2,32,128]{3,2,1,0:T(8,128)S(1)}, f32[2,2,32,128]{3,2,1,0:T(8,128)S(1)}, u32[]{:S(2)}, u32[]{:S(2)}) collective-permute-start(f32[2,2,32,128]{3,2,1,0:T(8,128)S(1)} %get-tuple-element.18), channel_id=1, source_target_pairs={{0,1},{1,0},{2,3},{3,2},{4,5},{5,4},{6,7},{7,6},{8,9},{9,8},{10,11... | collective-permute-start | bytes 196616 | tf_op jit(solution)/shard_map/ppermute | solution.py:324
  4.6 6.3 %collective-permute-start.1 = (f32[2,2,32,128]{3,2,1,0:T(8,128)S(1)}, f32[2,2,32,128]{3,2,1,0:T(8,128)S(1)}, u32[]{:S(2)}, u32[]{:S(2)}) collective-permute-start(f32[2,2,32,128]{3,2,1,0:T(8,128)S(1)} %add.60), channel_id=1, source_target_pairs={{0,3},{1,2},{2,1},{3,0},{4,7},{5,6},{6,5},{7,4},{8,11},{9,10},{10,... | collective-permute-start | bytes 196616 | tf_op jit(solution)/shard_map/ppermute | solution.py:324
  7.3 3.9 %collective-permute-start.2 = (f32[2,2,32,128]{3,2,1,0:T(8,128)S(1)}, f32[2,2,32,128]{3,2,1,0:T(8,128)S(1)}, u32[]{:S(2)}, u32[]{:S(2)}) collective-permute-start(f32[2,2,32,128]{3,2,1,0:T(8,128)S(1)} %add.60), channel_id=1, source_target_pairs={{0,5},{1,4},{2,7},{3,6},{4,1},{5,0},{6,3},{7,2},{8,13},{9,12},{10,... | collective-permute-start | bytes 196616 | tf_op jit(solution)/shard_map/ppermute | solution.py:324
  8.8 5.0 %collective-permute-start.3 = (f32[2,2,32,128]{3,2,1,0:T(8,128)S(1)}, f32[2,2,32,128]{3,2,1,0:T(8,128)S(1)}, u32[]{:S(2)}, u32[]{:S(2)}) collective-permute-start(f32[2,2,32,128]{3,2,1,0:T(8,128)S(1)} %add.60), channel_id=1, source_target_pairs={{0,7},{1,6},{2,5},{3,4},{4,3},{5,2},{6,1},{7,0},{8,15},{9,14},{10,... | collective-permute-start | bytes 196616 | tf_op jit(solution)/shard_map/ppermute | solution.py:324
  13.8 6.2 %collective-permute-start.6 = (f32[2,32,128]{2,1,0:T(8,128)S(1)}, f32[2,32,128]{2,1,0:T(8,128)S(1)}, u32[]{:S(2)}, u32[]{:S(2)}) collective-permute-start(f32[2,32,128]{2,1,0:T(8,128)S(1)} %fusion), channel_id=1, source_target_pairs={{0,25},{1,24},{2,27},{3,26},{4,29},{5,28},{6,31},{7,30},{8,17},{9,... | collective-permute-start | bytes 98312 | tf_op jit(solution)/shard_map/ppermute | solution.py:324
  17.2 3.3 %collective-permute-start.4 = (f32[2,32,128]{2,1,0:T(8,128)S(1)}, f32[2,32,128]{2,1,0:T(8,128)S(1)}, u32[]{:S(2)}, u32[]{:S(2)}) collective-permute-start(f32[2,32,128]{2,1,0:T(8,128)S(1)} %get-tuple-element.29), channel_id=1, source_target_pairs={{0,9},{1,8},{2,11},{3,10},{4,13},{5,12},{6,15},{7,14},{8,1},{9,0},... | collective-permute-start | bytes 98312 | tf_op jit(solution)/shard_map/ppermute | solution.py:324
  17.2 4.2 %collective-permute-start.5 = (f32[2,32,128]{2,1,0:T(8,128)S(1)}, f32[2,32,128]{2,1,0:T(8,128)S(1)}, u32[]{:S(2)}, u32[]{:S(2)}) collective-permute-start(f32[2,32,128]{2,1,0:T(8,128)S(1)} %get-tuple-element.30), channel_id=1, source_target_pairs={{0,17},{1,16},{2,19},{3,18},{4,21},{5,20},{6,23},{7,22},{8,25},{9,... | collective-permute-start | bytes 98312 | tf_op jit(solution)/shard_map/ppermute | solution.py:324
